TPU v7x, 128 devices: a whole 4x4x4 slice. The times are simulated.
128 devices in a mesh: tm: 32 (over z, x, core), head: 4 (over y).
Axes of the slice: x: 4, y: 4, z: 4, core: 2. Of those that a mesh axis runs over, the one named last changes fastest.
Arguments:
- query: bfloat16 [98304, 1536], P('tm', 'head'), may hold values from -60 to 60
- keys: bfloat16 [98304, 1536], P('tm', 'head'), may hold values from -4 to 4
- values: bfloat16 [98304, 1536], P('tm', 'head'), may hold values from -6 to 6
- out_weight: bfloat16 [1536, 1536], P('head'), may hold values from -0.5 to 0.5
- near_list: int32 [768, 16], P('tm'), may hold values from 0 to 767, as said below
- far_list: int32 [768, 16], replicated, may hold values from 0 to 767, as said below
- stride_table: int32 [64], replicated, may hold values from 1 to 64, as said below
Outputs:
- mixed: bfloat16 [98304, 1536], P(('tm', 'head'))
Inputs may be any that keep to these rules, and one draw needn't show every extreme that they name: `near_list`: row b lists 16 different blocks, the first being b itself, all in the frame of block b or the frames just before and after it. `far_list`: row b lists 16 different blocks. Over all query blocks held by one index of tm together, the listed blocks are exactly 6 blocks of every tm index two or more away from it and none of any other index. `stride_table`: entry d is 1 for d < 2 and one of 16, 32, 64 otherwise; entry 2 is 16 and the last entry is 64.
All inputs are finite; a program needn't handle non-finite values.
Results may differ from a plain program's by a relative error of at most 0.013.
Values may be sent and summed in bfloat16 or wider, within the bound.
No kernel may reach another device: no remote copies, remote signals or barrier semaphores. Data moves between devices by JAX's collectives and lax.ppermute only.
A program may use at most 128 MiB of HBM per device.

v0:
```python
import math

import jax
import jax.numpy as jnp
from jax import lax
from jax.sharding import PartitionSpec as P

HD = 128
BLK = 128
FRAME_BLK = 12
KNEAR = 16
KFAR = 16
MINSTRIDE = 16


def with_halo(shard, sides, width):
    for axis, dim in sides:
        size, length = (lax.axis_size(axis), shard.shape[dim])
        up = [(i, (i + 1) % size) for i in range(size - 1)]
        down = [(j, i) for i, j in up]
        last = lax.slice_in_dim(shard, length - width, length, axis=dim)
        first = lax.slice_in_dim(shard, 0, width, axis=dim)
        before = lax.ppermute(last, axis, up)
        after = lax.ppermute(first, axis, down)
        shard = jnp.concatenate([before, shard, after], axis=dim)
    return shard


def attend_group(queries, keys_near, values_near, keys_far, values_far, usable, scale):
    key_rows = jnp.concatenate([keys_near, keys_far], axis=2)
    value_rows = jnp.concatenate([values_near, values_far], axis=2)
    scores = (
        jnp.einsum("hgqd,hgkd->hgqk", queries, key_rows, preferred_element_type=jnp.float32) * scale
    )
    scores = jnp.where(usable[None, :, None, :], scores, -1e30)
    row_peak = jnp.max(scores, axis=-1, keepdims=True)
    weights = jnp.exp(scores - row_peak)
    totals = jnp.sum(weights, axis=-1)
    mixed = jnp.einsum(
        "hgqk,hgkd->hgqd",
        weights.astype(jnp.bfloat16),
        value_rows,
        preferred_element_type=jnp.float32,
    )
    return mixed / totals[..., None]


def head_major(array, heads):
    return jnp.transpose(array.reshape(array.shape[0], heads, HD), (1, 0, 2))


def per_device(query, keys, values, out_weight, near_list, far_list, stride_table):
    tok_rows, width = query.shape
    heads = width // HD
    blocks = tok_rows // BLK
    thin_rows = BLK // MINSTRIDE
    first = lax.axis_index("tm") * blocks
    stacked = jnp.stack([head_major(keys, heads), head_major(values, heads)], axis=0)
    framed = with_halo(stacked, (("tm", 2),), FRAME_BLK * BLK)
    extended = framed.reshape(2, heads, blocks + 2 * FRAME_BLK, BLK, HD)
    thinned = stacked.reshape(2, heads, blocks, thin_rows, MINSTRIDE, HD)[:, :, :, :, 0]
    listed_far = lax.dynamic_slice_in_dim(far_list, first, blocks, 0)
    listed = listed_far.reshape(-1)
    everything = lax.all_gather(thinned, "tm", axis=2, tiled=True)
    packed = everything[:, :, listed].reshape(2, heads, blocks, KFAR * thin_rows, HD)
    query_frame = (first + jnp.arange(blocks, dtype=jnp.int32)) // FRAME_BLK
    distance = jnp.abs(query_frame[:, None] - listed_far // FRAME_BLK)
    frame_count = stride_table.shape[0]
    stride = jnp.sum(
        jnp.where(distance[..., None] == jnp.arange(frame_count, dtype=jnp.int32), stride_table, 0),
        axis=-1,
    )
    offsets = jnp.arange(thin_rows, dtype=jnp.int32) * MINSTRIDE
    used = (offsets[None, None, :] % stride[..., None] == 0).reshape(blocks, KFAR * thin_rows)
    local_near = near_list - first + FRAME_BLK
    query_blocks = head_major(query, heads).reshape(heads, blocks, BLK, HD)
    scale = 1.0 / math.sqrt(HD)

    def group_step(index):
        lower = index * 4
        chosen = lax.dynamic_slice_in_dim(local_near, lower, 4, 0)
        near_pair = extended[:, :, chosen].reshape(2, heads, 4, KNEAR * BLK, HD)
        far_pair = lax.dynamic_slice_in_dim(packed, lower, 4, 2)
        usable = jnp.concatenate(
            [jnp.ones((4, KNEAR * BLK), jnp.bool_), lax.dynamic_slice_in_dim(used, lower, 4, 0)],
            axis=1,
        )
        queries = lax.dynamic_slice_in_dim(query_blocks, lower, 4, 1)
        result = attend_group(
            queries, near_pair[0], near_pair[1], far_pair[0], far_pair[1], usable, scale
        )
        return result.astype(jnp.bfloat16)

    grouped = lax.map(group_step, jnp.arange(blocks // 4, dtype=jnp.int32))
    attended = jnp.transpose(grouped, (0, 2, 3, 1, 4)).reshape(tok_rows, width)
    summed = lax.psum_scatter(
        jnp.dot(attended, out_weight, preferred_element_type=jnp.float32).astype(jnp.bfloat16),
        "head",
        scatter_dimension=0,
        tiled=True,
    )
    return summed


def solution(mesh):
    placed = (
        P("tm", "head"),
        P("tm", "head"),
        P("tm", "head"),
        P("head", None),
        P("tm", None),
        P(),
        P(),
    )
    return jax.shard_map(
        per_device, mesh=mesh, in_specs=placed, out_specs=P(("tm", "head"), None), check_vma=False
    )
```

profile of v0, /device:TPU:0, one launch (start us, length us, event | category | flops | bytes accessed | tf_op | source)
XLA Modules:
  0.0 527.7 jit_solution(2230199931397616158)
XLA Ops:
  49.8 7.1 %pad_maximum_fusion = bf16[2,3,6144,128]{2,3,1,0:T(8,128)(2,1)} fusion(bf16[2,3,1536,128]{2,3,1,0:T(8,128)(2,1)} %collective-permute-done.1, bf16[1,3,3072,128]{2,3,1,0:T(8,128)(2,1)} %bitcast.91, bf16[1,3,3072,128]{2,3,1,0:T(8,128)(2,1)S(1)} %bitcast.88, bf16[2,3,1536,128]{2,3,1,0:T(8,128)(2,1)} %collective-permute-done), kind=kLoop, calls=%fused_computation.36 | loop fusion | flops 37748736 | bytes 18874368 | tf_op jit(solution)/shard_map/concatenate | solution.py:25
  56.8 12.7 %copy.75 = bf16[2,3,6144,128]{3,2,1,0:T(8,128)(2,1)} copy(bf16[2,3,6144,128]{2,3,1,0:T(8,128)(2,1)} %pad_maximum_fusion) | data formatting | bytes 18874368 | tf_op jit(solution)/shard_map/while | solution.py:94
  69.5 57.3 %all-gather.3.cloned.1.call-done = bf16[2,3,768,8,1,128]{5,4,3,2,1,0:T(2,128)(2,1)} async-done(((bf16[2,3,24,8,1,128]{5,4,3,2,1,0:T(2,128)(2,1)}), bf16[2,3,768,8,1,128]{5,4,3,2,1,0:T(2,128)(2,1)}) %all-gather.3.cloned.1.call-update) | async-done | bytes 9437200 | tf_op jit(solution)/shard_map/all_gather | solution.py:64
  126.9 13.2 %copy.80 = bf16[2,3,768,8,1,128]{5,3,4,2,1,0:T(8,128)(2,1)} copy(bf16[2,3,768,8,1,128]{5,4,3,2,1,0:T(2,128)(2,1)} %all-gather.3.cloned.1.call-done) | data formatting | bytes 18874368
  140.1 7.8 %gather_fusion.1 = bf16[384,2,3,8,128]{4,3,2,1,0:T(8,128)(2,1)} fusion(bf16[2,3,768,8,128]{4,3,2,1,0:T(8,128)(2,1)} %bitcast.92, s32[1024]{0:T(1024)S(1)} %pad_clamp_fusion.1), kind=kCustom, calls=%fused_computation.1 | custom fusion | bytes 9438720 | tf_op jit(solution)/shard_map/gather | solution.py:65
  153.2 262.7 %while.10 = (s32[]{:T(128)}, bf16[6,3,4,128,128]{4,3,2,1,0:T(8,128)(2,1)}, s32[6]{0:T(128)S(1)}, pred[24,128]{1,0:T(8,128)(4,1)}, bf16[3,24,128,128]{3,2,1,0:T(8...) while((s32[]{:T(128)}, ...), condition=%wide.region_4.5_spmd, body=%wide.region_1.4_spmd.sunk | while | flops 1775171840 | bytes 131407576 | solution.py:94
  154.5 11.0 %gather_fusion = bf16[64,2,3,128,128]{4,3,2,1,0:T(8,128)(2,1)} fusion(bf16[2,3,48,128,128]{4,3,2,1,0:T(8,128)(2,1)} %get-tuple-element.201, s32[1024]{0:T(1024)S(1)} %pad_clamp_fusion.3), kind=kCustom, calls=%fused_computation.clone.1 | custom fusion | bytes 25166080 | tf_op jit(solution)/shard_map/while/body/eval_jaxpr/gather | solution.py:82
  165.5 6.5 %copy.82 = bf16[4,16,2,3,128,128]{5,4,1,0,3,2:T(8,128)(2,1)S(1)} copy(bf16[4,16,2,3,128,128]{5,4,3,2,1,0:T(8,128)(2,1)} %bitcast.82) | data formatting | bytes 25165824 | tf_op jit(solution)/shard_map/while/body/eval_jaxpr/gather | solution.py:82
  180.0 7.7 %fusion.65 = (f32[3,4,128]{2,1,0:T(4,128)S(1)}, f32[3,4,128,2176]{3,2,1,0:T(8,128)S(1)}) fusion(pred[4,2176]{1,0:T(4,128)(4,1)S(1)} %concatenate.15, bf16[3,4,128,128]{3,2,1,0:T(8,128)(2,1)} %get-tuple-element.163, bf16[3,4,2048,128]{3,2,1,0:T(8,128)(2,1)} %bitcast.85, bf16[3,24,128,128]{3,2,1,0:T(8,128)(2,1)} %get-tuple-element.199, s32[]{:T(128)S(6)} %select_n.113), kind=kOutput, calls=%fused_computation.5.clone.1 | convolution fusion | flops 879032832 | bytes 20462084 | tf_op jit(solution)/shard_map/while/body/eval_jaxpr/hgqd,hgkd->hgqk/dot_general | solution.py:33
  190.9 6.0 %fusion.67 = bf16[6,3,4,128,128]{4,3,2,1,0:T(8,128)(2,1)} fusion(bf16[6,3,4,128,128]{4,3,2,1,0:T(8,128)(2,1)} %get-tuple-element.182, s32[]{:T(128)} %get-tuple-element.181, bf16[3,4,128,128]{3,2,1,0:T(8,128)(2,1)} %get-tuple-element.161, bf16[3,4,2048,128]{3,2,1,0:T(8,128)(2,1)} %bitcast.84, f32[3,4,128,2176]{3,2,1,0:T(8,128)S(1)} %get-tuple-element.165, ...), kind=kOutput, calls=%fused_computation.23.clone.1 | convolution fusion | flops 882769920 | bytes 20468736 | tf_op jit(solution)/shard_map/while/body/eval_jaxpr/hgqk,hgkd->hgqd/dot_general | solution.py:39
  198.3 11.0 %gather_fusion = bf16[64,2,3,128,128]{4,3,2,1,0:T(8,128)(2,1)} fusion(bf16[2,3,48,128,128]{4,3,2,1,0:T(8,128)(2,1)} %get-tuple-element.201, s32[1024]{0:T(1024)S(1)} %pad_clamp_fusion.3), kind=kCustom, calls=%fused_computation.clone.1 | custom fusion | bytes 25166080 | tf_op jit(solution)/shard_map/while/body/eval_jaxpr/gather | solution.py:82
  209.3 6.5 %copy.82 = bf16[4,16,2,3,128,128]{5,4,1,0,3,2:T(8,128)(2,1)S(1)} copy(bf16[4,16,2,3,128,128]{5,4,3,2,1,0:T(8,128)(2,1)} %bitcast.82) | data formatting | bytes 25165824 | tf_op jit(solution)/shard_map/while/body/eval_jaxpr/gather | solution.py:82
  223.8 7.7 %fusion.65 = (f32[3,4,128]{2,1,0:T(4,128)S(1)}, f32[3,4,128,2176]{3,2,1,0:T(8,128)S(1)}) fusion(pred[4,2176]{1,0:T(4,128)(4,1)S(1)} %concatenate.15, bf16[3,4,128,128]{3,2,1,0:T(8,128)(2,1)} %get-tuple-element.163, bf16[3,4,2048,128]{3,2,1,0:T(8,128)(2,1)} %bitcast.85, bf16[3,24,128,128]{3,2,1,0:T(8,128)(2,1)} %get-tuple-element.199, s32[]{:T(128)S(6)} %select_n.113), kind=kOutput, calls=%fused_computation.5.clone.1 | convolution fusion | flops 879032832 | bytes 20462084 | tf_op jit(solution)/shard_map/while/body/eval_jaxpr/hgqd,hgkd->hgqk/dot_general | solution.py:33
  234.7 6.0 %fusion.67 = bf16[6,3,4,128,128]{4,3,2,1,0:T(8,128)(2,1)} fusion(bf16[6,3,4,128,128]{4,3,2,1,0:T(8,128)(2,1)} %get-tuple-element.182, s32[]{:T(128)} %get-tuple-element.181, bf16[3,4,128,128]{3,2,1,0:T(8,128)(2,1)} %get-tuple-element.161, bf16[3,4,2048,128]{3,2,1,0:T(8,128)(2,1)} %bitcast.84, f32[3,4,128,2176]{3,2,1,0:T(8,128)S(1)} %get-tuple-element.165, ...), kind=kOutput, calls=%fused_computation.23.clone.1 | convolution fusion | flops 882769920 | bytes 20468736 | tf_op jit(solution)/shard_map/while/body/eval_jaxpr/hgqk,hgkd->hgqd/dot_general | solution.py:39
  242.1 11.0 %gather_fusion = bf16[64,2,3,128,128]{4,3,2,1,0:T(8,128)(2,1)} fusion(bf16[2,3,48,128,128]{4,3,2,1,0:T(8,128)(2,1)} %get-tuple-element.201, s32[1024]{0:T(1024)S(1)} %pad_clamp_fusion.3), kind=kCustom, calls=%fused_computation.clone.1 | custom fusion | bytes 25166080 | tf_op jit(solution)/shard_map/while/body/eval_jaxpr/gather | solution.py:82
  253.1 6.5 %copy.82 = bf16[4,16,2,3,128,128]{5,4,1,0,3,2:T(8,128)(2,1)S(1)} copy(bf16[4,16,2,3,128,128]{5,4,3,2,1,0:T(8,128)(2,1)} %bitcast.82) | data formatting | bytes 25165824 | tf_op jit(solution)/shard_map/while/body/eval_jaxpr/gather | solution.py:82
  267.6 7.7 %fusion.65 = (f32[3,4,128]{2,1,0:T(4,128)S(1)}, f32[3,4,128,2176]{3,2,1,0:T(8,128)S(1)}) fusion(pred[4,2176]{1,0:T(4,128)(4,1)S(1)} %concatenate.15, bf16[3,4,128,128]{3,2,1,0:T(8,128)(2,1)} %get-tuple-element.163, bf16[3,4,2048,128]{3,2,1,0:T(8,128)(2,1)} %bitcast.85, bf16[3,24,128,128]{3,2,1,0:T(8,128)(2,1)} %get-tuple-element.199, s32[]{:T(128)S(6)} %select_n.113), kind=kOutput, calls=%fused_computation.5.clone.1 | convolution fusion | flops 879032832 | bytes 20462084 | tf_op jit(solution)/shard_map/while/body/eval_jaxpr/hgqd,hgkd->hgqk/dot_general | solution.py:33
  278.5 6.0 %fusion.67 = bf16[6,3,4,128,128]{4,3,2,1,0:T(8,128)(2,1)} fusion(bf16[6,3,4,128,128]{4,3,2,1,0:T(8,128)(2,1)} %get-tuple-element.182, s32[]{:T(128)} %get-tuple-element.181, bf16[3,4,128,128]{3,2,1,0:T(8,128)(2,1)} %get-tuple-element.161, bf16[3,4,2048,128]{3,2,1,0:T(8,128)(2,1)} %bitcast.84, f32[3,4,128,2176]{3,2,1,0:T(8,128)S(1)} %get-tuple-element.165, ...), kind=kOutput, calls=%fused_computation.23.clone.1 | convolution fusion | flops 882769920 | bytes 20468736 | tf_op jit(solution)/shard_map/while/body/eval_jaxpr/hgqk,hgkd->hgqd/dot_general | solution.py:39
  285.9 11.0 %gather_fusion = bf16[64,2,3,128,128]{4,3,2,1,0:T(8,128)(2,1)} fusion(bf16[2,3,48,128,128]{4,3,2,1,0:T(8,128)(2,1)} %get-tuple-element.201, s32[1024]{0:T(1024)S(1)} %pad_clamp_fusion.3), kind=kCustom, calls=%fused_computation.clone.1 | custom fusion | bytes 25166080 | tf_op jit(solution)/shard_map/while/body/eval_jaxpr/gather | solution.py:82
  296.9 6.5 %copy.82 = bf16[4,16,2,3,128,128]{5,4,1,0,3,2:T(8,128)(2,1)S(1)} copy(bf16[4,16,2,3,128,128]{5,4,3,2,1,0:T(8,128)(2,1)} %bitcast.82) | data formatting | bytes 25165824 | tf_op jit(solution)/shard_map/while/body/eval_jaxpr/gather | solution.py:82
  311.4 7.7 %fusion.65 = (f32[3,4,128]{2,1,0:T(4,128)S(1)}, f32[3,4,128,2176]{3,2,1,0:T(8,128)S(1)}) fusion(pred[4,2176]{1,0:T(4,128)(4,1)S(1)} %concatenate.15, bf16[3,4,128,128]{3,2,1,0:T(8,128)(2,1)} %get-tuple-element.163, bf16[3,4,2048,128]{3,2,1,0:T(8,128)(2,1)} %bitcast.85, bf16[3,24,128,128]{3,2,1,0:T(8,128)(2,1)} %get-tuple-element.199, s32[]{:T(128)S(6)} %select_n.113), kind=kOutput, calls=%fused_computation.5.clone.1 | convolution fusion | flops 879032832 | bytes 20462084 | tf_op jit(solution)/shard_map/while/body/eval_jaxpr/hgqd,hgkd->hgqk/dot_general | solution.py:33
  322.3 6.0 %fusion.67 = bf16[6,3,4,128,128]{4,3,2,1,0:T(8,128)(2,1)} fusion(bf16[6,3,4,128,128]{4,3,2,1,0:T(8,128)(2,1)} %get-tuple-element.182, s32[]{:T(128)} %get-tuple-element.181, bf16[3,4,128,128]{3,2,1,0:T(8,128)(2,1)} %get-tuple-element.161, bf16[3,4,2048,128]{3,2,1,0:T(8,128)(2,1)} %bitcast.84, f32[3,4,128,2176]{3,2,1,0:T(8,128)S(1)} %get-tuple-element.165, ...), kind=kOutput, calls=%fused_computation.23.clone.1 | convolution fusion | flops 882769920 | bytes 20468736 | tf_op jit(solution)/shard_map/while/body/eval_jaxpr/hgqk,hgkd->hgqd/dot_general | solution.py:39
  329.7 11.0 %gather_fusion = bf16[64,2,3,128,128]{4,3,2,1,0:T(8,128)(2,1)} fusion(bf16[2,3,48,128,128]{4,3,2,1,0:T(8,128)(2,1)} %get-tuple-element.201, s32[1024]{0:T(1024)S(1)} %pad_clamp_fusion.3), kind=kCustom, calls=%fused_computation.clone.1 | custom fusion | bytes 25166080 | tf_op jit(solution)/shard_map/while/body/eval_jaxpr/gather | solution.py:82
  340.7 6.5 %copy.82 = bf16[4,16,2,3,128,128]{5,4,1,0,3,2:T(8,128)(2,1)S(1)} copy(bf16[4,16,2,3,128,128]{5,4,3,2,1,0:T(8,128)(2,1)} %bitcast.82) | data formatting | bytes 25165824 | tf_op jit(solution)/shard_map/while/body/eval_jaxpr/gather | solution.py:82
  355.1 7.7 %fusion.65 = (f32[3,4,128]{2,1,0:T(4,128)S(1)}, f32[3,4,128,2176]{3,2,1,0:T(8,128)S(1)}) fusion(pred[4,2176]{1,0:T(4,128)(4,1)S(1)} %concatenate.15, bf16[3,4,128,128]{3,2,1,0:T(8,128)(2,1)} %get-tuple-element.163, bf16[3,4,2048,128]{3,2,1,0:T(8,128)(2,1)} %bitcast.85, bf16[3,24,128,128]{3,2,1,0:T(8,128)(2,1)} %get-tuple-element.199, s32[]{:T(128)S(6)} %select_n.113), kind=kOutput, calls=%fused_computation.5.clone.1 | convolution fusion | flops 879032832 | bytes 20462084 | tf_op jit(solution)/shard_map/while/body/eval_jaxpr/hgqd,hgkd->hgqk/dot_general | solution.py:33
  366.1 6.0 %fusion.67 = bf16[6,3,4,128,128]{4,3,2,1,0:T(8,128)(2,1)} fusion(bf16[6,3,4,128,128]{4,3,2,1,0:T(8,128)(2,1)} %get-tuple-element.182, s32[]{:T(128)} %get-tuple-element.181, bf16[3,4,128,128]{3,2,1,0:T(8,128)(2,1)} %get-tuple-element.161, bf16[3,4,2048,128]{3,2,1,0:T(8,128)(2,1)} %bitcast.84, f32[3,4,128,2176]{3,2,1,0:T(8,128)S(1)} %get-tuple-element.165, ...), kind=kOutput, calls=%fused_computation.23.clone.1 | convolution fusion | flops 882769920 | bytes 20468736 | tf_op jit(solution)/shard_map/while/body/eval_jaxpr/hgqk,hgkd->hgqd/dot_general | solution.py:39
  373.5 11.0 %gather_fusion = bf16[64,2,3,128,128]{4,3,2,1,0:T(8,128)(2,1)} fusion(bf16[2,3,48,128,128]{4,3,2,1,0:T(8,128)(2,1)} %get-tuple-element.201, s32[1024]{0:T(1024)S(1)} %pad_clamp_fusion.3), kind=kCustom, calls=%fused_computation.clone.1 | custom fusion | bytes 25166080 | tf_op jit(solution)/shard_map/while/body/eval_jaxpr/gather | solution.py:82
  384.5 6.5 %copy.82 = bf16[4,16,2,3,128,128]{5,4,1,0,3,2:T(8,128)(2,1)S(1)} copy(bf16[4,16,2,3,128,128]{5,4,3,2,1,0:T(8,128)(2,1)} %bitcast.82) | data formatting | bytes 25165824 | tf_op jit(solution)/shard_map/while/body/eval_jaxpr/gather | solution.py:82
  398.9 7.7 %fusion.65 = (f32[3,4,128]{2,1,0:T(4,128)S(1)}, f32[3,4,128,2176]{3,2,1,0:T(8,128)S(1)}) fusion(pred[4,2176]{1,0:T(4,128)(4,1)S(1)} %concatenate.15, bf16[3,4,128,128]{3,2,1,0:T(8,128)(2,1)} %get-tuple-element.163, bf16[3,4,2048,128]{3,2,1,0:T(8,128)(2,1)} %bitcast.85, bf16[3,24,128,128]{3,2,1,0:T(8,128)(2,1)} %get-tuple-element.199, s32[]{:T(128)S(6)} %select_n.113), kind=kOutput, calls=%fused_computation.5.clone.1 | convolution fusion | flops 879032832 | bytes 20462084 | tf_op jit(solution)/shard_map/while/body/eval_jaxpr/hgqd,hgkd->hgqk/dot_general | solution.py:33
  409.8 6.0 %fusion.67 = bf16[6,3,4,128,128]{4,3,2,1,0:T(8,128)(2,1)} fusion(bf16[6,3,4,128,128]{4,3,2,1,0:T(8,128)(2,1)} %get-tuple-element.182, s32[]{:T(128)} %get-tuple-element.181, bf16[3,4,128,128]{3,2,1,0:T(8,128)(2,1)} %get-tuple-element.161, bf16[3,4,2048,128]{3,2,1,0:T(8,128)(2,1)} %bitcast.84, f32[3,4,128,2176]{3,2,1,0:T(8,128)S(1)} %get-tuple-element.165, ...), kind=kOutput, calls=%fused_computation.23.clone.1 | convolution fusion | flops 882769920 | bytes 20468736 | tf_op jit(solution)/shard_map/while/body/eval_jaxpr/hgqk,hgkd->hgqd/dot_general | solution.py:39
  423.0 9.3 %convolution_convert_fusion = bf16[3072,1536]{1,0:T(8,128)(2,1)} fusion(bf16[3072,384]{0,1:T(8,128)(2,1)} %reshape.106, bf16[384,1536]{1,0:T(8,128)(2,1)S(1)} %copy-done), kind=kOutput, calls=%fused_computation.35 | convolution fusion | flops 3628597248 | bytes 12976128 | tf_op jit(solution)/shard_map/dot_general | solution.py:97
  432.4 88.5 %reduce-scatter.2.cloned.1.call-done = bf16[768,1536]{1,0:T(8,128)(2,1)} async-done(((bf16[3072,1536]{1,0:T(8,128)(2,1)}), bf16[768,1536]{1,0:T(8,128)(2,1)}) %reduce-scatter.2.cloned.1.call-update) | async-done | bytes 2359312 | tf_op jit(solution)/shard_map/reduce_scatter | solution.py:96
  (97 shorter events, 127.1 us)
Async XLA Ops:
  6.5 416.5 %copy-start = (bf16[384,1536]{1,0:T(8,128)(2,1)S(1)}, bf16[384,1536]{1,0:T(8,128)(2,1)}, u32[]{:S(2)}) copy-start(bf16[384,1536]{1,0:T(8,128)(2,1)} %param.12) | copy-start | bytes 3538948
  6.5 120.3 %all-gather.3.cloned.1.call-start = ((), (), s32[]{:S(2)}) async-start(), calls=%async_computation.2 | async-start | bytes 19464192 | tf_op jit(solution)/shard_map/all_gather | solution.py:64
  23.4 10.0 %copy-start.1 = (s32[64]{0:T(128)S(1)}, s32[64]{0:T(128)}, u32[]{:S(2)}) copy-start(s32[64]{0:T(128)} %param.15) | copy-start | bytes 772
  23.5 497.4 %reduce-scatter.2.cloned.1.call-start = ((), (), s32[]{:S(2)}) async-start(), calls=%async_computation.1 | async-start | bytes 11796480 | tf_op jit(solution)/shard_map/reduce_scatter | solution.py:96
  27.2 22.6 %collective-permute-start = (bf16[2,3,1536,128]{2,3,1,0:T(8,128)(2,1)}, bf16[2,3,1536,128]{2,3,1,0:T(8,128)(2,1)}, u32[]{:S(2)}, u32[]{:S(2)}) collective-permute-start(bf16[2,3,1536,128]{2,3,1,0:T(8,128)(2,1)} %get-tuple-element.104), channel_id=1, source_target_pairs={{0,4},{4,8},{8,12},{12,16},{16,20},{20,24},{24,28},{28,32},{32,36}... | collective-permute-start | bytes 7077896 | tf_op jit(solution)/shard_map/ppermute | solution.py:23
  29.9 19.8 %collective-permute-start.1 = (bf16[2,3,1536,128]{2,3,1,0:T(8,128)(2,1)}, bf16[2,3,1536,128]{2,3,1,0:T(8,128)(2,1)}, u32[]{:S(2)}, u32[]{:S(2)}) collective-permute-start(bf16[2,3,1536,128]{2,3,1,0:T(8,128)(2,1)} %get-tuple-element.105), channel_id=1, source_target_pairs={{4,0},{8,4},{12,8},{16,12},{20,16},{24,20},{28,24},{32,28},{36,32}... | collective-permute-start | bytes 7077896 | tf_op jit(solution)/shard_map/ppermute | solution.py:24
Sparse Core Ops, SparseCore 0:
  23.6 103.2 all-gather.2
  432.5 88.3 reduce-scatter.1
where the time goes:
time: 531 us; the launch traced here: 528 us
  local copies, waits for them, and re-layouts  230 us (43%)
  waiting for transfers between devices  146 us (27%)
  matrix products  91.7 us (17%)
  other arithmetic  38.7 us (7%)
  between operations  13.5 us (3%)
    gather x12, local copies, waits for them, and re-layouts, group_step(): near_pair = extended[:, :, chosen].reshape(2, heads, 4, KNEAR * BLK, HD)  105 us
    reduce_scatter x1, waiting for transfers between devices, per_device(): lax.psum_scatter(jnp.dot(attended, out_weight, preferred_element_type=jnp...  88.5 us
    all_gather x1, waiting for transfers between devices, per_device(): everything = lax.all_gather(thinned, 'tm', axis=2, tiled=True)  57.3 us
    dot_general x6, matrix products, attend_group(): jnp.einsum('hgqd,hgkd->hgqk', queries, key_rows, preferred_element_type=j...  46.1 us
    dot_general x6, matrix products, attend_group(): jnp.einsum('hgqk,hgkd->hgqd', weights.astype(jnp.bfloat16), value_rows, p...  36.3 us
    slice x6, local copies, waits for them, and re-layouts, group_step(): near_pair[0]  31 us
    unnamed x8, local copies, waits for them, and re-layouts  24.7 us
    reduce_sum x6, other arithmetic, attend_group(): totals = jnp.sum(weights, axis=-1)  19.5 us
  transfers between devices with their start and end apart: 4, of which 2 were waited for; matrix products, arithmetic and copies ran while one was open for 8% of the time, Pallas kernels for 0%

commit v1 on v0

v1 whole, which is shorter than its diff:
```python
import functools
import math

import jax
import jax.numpy as jnp
from jax import lax
from jax.experimental import pallas as pl
from jax.experimental.pallas import tpu as pltpu
from jax.sharding import PartitionSpec as P

HD = 128
BLK = 128
FRAME_BLK = 12
KNEAR = 16
KFAR = 16
CAP = 6
MINSTRIDE = 16
THIN = BLK // MINSTRIDE
HEADS = 3
WIDTH = HEADS * HD
BLOCKS = 24
NX, NZ, NC = 4, 4, 2
NTM = NX * NZ * NC
NHEAD = 4
CHUNK = BLOCKS // NHEAD
FRAME = FRAME_BLK * BLK
LOG2_SCALE = math.log2(math.e) / math.sqrt(HD)
NT = (((1,), (1,)), ((), ()))
VMEM_LIMIT = 56 * 2**20


def tm_index(z, x, c):
    return (z % NZ) * NX * NC + (x % NX) * NC + c


def far_block(far_vm, slots, strides, base):
    tiles = [
        far_vm[pl.ds(pl.multiple_of(slots[base + j] * 2 * THIN, 2 * THIN), 2 * THIN), :].astype(
            jnp.float32
        )
        for j in range(KFAR)
    ]
    keys = jnp.concatenate([t[:THIN] for t in tiles], axis=0).astype(jnp.bfloat16)
    values = jnp.concatenate([t[THIN:] for t in tiles], axis=0).astype(jnp.bfloat16)
    lane = lax.broadcasted_iota(jnp.int32, (1, BLK), 1)
    stride = jnp.zeros((1, BLK), jnp.int32)
    for j in range(KFAR):
        stride = jnp.where(lane // THIN == j, strides[base + j], stride)
    used = (((lane % THIN) * MINSTRIDE) & (stride - 1)) == 0
    return keys, values, used


def with_ones(values):
    return jnp.concatenate([values, jnp.ones((values.shape[0], HD), jnp.bfloat16)], axis=1)


def attend_kernel(
    scalars, near, slots, strides, q_ref, k_ref, v_ref, halo_ref, *rest, per_step, with_far
):
    if with_far:
        far_refs, (out_ref, k_vm, v_vm, far_vm, sems) = rest[:8], rest[8:]
    else:
        acc_ref, stat_ref, k_vm, v_vm, sems = rest
    step = pl.program_id(0)
    own = BLOCKS * BLK

    @pl.when(step == 0)
    def _():
        copies = [
            pltpu.make_async_copy(k_ref, k_vm.at[pl.ds(0, own)], sems.at[0]),
            pltpu.make_async_copy(v_ref, v_vm.at[pl.ds(0, own)], sems.at[1]),
            pltpu.make_async_copy(halo_ref.at[0], k_vm.at[pl.ds(own, FRAME)], sems.at[2]),
            pltpu.make_async_copy(halo_ref.at[1], v_vm.at[pl.ds(own, FRAME)], sems.at[3]),
        ]
        if with_far:
            rows = far_refs[0].shape[0]
            for n, ref in enumerate(far_refs):
                copies.append(
                    pltpu.make_async_copy(ref, far_vm.at[pl.ds(n * rows, rows)], sems.at[4 + n])
                )
        for copy in copies:
            copy.start()
        for copy in copies:
            copy.wait()

    first = scalars[0] + step * per_step
    prepared = {}

    def prepare(unit):
        if unit not in prepared:
            base = (first + unit) * KNEAR
            offsets = [pl.multiple_of(near[base + j] * BLK, BLK) for j in range(KNEAR)]
            far = far_block(far_vm, slots, strides, base) if with_far else None
            prepared[unit] = offsets, far
        return prepared[unit]

    def scores_of(unit, head):
        offsets, far = prepare(unit)
        cols = slice(head * HD, head * HD + HD)
        query = q_ref[unit * BLK : unit * BLK + BLK, cols]
        scores = []
        for j in range(0, KNEAR, 2):
            keys = jnp.concatenate([k_vm[pl.ds(o, BLK), cols] for o in offsets[j : j + 2]], axis=0)
            both = lax.dot_general(query, keys, NT, preferred_element_type=jnp.float32)
            scores += [both[:, :BLK], both[:, BLK:]]
        if with_far:
            last = lax.dot_general(query, far[0][:, cols], NT, preferred_element_type=jnp.float32)
            scores.append(jnp.where(far[2], last, -1e30))
        return scores

    def finish(unit, head, scores):
        offsets, far = prepare(unit)
        cols = slice(head * HD, head * HD + HD)
        rows = slice(unit * BLK, unit * BLK + BLK)
        peak = (
            jnp.max(functools.reduce(jnp.maximum, scores), axis=1, keepdims=True) * LOG2_SCALE
        )
        acc = jnp.zeros((BLK, 2 * HD), jnp.float32)
        for j in range(0, len(scores), 2):
            some = range(j, min(j + 2, len(scores)))
            weights = jnp.concatenate(
                [jnp.exp2(scores[i] * LOG2_SCALE - peak).astype(jnp.bfloat16) for i in some], axis=1
            )
            values = jnp.concatenate(
                [
                    v_vm[pl.ds(offsets[i], BLK), cols] if i < KNEAR else far[1][:, cols]
                    for i in some
                ],
                axis=0,
            )
            acc += jnp.dot(weights, with_ones(values), preferred_element_type=jnp.float32)
        if with_far:
            out_ref[rows, cols] = (acc[:, :HD] / acc[:, HD : HD + 1]).astype(jnp.bfloat16)
        else:
            acc_ref[rows, cols] = acc[:, :HD]
            lane = lax.broadcasted_iota(jnp.int32, (BLK, HD), 1)
            held = stat_ref[rows, :] if head else jnp.zeros((BLK, HD), jnp.float32)
            held = jnp.where(lane == head, peak, held)
            stat_ref[rows, :] = jnp.where(lane == HEADS + head, acc[:, HD:], held)

    pending = None
    for unit in range(per_step):
        for head in range(HEADS):
            scores = scores_of(unit, head)
            if pending:
                finish(*pending)
            pending = unit, head, scores
    finish(*pending)


def attend(scalars, near, slots, strides, query, keys, values, halo, far, blocks, per_step):
    with_far = far is not None
    spot = lambda i, s, *_: (s[0] // per_step + i, 0)
    same = lambda i, *_: (i, 0)
    anywhere = pl.BlockSpec(memory_space=pl.ANY)
    rows = blocks * BLK
    step_rows = per_step * BLK
    scratch = [pltpu.VMEM((BLOCKS * BLK + FRAME, WIDTH), jnp.bfloat16) for _ in range(2)]
    if with_far:
        scratch.append(pltpu.VMEM((8 * far[0].shape[0], WIDTH), jnp.bfloat16))
        out_shape = jax.ShapeDtypeStruct((rows, WIDTH), jnp.bfloat16)
        out_specs = pl.BlockSpec((step_rows, WIDTH), same)
    else:
        out_shape = (
            jax.ShapeDtypeStruct((rows, WIDTH), jnp.float32),
            jax.ShapeDtypeStruct((rows, HD), jnp.float32),
        )
        out_specs = (pl.BlockSpec((step_rows, WIDTH), same), pl.BlockSpec((step_rows, HD), same))
    scratch.append(pltpu.SemaphoreType.DMA((12,)))
    extra = tuple(far) if with_far else ()
    return pl.pallas_call(
        functools.partial(attend_kernel, per_step=per_step, with_far=with_far),
        grid_spec=pltpu.PrefetchScalarGridSpec(
            num_scalar_prefetch=4,
            grid=(blocks // per_step,),
            in_specs=[pl.BlockSpec((step_rows, WIDTH), spot)] + [anywhere] * (3 + len(extra)),
            out_specs=out_specs,
            scratch_shapes=scratch,
        ),
        out_shape=out_shape,
        compiler_params=pltpu.CompilerParams(vmem_limit_bytes=VMEM_LIMIT),
        cost_estimate=pl.CostEstimate(
            flops=blocks * HEADS * 17 * 4 * BLK * BLK * HD * 3,
            bytes_accessed=8 * 2**20,
            transcendentals=0,
        ),
    )(scalars, near, slots, strides, query, keys, values, halo, *extra)


def merge_kernel(scalars, slots, strides, q_ref, acc_ref, stat_ref, *rest, per_step):
    far_refs, (out_ref, far_vm, sems) = rest[:8], rest[8:]
    step = pl.program_id(0)

    @pl.when(step == 0)
    def _():
        rows = far_refs[0].shape[0]
        copies = [
            pltpu.make_async_copy(ref, far_vm.at[pl.ds(n * rows, rows)], sems.at[n])
            for n, ref in enumerate(far_refs)
        ]
        for copy in copies:
            copy.start()
        for copy in copies:
            copy.wait()

    first = scalars[0] + step * per_step
    for unit in range(per_step):
        keys, values, used = far_block(far_vm, slots, strides, (first + unit) * KFAR)
        rows = slice(unit * BLK, unit * BLK + BLK)
        for head in range(HEADS):
            cols = slice(head * HD, head * HD + HD)
            scores = lax.dot_general(
                q_ref[rows, cols], keys[:, cols], NT, preferred_element_type=jnp.float32
            )
            scores = jnp.where(used, scores, -1e30) * LOG2_SCALE
            held = stat_ref[rows, head : head + 1]
            peak = jnp.maximum(jnp.max(scores, axis=1, keepdims=True), held)
            weights = jnp.exp2(scores - peak).astype(jnp.bfloat16)
            acc = jnp.dot(weights, with_ones(values[:, cols]), preferred_element_type=jnp.float32)
            shrink = jnp.exp2(held - peak)
            total = shrink * stat_ref[rows, HEADS + head : HEADS + head + 1] + acc[:, HD : HD + 1]
            mixed = shrink * acc_ref[rows, cols] + acc[:, :HD]
            out_ref[rows, cols] = (mixed / total).astype(jnp.bfloat16)


def merge_far(scalars, slots, strides, query, acc, stat, far, blocks, per_step):
    spot = lambda i, s, *_: (s[0] // per_step + i, 0)
    same = lambda i, *_: (i, 0)
    step_rows = per_step * BLK
    return pl.pallas_call(
        functools.partial(merge_kernel, per_step=per_step),
        grid_spec=pltpu.PrefetchScalarGridSpec(
            num_scalar_prefetch=3,
            grid=(blocks // per_step,),
            in_specs=[
                pl.BlockSpec((step_rows, WIDTH), spot),
                pl.BlockSpec((step_rows, WIDTH), same),
                pl.BlockSpec((step_rows, HD), same),
            ]
            + [pl.BlockSpec(memory_space=pl.ANY)] * 8,
            out_specs=pl.BlockSpec((step_rows, WIDTH), same),
            scratch_shapes=[
                pltpu.VMEM((8 * far[0].shape[0], WIDTH), jnp.bfloat16),
                pltpu.SemaphoreType.DMA((8,)),
            ],
        ),
        out_shape=jax.ShapeDtypeStruct((blocks * BLK, WIDTH), jnp.bfloat16),
        compiler_params=pltpu.CompilerParams(vmem_limit_bytes=VMEM_LIMIT),
        cost_estimate=pl.CostEstimate(
            flops=blocks * HEADS * 4 * BLK * BLK * HD * 6, bytes_accessed=8 * 2**20, transcendentals=0
        ),
    )(scalars, slots, strides, query, acc, stat, *far)


def select_kernel(picks, *refs):
    sources, outs = refs[:NX], refs[NX:]
    per = NX * CAP
    for n, out in enumerate(outs):

        def move(i, _, n=n, out=out):
            for s in range(NX):
                block = picks[n * per + s * CAP + i]
                at = pl.ds(pl.multiple_of(block * 2 * THIN, 2 * THIN), 2 * THIN)
                to = pl.ds(pl.multiple_of((s * CAP + i) * 2 * THIN, 2 * THIN), 2 * THIN)
                out[to, :] = sources[s][at, :]
            return 0

        lax.fori_loop(0, CAP, move, 0, unroll=True)


def select(picks, sources):
    shape = jax.ShapeDtypeStruct((NX * CAP * 2 * THIN, WIDTH), jnp.bfloat16)
    whole = lambda a: pl.BlockSpec(a.shape, lambda i, *_: (0, 0))
    return pl.pallas_call(
        select_kernel,
        grid_spec=pltpu.PrefetchScalarGridSpec(
            num_scalar_prefetch=1,
            grid=(1,),
            in_specs=[whole(s) for s in sources],
            out_specs=[whole(shape)] * (NZ * NC),
        ),
        out_shape=[shape] * (NZ * NC),
        compiler_params=pltpu.CompilerParams(vmem_limit_bytes=VMEM_LIMIT),
    )(picks, *sources)


def project_kernel(scalars, a0, a1, a2, a3, w0, w1, w2, w3, out_ref):
    total = None
    for a, w in ((a0, w0), (a1, w1), (a2, w2), (a3, w3)):
        part = jnp.dot(a[...], w[0, 0], preferred_element_type=jnp.float32)
        part = part.astype(jnp.bfloat16).astype(jnp.float32)
        total = part if total is None else total + part
    out_ref[...] = total.astype(jnp.bfloat16)


def project(scalars, parts, weights):
    halves, _, depth, cols = weights.shape
    rows = parts[0].shape[0]
    tile = rows // 3
    weight_spec = lambda n: pl.BlockSpec((1, 1, depth, cols), lambda c, r, s: (c, s[n], 0, 0))
    return pl.pallas_call(
        project_kernel,
        grid_spec=pltpu.PrefetchScalarGridSpec(
            num_scalar_prefetch=1,
            grid=(halves, 3),
            in_specs=[pl.BlockSpec((tile, depth), lambda c, r, s: (r, 0))] * NHEAD
            + [weight_spec(n) for n in range(NHEAD)],
            out_specs=pl.BlockSpec((tile, cols), lambda c, r, s: (r, c)),
        ),
        out_shape=jax.ShapeDtypeStruct((rows, halves * cols), jnp.bfloat16),
        compiler_params=pltpu.CompilerParams(vmem_limit_bytes=VMEM_LIMIT),
        cost_estimate=pl.CostEstimate(
            flops=2 * rows * NHEAD * depth * halves * cols,
            bytes_accessed=10 * 2**20,
            transcendentals=0,
        ),
    )(scalars, *parts, *([weights] * NHEAD))


def per_device(query, keys, values, out_weight, near_list, far_list, stride_table):
    t = lax.axis_index("tm")
    h = lax.axis_index("head")
    core, x, z = t % NC, (t // NC) % NX, t // (NC * NX)
    fast_frame = 1 - core
    coords = [(zz, xx, cc) for zz in range(NZ) for xx in range(NX) for cc in range(NC)]

    def thin(a):
        return a.reshape(BLOCKS, THIN, MINSTRIDE, WIDTH)[:, :, 0]

    thinned = jnp.concatenate([thin(keys), thin(values)], axis=1).reshape(-1, WIDTH)

    def frame_of(index):
        return jnp.stack(
            [lax.dynamic_slice_in_dim(a, index * FRAME, FRAME, 0) for a in (keys, values)]
        )

    swap = [(i, i ^ 1) for i in range(NTM)]
    across = [(i, i + 1) for i in range(1, NTM - 1, 2)]
    across = across + [(j, i) for i, j in across]
    along_x = [
        lax.ppermute(
            thinned, "tm", [(tm_index(*p), tm_index(p[0], p[1] + d, p[2])) for p in coords]
        )
        for d in range(1, NX)
    ]
    halo_fast = lax.ppermute(frame_of(fast_frame), "tm", swap)

    cols = out_weight.shape[1] // NC
    half = lax.dynamic_slice_in_dim(out_weight, core * cols, cols, 1)
    gathered = lax.all_gather(half, "head", axis=0)
    weights = lax.all_gather(
        gathered, "tm", axis=0, axis_index_groups=[[i, i + 1] for i in range(0, NTM, 2)]
    )

    listed = far_list.reshape(NTM, BLOCKS * KFAR)
    block_ids = jnp.arange(BLOCKS, dtype=jnp.int32)

    wanted = lax.dynamic_slice_in_dim(
        listed.reshape(NZ, NX, NC, -1), x, 1, 1
    )[:, 0]
    order = [(dz, dc) for dz in range(NZ) for dc in range(NC)]
    receivers = jnp.stack([((z + dz) % NZ) * NC + (core ^ dc) for dz, dc in order])
    wanted = wanted.reshape(NZ * NC, -1)[receivers]
    source = jnp.stack([tm_index(z, x - dx + NX, core) for dx in range(NX)])
    target = source[:, None] * BLOCKS + block_ids[None, :]
    present = jnp.any(wanted[:, None, None, :] == target[None, :, :, None], axis=-1)
    rank = jnp.cumsum(present.astype(jnp.int32), axis=-1) - 1
    hit = present[..., None] & (rank[..., None] == jnp.arange(CAP, dtype=jnp.int32))
    picks = jnp.sum(jnp.where(hit, block_ids[:, None], 0), axis=2).reshape(-1)

    mine = lax.dynamic_slice_in_dim(listed, t, 1, 0)[0]
    ids = jnp.arange(NTM * BLOCKS, dtype=jnp.int32)
    have = jnp.any(mine[:, None] == ids[None, :], axis=0).reshape(NTM, BLOCKS)
    place = jnp.cumsum(have.astype(jnp.int32), axis=-1) - 1
    device = jnp.arange(NTM, dtype=jnp.int32)
    dz = (z - device // (NX * NC)) % NZ
    dx = (x - (device // NC) % NX) % NX
    dc = core ^ (device % NC)
    lies = (((dz * NC + dc) * NX + dx) * CAP)[:, None] + place
    slots = jnp.sum(jnp.where(mine[:, None] == ids[None, :], lies.reshape(-1)[None, :], 0), axis=1)
    row_frame = (t * BLOCKS + jnp.arange(BLOCKS * KFAR, dtype=jnp.int32) // KFAR) // FRAME_BLK
    distance = jnp.abs(row_frame - mine // FRAME_BLK)
    frames = jnp.arange(stride_table.shape[0], dtype=jnp.int32)
    strides = jnp.sum(
        jnp.where(distance[:, None] == frames[None, :], stride_table[None, :], 0), axis=1
    )

    local = near_list - t * BLOCKS
    near = jnp.where(local < 0, local + FRAME_BLK + BLOCKS, local).reshape(-1)

    packs = select(picks, [thinned] + along_x)
    slow_part, packs = lax.optimization_barrier((frame_of(core), packs))
    far = [packs[0]]
    for n, (dz_, dc_) in enumerate(order):
        if n:
            pairs = [(tm_index(*p), tm_index(p[0] + dz_, p[1], p[2] ^ dc_)) for p in coords]
            far.append(lax.ppermute(packs[n], "tm", pairs))
    halo_slow = lax.ppermute(slow_part, "tm", across)

    def start_at(block):
        return jnp.stack([block]).astype(jnp.int32)

    fast_start = start_at(fast_frame * FRAME_BLK)
    acc, stat = attend(
        fast_start, near, slots, strides, query, keys, values, halo_fast, None, FRAME_BLK, 4
    )
    done_fast = merge_far(fast_start, slots, strides, query, acc, stat, far, FRAME_BLK, 4)

    slow_frame = core
    in_half = (h // 2) == slow_frame
    first_dest = jnp.where(in_half, h ^ 1, h ^ 2)
    last_dest = jnp.where(in_half, h, h ^ 3)
    early, late = [
        attend(
            start_at(dest * CHUNK),
            near,
            slots,
            strides,
            query,
            keys,
            values,
            halo_slow,
            far,
            CHUNK,
            CHUNK,
        )
        for dest in (first_dest, last_dest)
    ]

    def exchange(chunk, e, fast):
        pairs = []
        for c in range(NC):
            frame = 1 - c if fast else c
            for i in range(NTM):
                if i % NC == c:
                    for g in range(NHEAD):
                        if (e >= 2) == (g // 2 != frame):
                            pairs.append((i * NHEAD + g, i * NHEAD + (g ^ e)))
        return lax.ppermute(chunk, ("tm", "head"), pairs)

    def fast_chunk(dest):
        return lax.dynamic_slice_in_dim(done_fast, (dest % 2) * CHUNK * BLK, CHUNK * BLK, 0)

    gets_fast = (h // 2) == fast_frame
    parts = [jnp.where(gets_fast, fast_chunk(h), late)]
    for e, chunk in ((1, early), (2, early), (3, late)):
        received_fast = exchange(fast_chunk(h ^ e), e, True)
        received_slow = exchange(chunk, e, False)
        parts.append(jnp.where(gets_fast, received_fast, received_slow))
    scalars = jnp.stack([h, h ^ 1, h ^ 2, h ^ 3]).astype(jnp.int32)
    return project(scalars, parts, weights)


def solution(mesh):
    placed = (
        P("tm", "head"),
        P("tm", "head"),
        P("tm", "head"),
        P("head", None),
        P("tm", None),
        P(),
        P(),
    )
    return jax.shard_map(
        per_device, mesh=mesh, in_specs=placed, out_specs=P(("tm", "head"), None), check_vma=False
    )
```

time: 531 us -> 228 us (0.43)
  the two profiles are of different devices: /device:TPU:0 before, /device:TPU:97 now
where the time goes in v1:
time: 228 us; the launch traced here: 226 us
  Pallas kernels  77.5 us (34%)
  waiting for transfers between devices  56.6 us (25%)
  starting transfers between devices  40.2 us (18%)
  local copies, waits for them, and re-layouts  21 us (9%)
  other arithmetic  17.1 us (8%)
  between operations  13.9 us (6%)
    pallas_call x3, Pallas kernels, attend(): pl.pallas_call(functools.partial(attend_kernel, per_step=per_step, with_f...  46 us
    ppermute x7, waiting for transfers between devices, per_device(): far.append(lax.ppermute(packs[n], 'tm', pairs))  32.1 us
    ppermute x6, waiting for transfers between devices, exchange(): return lax.ppermute(chunk, ('tm', 'head'), pairs)  24.5 us
    ppermute x7, starting transfers between devices, per_device(): far.append(lax.ppermute(packs[n], 'tm', pairs))  18.1 us
    pallas_call x1, Pallas kernels, merge_far(): pl.pallas_call(functools.partial(merge_kernel, per_step=per_step), grid_s...  17 us
    ppermute x6, starting transfers between devices, exchange(): return lax.ppermute(chunk, ('tm', 'head'), pairs)  13.7 us
    pallas_call x1, Pallas kernels, project(): pl.pallas_call(project_kernel, grid_spec=pltpu.PrefetchScalarGridSpec(num...  10.8 us
    ppermute x3, starting transfers between devices, per_device(): lax.ppermute(thinned, 'tm', [(tm_index(*p), tm_index(p[0], p[1] + d, p[2]...  4.81 us
  transfers between devices with their start and end apart: 20, of which 4 were waited for; matrix products, arithmetic and copies ran while one was open for 14% of the time, Pallas kernels for 29%

profile of v1, /device:TPU:97, one launch (start us, length us, event | category | flops | bytes accessed | tf_op | source)
XLA Modules:
  0.0 226.4 jit_solution(10885161658619256503)
XLA Ops:
  6.5 1.5 slice.11
  8.1 1.4 slice.10
  11.5 2.5 %collective-permute-start.2 = (bf16[384,384]{1,0:T(8,128)(2,1)}, bf16[384,384]{1,0:T(8,128)(2,1)}, u32[]{:S(2)}, u32[]{:S(2)}) collective-permute-start(bf16[384,384]{1,0:T(8,128)(2,1)} %bitcast.26.refs_0_), channel_id=1, source_target_pairs={{0,16},{4,20},{8,24},{12,28},{16,0},{20,4},{24,8},{28,12},{32,48},... | collective-permute-start | bytes 884744 | tf_op jit(solution)/shard_map/ppermute | solution.py:341
  16.1 2.8 %dynamic-slice_bitcast_fusion.2 = (bf16[1,1536,384]{2,1,0:T(8,128)(2,1)S(1)}, bf16[1,1536,384]{2,1,0:T(8,128)(2,1)S(1)}, bf16[1,1536,384]{2,1,0:T(8,128)(2,1)S(1)}, bf16[1,1536,384]{2,1,0:T(8,128)(2,1)S(1)}) fusion(bf16[3072,384]{1,0:T(8,128)(2,1)} %v_ref.5, s32[]{:T(128)S(6)} %select_n.259, s32[]{:T(128)S(6)} %select_n.260, bf16[3072,384]{1,0:T(8,128)(2,1)} %k_ref.5), kind=kLoop, calls=%fused_computation.5 | loop fusion | bytes 9437192 | tf_op jit(solution)/shard_map/stack | solution.py:333
  18.9 1.7 pad_maximum_fusion
  20.6 1.5 collective-permute-start
  22.1 1.7 copy.34
  23.8 1.8 reshape.529
  25.6 1.9 reshape_reshape.3
  27.5 1.3 constant_dynamic-slice_fusion.4
  30.9 1.4 compare_reduce_fusion
  32.9 1.7 reduce_window_sum.23
  37.2 1.4 reshape.531.picks
  40.2 1.7 pad_maximum_fusion.1
  41.9 3.7 %shard_map.74 = (bf16[384,384]{1,0:T(8,128)(2,1)}, bf16[384,384]{1,0:T(8,128)(2,1)}, bf16[384,384]{1,0:T(8,128)(2,1)}, bf16[384,384]{1,0:T(8,128)(2,1)}, bf16[38...) custom-call(s32[192]{0:T(256)} %reshape.531.picks, ...), custom_call_target="tpu_custom_call" | custom-call | tf_op jit(solution)/shard_map/pallas_call | solution.py:274
  45.6 2.1 collective-permute-start.11
  52.8 2.7 %collective-permute-start.7 = (bf16[384,384]{1,0:T(8,128)(2,1)S(1)}, bf16[384,384]{1,0:T(8,128)(2,1)S(1)}, u32[]{:S(2)}, u32[]{:S(2)}) collective-permute-start(bf16[384,384]{1,0:T(8,128)(2,1)S(1)} %copy-done.14), channel_id=1, source_target_pairs={{0,64},{4,68},{8,72},{12,76},{16,80},{20,84},{24,88},{28,92},{32,9... | collective-permute-start | bytes 884744 | tf_op jit(solution)/shard_map/ppermute | solution.py:397
  55.5 26.3 %collective-permute-done.5.rest_2_ = bf16[384,384]{1,0:T(8,128)(2,1)S(1)} collective-permute-done((bf16[384,384]{1,0:T(8,128)(2,1)}, bf16[384,384]{1,0:T(8,128)(2,1)S(1)}, u32[]{:S(2)}, u32[]{:S(2)}) %collective-permute-start.5) | collective-permute-done | bytes 294944 | tf_op jit(solution)/shard_map/ppermute | solution.py:397
  81.8 2.3 %collective-permute-start.8 = (bf16[384,384]{1,0:T(8,128)(2,1)S(1)}, bf16[384,384]{1,0:T(8,128)(2,1)S(1)}, u32[]{:S(2)}, u32[]{:S(2)}) collective-permute-start(bf16[384,384]{1,0:T(8,128)(2,1)S(1)} %copy-done.13), channel_id=1, source_target_pairs={{0,68},{4,64},{8,76},{12,72},{16,84},{20,80},{24,92},{28,88},{32,1... | collective-permute-start | bytes 884744 | tf_op jit(solution)/shard_map/ppermute | solution.py:397
  84.1 5.8 %collective-permute-done.6.rest_3_ = bf16[384,384]{1,0:T(8,128)(2,1)S(1)} collective-permute-done((bf16[384,384]{1,0:T(8,128)(2,1)}, bf16[384,384]{1,0:T(8,128)(2,1)S(1)}, u32[]{:S(2)}, u32[]{:S(2)}) %collective-permute-start.6) | collective-permute-done | bytes 294944 | tf_op jit(solution)/shard_map/ppermute | solution.py:397
  89.9 11.6 %collective-permute-start.9 = (bf16[384,384]{1,0:T(8,128)(2,1)S(1)}, bf16[384,384]{1,0:T(8,128)(2,1)S(1)}, u32[]{:S(2)}, u32[]{:S(2)}) collective-permute-start(bf16[384,384]{1,0:T(8,128)(2,1)S(1)} %copy-done.12), channel_id=1, source_target_pairs={{0,96},{4,100},{8,104},{12,108},{16,112},{20,116},{24,120},{28,124... | collective-permute-start | bytes 884744 | tf_op jit(solution)/shard_map/ppermute | solution.py:397
  101.7 18.9 %shard_map.73 = (f32[1536,384]{1,0:T(8,128)}, f32[1536,128]{1,0:T(8,128)}) custom-call(s32[1]{0:T(128)} %bitcast.4.scalars, s32[384]{0:T(512)} %reshape.530.near, s32[384]{0:T(512)} %select_reduce_fusion.slots, s32[384]{0:T(512)} %select_reduce_fusion.2.strides, bf16[3072,384]{1,0:T(8,128)(2,1)} %q_ref.7, bf16[3072,384]{1,0:T(8,128)(2,1)} %k_ref.5, ...), custom_call_target="tpu_custom_call" | custom-call | flops 15401484288 | bytes 8388608 | tf_op jit(solution)/shard_map/pallas_call | solution.py:171
  121.8 17.0 %shard_map.75 = bf16[1536,384]{1,0:T(8,128)(2,1)} custom-call(s32[1]{0:T(128)} %bitcast.4.scalars, s32[384]{0:T(512)} %select_reduce_fusion.slots, s32[384]{0:T(512)} %select_reduce_fusion.2.strides, bf16[3072,384]{1,0:T(8,128)(2,1)} %q_ref.7, f32[1536,384]{1,0:T(8,128)} %get-tuple-element.24.acc_ref, f32[1536,128]{1,0:T(8,128)} %get-tuple-element.25.stat_ref, ...), custom_call_target="tpu_custom_call" | custom-call | flops 1811939328 | bytes 8388608 | tf_op jit(solution)/shard_map/pallas_call | solution.py:230
  138.8 13.5 %shard_map.76 = bf16[768,384]{1,0:T(8,128)(2,1)} custom-call(s32[1]{0:T(128)} %bitcast.27.scalars, s32[384]{0:T(512)} %reshape.530.near, s32[384]{0:T(512)} %select_reduce_fusion.slots, s32[384]{0:T(512)} %select_reduce_fusion.2.strides, bf16[3072,384]{1,0:T(8,128)(2,1)} %q_ref.7, bf16[3072,384]{1,0:T(8,128)(2,1)} %k_ref.5, bf16[3072,384]{1,0:T(8,128)(2,1)} %v_ref.5, ...), custom_call_target="tpu_custom_call" | custom-call | flops 7700742144 | bytes 8388608 | tf_op jit(solution)/shard_map/pallas_call | solution.py:171
  153.4 3.5 %collective-permute-start.12 = (bf16[768,384]{1,0:T(8,128)(2,1)S(1)}, bf16[768,384]{1,0:T(8,128)(2,1)S(1)}, u32[]{:S(2)}, u32[]{:S(2)}) collective-permute-start(bf16[768,384]{1,0:T(8,128)(2,1)S(1)} %get-tuple-element.49), channel_id=1, source_target_pairs={{2,3},{3,2},{10,11},{11,10},{18,19},{19,18},{26,27},{27,26},{34,35... | collective-permute-start | bytes 1769480 | tf_op jit(solution)/shard_map/ppermute | solution.py:439
  156.9 13.6 %shard_map.77 = bf16[768,384]{1,0:T(8,128)(2,1)} custom-call(s32[1]{0:T(128)} %bitcast.28.scalars, s32[384]{0:T(512)} %reshape.530.near, s32[384]{0:T(512)} %select_reduce_fusion.slots, s32[384]{0:T(512)} %select_reduce_fusion.2.strides, bf16[3072,384]{1,0:T(8,128)(2,1)} %q_ref.7, bf16[3072,384]{1,0:T(8,128)(2,1)} %k_ref.5, bf16[3072,384]{1,0:T(8,128)(2,1)} %v_ref.5, ...), custom_call_target="tpu_custom_call" | custom-call | flops 7700742144 | bytes 8388608 | tf_op jit(solution)/shard_map/pallas_call | solution.py:171
  171.2 1.3 collective-permute-start.14
  172.5 5.6 %collective-permute-start.15 = (bf16[768,384]{1,0:T(8,128)(2,1)}, bf16[768,384]{1,0:T(8,128)(2,1)S(1)}, u32[]{:S(2)}, u32[]{:S(2)}) collective-permute-start(bf16[768,384]{1,0:T(8,128)(2,1)} %shard_map.77), channel_id=1, source_target_pairs={{2,0},{3,1},{10,8},{11,9},{18,16},{19,17},{26,24},{27,25},{34,32},... | collective-permute-start | bytes 1769480 | tf_op jit(solution)/shard_map/ppermute | solution.py:439
  178.2 1.3 collective-permute-start.17
  182.4 12.0 %collective-permute-done.14 = bf16[768,384]{1,0:T(8,128)(2,1)S(1)} collective-permute-done((bf16[768,384]{1,0:T(8,128)(2,1)S(1)}, bf16[768,384]{1,0:T(8,128)(2,1)S(1)}, u32[]{:S(2)}, u32[]{:S(2)}) %collective-permute-start.14) | collective-permute-done | bytes 589856 | tf_op jit(solution)/shard_map/ppermute | solution.py:439
  195.3 12.5 %collective-permute-done.16 = bf16[768,384]{1,0:T(8,128)(2,1)S(1)} collective-permute-done((bf16[768,384]{1,0:T(8,128)(2,1)S(1)}, bf16[768,384]{1,0:T(8,128)(2,1)S(1)}, u32[]{:S(2)}, u32[]{:S(2)}) %collective-permute-start.16) | collective-permute-done | bytes 589856 | tf_op jit(solution)/shard_map/ppermute | solution.py:439
  208.7 10.8 %shard_map.78 = bf16[768,1536]{1,0:T(8,128)(2,1)} custom-call(s32[4]{0:T(128)} %pad_add_fusion.scalars, bf16[768,384]{1,0:T(8,128)(2,1)} %get-tuple-element.50.a0, bf16[768,384]{1,0:T(8,128)(2,1)} %broadcast_select_fusion.2.a1, bf16[768,384]{1,0:T(8,128)(2,1)} %broadcast_select_fusion.1.a2, bf16[768,384]{1,0:T(8,128)(2,1)} %broadcast_select_fusion.a3, ...), custom_call_target="tpu_custom_call" | custom-call | flops 3623878656 | bytes 10485760 | tf_op jit(solution)/shard_map/pallas_call | solution.py:301
  (91 shorter events, 23.8 us)
Async XLA Ops:
  6.5 8.6 %copy-start = (bf16[384,1536]{1,0:T(8,128)(2,1)S(1)}, bf16[384,1536]{1,0:T(8,128)(2,1)}, u32[]{:S(2)}) copy-start(bf16[384,1536]{1,0:T(8,128)(2,1)} %param.10) | copy-start | bytes 3538948
  6.5 45.3 %all-gather.5.cloned.1.call-start = ((), (), s32[]{:S(2)}) async-start(), calls=%async_computation | async-start | bytes 2949120 | tf_op jit(solution)/shard_map/all_gather | solution.py:350
  10.3 31.6 %collective-permute-start.1 = (bf16[384,384]{1,0:T(8,128)(2,1)}, bf16[384,384]{1,0:T(8,128)(2,1)}, u32[]{:S(2)}, u32[]{:S(2)}) collective-permute-start(bf16[384,384]{1,0:T(8,128)(2,1)} %bitcast.26.refs_0_), channel_id=1, source_target_pairs={{0,8},{4,12},{8,16},{12,20},{16,24},{20,28},{24,0},{28,4},{32,40},... | collective-permute-start | bytes 884744 | tf_op jit(solution)/shard_map/ppermute | solution.py:341
  11.5 30.4 %collective-permute-start.2 = (bf16[384,384]{1,0:T(8,128)(2,1)}, bf16[384,384]{1,0:T(8,128)(2,1)}, u32[]{:S(2)}, u32[]{:S(2)}) collective-permute-start(bf16[384,384]{1,0:T(8,128)(2,1)} %bitcast.26.refs_0_), channel_id=1, source_target_pairs={{0,16},{4,20},{8,24},{12,28},{16,0},{20,4},{24,8},{28,12},{32,48},... | collective-permute-start | bytes 884744 | tf_op jit(solution)/shard_map/ppermute | solution.py:341
  14.0 27.9 %collective-permute-start.3 = (bf16[384,384]{1,0:T(8,128)(2,1)}, bf16[384,384]{1,0:T(8,128)(2,1)}, u32[]{:S(2)}, u32[]{:S(2)}) collective-permute-start(bf16[384,384]{1,0:T(8,128)(2,1)} %bitcast.26.refs_0_), channel_id=1, source_target_pairs={{0,24},{4,28},{8,0},{12,4},{16,8},{20,12},{24,16},{28,20},{32,56},... | collective-permute-start | bytes 884744 | tf_op jit(solution)/shard_map/ppermute | solution.py:341
  16.0 192.7 %all-gather.7.cloned.1.call-start = ((), (), s32[]{:S(2)}) async-start(), calls=%async_computation.1 | async-start | bytes 7077888 | tf_op jit(solution)/shard_map/all_gather | solution.py:351
  20.6 80.9 %collective-permute-start = (bf16[2,1536,384]{2,1,0:T(8,128)(2,1)}, bf16[2,1536,384]{2,1,0:T(8,128)(2,1)}, u32[]{:S(2)}, u32[]{:S(2)}) collective-permute-start(bf16[2,1536,384]{2,1,0:T(8,128)(2,1)} %pad_maximum_fusion), channel_id=1, source_target_pairs={{0,4},{4,0},{8,12},{12,8},{16,20},{20,16},{24,28},{28,24},{32,36},... | collective-permute-start | bytes 7077896 | tf_op jit(solution)/shard_map/ppermute | solution.py:346
  41.9 8.3 %copy-start.10 = (s32[64]{0:T(128)S(1)}, s32[64]{0:T(128)}, u32[]{:S(2)}) copy-start(s32[64]{0:T(128)} %param.13) | copy-start | bytes 772
  45.6 93.2 %collective-permute-start.11 = (bf16[2,1536,384]{2,1,0:T(8,128)(2,1)}, bf16[2,1536,384]{2,1,0:T(8,128)(2,1)}, u32[]{:S(2)}, u32[]{:S(2)}) collective-permute-start(bf16[2,1536,384]{2,1,0:T(8,128)(2,1)} %pad_maximum_fusion.1), channel_id=1, source_target_pairs={{4,8},{12,16},{20,24},{28,32},{36,40},{44,48},{52,56},{60,64},{68,... | collective-permute-start | bytes 7077896 | tf_op jit(solution)/shard_map/ppermute | solution.py:398
  48.0 3.8 %collective-permute-start.4 = (bf16[384,384]{1,0:T(8,128)(2,1)}, bf16[384,384]{1,0:T(8,128)(2,1)S(1)}, u32[]{:S(2)}, u32[]{:S(2)}) collective-permute-start(bf16[384,384]{1,0:T(8,128)(2,1)} %get-tuple-element.35), channel_id=1, source_target_pairs={{0,4},{4,0},{8,12},{12,8},{16,20},{20,16},{24,28},{28,24},{32,36},... | collective-permute-start | bytes 884744 | tf_op jit(solution)/shard_map/ppermute | solution.py:397
  48.1 33.7 %collective-permute-start.5 = (bf16[384,384]{1,0:T(8,128)(2,1)}, bf16[384,384]{1,0:T(8,128)(2,1)S(1)}, u32[]{:S(2)}, u32[]{:S(2)}) collective-permute-start(bf16[384,384]{1,0:T(8,128)(2,1)} %get-tuple-element.36), channel_id=1, source_target_pairs={{0,32},{4,36},{8,40},{12,44},{16,48},{20,52},{24,56},{28,60},{32,6... | collective-permute-start | bytes 884744 | tf_op jit(solution)/shard_map/ppermute | solution.py:397
  48.2 41.7 %collective-permute-start.6 = (bf16[384,384]{1,0:T(8,128)(2,1)}, bf16[384,384]{1,0:T(8,128)(2,1)S(1)}, u32[]{:S(2)}, u32[]{:S(2)}) collective-permute-start(bf16[384,384]{1,0:T(8,128)(2,1)} %get-tuple-element.37), channel_id=1, source_target_pairs={{0,36},{4,32},{8,44},{12,40},{16,52},{20,48},{24,60},{28,56},{32,6... | collective-permute-start | bytes 884744 | tf_op jit(solution)/shard_map/ppermute | solution.py:397
  51.8 1.0 copy-start.14
  51.8 30.0 %copy-start.13 = (bf16[384,384]{1,0:T(8,128)(2,1)S(1)}, bf16[384,384]{1,0:T(8,128)(2,1)}, u32[]{:S(2)}) copy-start(bf16[384,384]{1,0:T(8,128)(2,1)} %get-tuple-element.39) | copy-start | bytes 884740
  51.8 38.1 %copy-start.12 = (bf16[384,384]{1,0:T(8,128)(2,1)S(1)}, bf16[384,384]{1,0:T(8,128)(2,1)}, u32[]{:S(2)}) copy-start(bf16[384,384]{1,0:T(8,128)(2,1)} %get-tuple-element.40) | copy-start | bytes 884740
  51.8 49.7 %copy-start.11 = (bf16[384,384]{1,0:T(8,128)(2,1)S(1)}, bf16[384,384]{1,0:T(8,128)(2,1)}, u32[]{:S(2)}) copy-start(bf16[384,384]{1,0:T(8,128)(2,1)} %get-tuple-element.41) | copy-start | bytes 884740
  52.8 67.9 %copy-start.3 = (bf16[384,384]{1,0:T(8,128)(2,1)}, bf16[384,384]{1,0:T(8,128)(2,1)S(1)}, u32[]{:S(2)}) copy-start(bf16[384,384]{1,0:T(8,128)(2,1)S(1)} %collective-permute-done.4.rest_1_) | copy-start | bytes 884740
  52.8 67.9 %collective-permute-start.7 = (bf16[384,384]{1,0:T(8,128)(2,1)S(1)}, bf16[384,384]{1,0:T(8,128)(2,1)S(1)}, u32[]{:S(2)}, u32[]{:S(2)}) collective-permute-start(bf16[384,384]{1,0:T(8,128)(2,1)S(1)} %copy-done.14), channel_id=1, source_target_pairs={{0,64},{4,68},{8,72},{12,76},{16,80},{20,84},{24,88},{28,92},{32,9... | collective-permute-start | bytes 884744 | tf_op jit(solution)/shard_map/ppermute | solution.py:397
  81.8 38.8 %copy-start.4 = (bf16[384,384]{1,0:T(8,128)(2,1)}, bf16[384,384]{1,0:T(8,128)(2,1)S(1)}, u32[]{:S(2)}) copy-start(bf16[384,384]{1,0:T(8,128)(2,1)S(1)} %collective-permute-done.5.rest_2_) | copy-start | bytes 884740
  81.8 38.9 %collective-permute-start.8 = (bf16[384,384]{1,0:T(8,128)(2,1)S(1)}, bf16[384,384]{1,0:T(8,128)(2,1)S(1)}, u32[]{:S(2)}, u32[]{:S(2)}) collective-permute-start(bf16[384,384]{1,0:T(8,128)(2,1)S(1)} %copy-done.13), channel_id=1, source_target_pairs={{0,68},{4,64},{8,76},{12,72},{16,84},{20,80},{24,92},{28,88},{32,1... | collective-permute-start | bytes 884744 | tf_op jit(solution)/shard_map/ppermute | solution.py:397
  89.9 30.8 %copy-start.5 = (bf16[384,384]{1,0:T(8,128)(2,1)}, bf16[384,384]{1,0:T(8,128)(2,1)S(1)}, u32[]{:S(2)}) copy-start(bf16[384,384]{1,0:T(8,128)(2,1)S(1)} %collective-permute-done.6.rest_3_) | copy-start | bytes 884740
  89.9 30.8 %collective-permute-start.9 = (bf16[384,384]{1,0:T(8,128)(2,1)S(1)}, bf16[384,384]{1,0:T(8,128)(2,1)S(1)}, u32[]{:S(2)}, u32[]{:S(2)}) collective-permute-start(bf16[384,384]{1,0:T(8,128)(2,1)S(1)} %copy-done.12), channel_id=1, source_target_pairs={{0,96},{4,100},{8,104},{12,108},{16,112},{20,116},{24,120},{28,124... | collective-permute-start | bytes 884744 | tf_op jit(solution)/shard_map/ppermute | solution.py:397
  101.5 19.3 %collective-permute-start.10 = (bf16[384,384]{1,0:T(8,128)(2,1)S(1)}, bf16[384,384]{1,0:T(8,128)(2,1)S(1)}, u32[]{:S(2)}, u32[]{:S(2)}) collective-permute-start(bf16[384,384]{1,0:T(8,128)(2,1)S(1)} %copy-done.11), channel_id=1, source_target_pairs={{0,100},{4,96},{8,108},{12,104},{16,116},{20,112},{24,124},{28,120... | collective-permute-start | bytes 884744 | tf_op jit(solution)/shard_map/ppermute | solution.py:397
  120.7 1.0 copy-start.9
  138.8 13.6 %copy-start.1 = (bf16[1536,384]{1,0:T(8,128)(2,1)S(1)}, bf16[1536,384]{1,0:T(8,128)(2,1)}, u32[]{:S(2)}) copy-start(bf16[1536,384]{1,0:T(8,128)(2,1)} %shard_map.75) | copy-start | bytes 3538948
  153.4 26.1 %collective-permute-start.12 = (bf16[768,384]{1,0:T(8,128)(2,1)S(1)}, bf16[768,384]{1,0:T(8,128)(2,1)S(1)}, u32[]{:S(2)}, u32[]{:S(2)}) collective-permute-start(bf16[768,384]{1,0:T(8,128)(2,1)S(1)} %get-tuple-element.49), channel_id=1, source_target_pairs={{2,3},{3,2},{10,11},{11,10},{18,19},{19,18},{26,27},{27,26},{34,35... | collective-permute-start | bytes 1769480 | tf_op jit(solution)/shard_map/ppermute | solution.py:439
  156.9 21.3 %copy-start.2 = (bf16[768,384]{1,0:T(8,128)(2,1)S(1)}, bf16[768,384]{1,0:T(8,128)(2,1)}, u32[]{:S(2)}) copy-start(bf16[768,384]{1,0:T(8,128)(2,1)} %shard_map.76) | copy-start | bytes 1769476
  170.5 10.9 %collective-permute-start.13 = (bf16[768,384]{1,0:T(8,128)(2,1)}, bf16[768,384]{1,0:T(8,128)(2,1)S(1)}, u32[]{:S(2)}, u32[]{:S(2)}) collective-permute-start(bf16[768,384]{1,0:T(8,128)(2,1)} %shard_map.77), channel_id=1, source_target_pairs={{0,1},{1,0},{8,9},{9,8},{16,17},{17,16},{24,25},{25,24},{32,33},{3... | collective-permute-start | bytes 1769480 | tf_op jit(solution)/shard_map/ppermute | solution.py:439
  171.2 23.1 %collective-permute-start.14 = (bf16[768,384]{1,0:T(8,128)(2,1)S(1)}, bf16[768,384]{1,0:T(8,128)(2,1)S(1)}, u32[]{:S(2)}, u32[]{:S(2)}) collective-permute-start(bf16[768,384]{1,0:T(8,128)(2,1)S(1)} %get-tuple-element.48), channel_id=1, source_target_pairs={{0,2},{1,3},{8,10},{9,11},{16,18},{17,19},{24,26},{25,27},{32,34},... | collective-permute-start | bytes 1769480 | tf_op jit(solution)/shard_map/ppermute | solution.py:439
  172.5 21.8 %collective-permute-start.15 = (bf16[768,384]{1,0:T(8,128)(2,1)}, bf16[768,384]{1,0:T(8,128)(2,1)S(1)}, u32[]{:S(2)}, u32[]{:S(2)}) collective-permute-start(bf16[768,384]{1,0:T(8,128)(2,1)} %shard_map.77), channel_id=1, source_target_pairs={{2,0},{3,1},{10,8},{11,9},{18,16},{19,17},{26,24},{27,25},{34,32},... | collective-permute-start | bytes 1769480 | tf_op jit(solution)/shard_map/ppermute | solution.py:439
  178.2 29.6 %collective-permute-start.17 = (bf16[768,384]{1,0:T(8,128)(2,1)S(1)}, bf16[768,384]{1,0:T(8,128)(2,1)S(1)}, u32[]{:S(2)}, u32[]{:S(2)}) collective-permute-start(bf16[768,384]{1,0:T(8,128)(2,1)S(1)} %copy-done.2), channel_id=1, source_target_pairs={{2,1},{3,0},{10,9},{11,8},{18,17},{19,16},{26,25},{27,24},{34,33},... | collective-permute-start | bytes 1769480 | tf_op jit(solution)/shard_map/ppermute | solution.py:439
  179.5 28.3 %collective-permute-start.16 = (bf16[768,384]{1,0:T(8,128)(2,1)S(1)}, bf16[768,384]{1,0:T(8,128)(2,1)S(1)}, u32[]{:S(2)}, u32[]{:S(2)}) collective-permute-start(bf16[768,384]{1,0:T(8,128)(2,1)S(1)} %get-tuple-element.47), channel_id=1, source_target_pairs={{0,3},{1,2},{8,11},{9,10},{16,19},{17,18},{24,27},{25,26},{32,35},... | collective-permute-start | bytes 1769480 | tf_op jit(solution)/shard_map/ppermute | solution.py:439
  (3 other events, 2.5 us)
Sparse Core Ops, SparseCore 0:
  16.1 32.7 all-gather.4
  52.0 19.4 all-gather.6

commit v2 on v0

v2 whole, which is shorter than its diff:
```python
import functools
import math

import jax
import jax.numpy as jnp
from jax import lax
from jax.experimental import pallas as pl
from jax.experimental.pallas import tpu as pltpu
from jax.sharding import PartitionSpec as P

HD = 128
BLK = 128
FRAME_BLK = 12
KNEAR = 16
KFAR = 16
CAP = 6
MINSTRIDE = 16
THIN = BLK // MINSTRIDE
HEADS = 3
WIDTH = HEADS * HD
BLOCKS = 24
NX, NZ, NC = 4, 4, 2
NTM = NX * NZ * NC
NHEAD = 4
CHUNK = BLOCKS // NHEAD
FAR_ROWS = NTM * CAP * 2 * THIN
FRAME = FRAME_BLK * BLK
LOG2_SCALE = math.log2(math.e) / math.sqrt(HD)
NT = (((1,), (1,)), ((), ()))
VMEM_LIMIT = 56 * 2**20
UNROLL = 3
SLOT, STRIDE, ORDER = KNEAR, KNEAR + KFAR, BLOCKS
FAST_FIRST, FAST_LAST, SLOW_FIRST, SLOW_LAST = range(4)
IN_HBM = pl.BlockSpec(memory_space=pltpu.HBM)


def tm_index(z, x, c):
    return (z % NZ) * NX * NC + (x % NX) * NC + c


def load_far(far_refs, far_vm, sems, first_sem):
    part = NX * CAP * 2 * THIN
    copies = []
    for n, ref in enumerate(far_refs):
        rows = part if n < NZ else NZ * part
        copies.append(
            pltpu.make_async_copy(
                ref.at[pl.ds(0, rows)], far_vm.at[pl.ds(n * part, rows)], sems.at[first_sem + n]
            )
        )
    return copies


def far_block(far_vm, table, block):
    tiles = [
        far_vm[
            pl.ds(pl.multiple_of(table[block, SLOT + j] * 2 * THIN, 2 * THIN), 2 * THIN), :
        ].astype(jnp.float32)
        for j in range(KFAR)
    ]
    keys = jnp.concatenate([t[:THIN] for t in tiles], axis=0).astype(jnp.bfloat16)
    values = jnp.concatenate([t[THIN:] for t in tiles], axis=0).astype(jnp.bfloat16)
    lane = lax.broadcasted_iota(jnp.int32, (1, BLK), 1)
    stride = jnp.zeros((1, BLK), jnp.int32)
    for j in range(KFAR):
        stride = jnp.where(lane // THIN == j, table[block, STRIDE + j], stride)
    used = (((lane % THIN) * MINSTRIDE) & (stride - 1)) == 0
    return keys, values, used


def with_ones(values):
    return jnp.concatenate([values, jnp.ones((values.shape[0], HD), jnp.bfloat16)], axis=1)


def attend_kernel(table, q_ref, k_ref, v_ref, halo_ref, *rest, chunk, with_far):
    if with_far:
        far_refs, (out_ref, k_vm, v_vm, s_vm, far_vm, sems) = rest[:5], rest[5:]
    else:
        near_ref, level_ref, k_vm, v_vm, s_vm, sems = rest
    step = pl.program_id(0)
    own = BLOCKS * BLK
    halo = pl.ds(own, FRAME)
    key_copies = [
        pltpu.make_async_copy(k_ref, k_vm.at[pl.ds(0, own)], sems.at[0]),
        pltpu.make_async_copy(halo_ref.at[pl.ds(0, FRAME)], k_vm.at[halo], sems.at[1]),
    ]
    value_copies = [
        pltpu.make_async_copy(v_ref, v_vm.at[pl.ds(0, own)], sems.at[2]),
        pltpu.make_async_copy(halo_ref.at[pl.ds(FRAME, FRAME)], v_vm.at[halo], sems.at[3]),
    ]
    if with_far:
        key_copies += load_far(far_refs, far_vm, sems, 4)

    @pl.when(step == 0)
    def _():
        for copy in key_copies + value_copies:
            copy.start()
        for copy in key_copies:
            copy.wait()

    first = table[ORDER, chunk + step] * CHUNK

    def prepare(unit):
        block = first + unit
        offsets = [pl.multiple_of(table[block, j] * BLK, BLK) for j in range(KNEAR)]
        far = far_block(far_vm, table, block) if with_far else None
        return offsets, far, pl.ds(pl.multiple_of(unit * BLK, BLK), BLK)

    count = KNEAR + (1 if with_far else 0)

    def score_pair(prepared, head, j):
        offsets, far, rows = prepared
        cols = slice(head * HD, head * HD + HD)
        query = q_ref[rows, cols]
        if j < KNEAR:
            keys = jnp.concatenate([k_vm[pl.ds(o, BLK), cols] for o in offsets[j : j + 2]], axis=0)
            both = lax.dot_general(query, keys, NT, preferred_element_type=jnp.float32)
            return [both[:, :BLK], both[:, BLK:]]
        last = lax.dot_general(query, far[0][:, cols], NT, preferred_element_type=jnp.float32)
        return [jnp.where(far[2], last, -1e30)]

    def peak_of(scores):
        top = functools.reduce(jnp.maximum, scores)
        return jnp.max(top, axis=1, keepdims=True) * LOG2_SCALE

    def add_pair(acc, prepared, head, scores, peak, j):
        offsets, far, _ = prepared
        cols = slice(head * HD, head * HD + HD)
        some = range(j, min(j + 2, count))
        weights = jnp.concatenate(
            [jnp.exp2(scores[i] * LOG2_SCALE - peak).astype(jnp.bfloat16) for i in some], axis=1
        )
        values = jnp.concatenate(
            [v_vm[pl.ds(offsets[i], BLK), cols] if i < KNEAR else far[1][:, cols] for i in some],
            axis=0,
        )
        part = jnp.dot(weights, with_ones(values), preferred_element_type=jnp.float32)
        return part if acc is None else acc + part

    def store(prepared, head, peak, acc):
        rows = prepared[2]
        cols = slice(head * HD, head * HD + HD)
        if with_far:
            out_ref[rows, cols] = (acc[:, :HD] / acc[:, HD:]).astype(jnp.bfloat16)
        else:
            near_ref[rows, cols] = (acc[:, :HD] / acc[:, HD:]).astype(jnp.bfloat16)
            level_ref[rows, cols] = peak + jnp.log2(acc[:, HD:])

    def scores_of(prepared, head):
        scores = []
        for j in range(0, count, 2):
            scores += score_pair(prepared, head, j)
        return scores

    def overlap(fresh, pending):
        prepared, head, scores = pending
        peak = peak_of(scores)
        following, acc = [], None
        for j in range(0, count, 2):
            following += score_pair(*fresh, j)
            acc = add_pair(acc, prepared, head, scores, peak, j)
        store(prepared, head, peak, acc)
        return following

    def hold(scores):
        for i, some in enumerate(scores):
            s_vm[:, i * BLK : i * BLK + BLK] = some

    hold(scores_of(prepare(0), 0))

    @pl.when(step == 0)
    def _():
        for copy in value_copies:
            copy.wait()

    units = CHUNK // UNROLL

    def body(i, _):
        pending = None
        scores = [s_vm[:, n * BLK : n * BLK + BLK] for n in range(count)]
        for u in range(UNROLL):
            unit = i * UNROLL + u
            prepared = prepare(unit)
            for head in range(HEADS):
                if head or u:
                    scores = overlap((prepared, head), pending)
                pending = prepared, head, scores
        after = prepare(jnp.minimum(i * UNROLL + UNROLL, CHUNK - 1))
        hold(overlap((after, 0), pending))
        return 0

    lax.fori_loop(0, units, body, 0)


def attend(table, query, keys, values, halo, far, chunk, chunks):
    with_far = far is not None
    spot = lambda i, s: (s[ORDER, chunk + i], 0)
    same = lambda i, s: (i, 0)
    rows = CHUNK * BLK
    scratch = [pltpu.VMEM((BLOCKS * BLK + FRAME, WIDTH), jnp.bfloat16) for _ in range(2)]
    scratch.append(pltpu.VMEM((BLK, (KNEAR + 1) * BLK), jnp.float32))
    if with_far:
        scratch.append(pltpu.VMEM((FAR_ROWS, WIDTH), jnp.bfloat16))
        out_shape = jax.ShapeDtypeStruct((chunks * rows, WIDTH), jnp.bfloat16)
        out_specs = pl.BlockSpec((rows, WIDTH), same)
    else:
        out_shape = [
            jax.ShapeDtypeStruct((chunks * rows, WIDTH), kind)
            for kind in (jnp.bfloat16, jnp.float32)
        ]
        out_specs = [pl.BlockSpec((rows, WIDTH), same)] * 2
    scratch.append(pltpu.SemaphoreType.DMA((9,)))
    extra = tuple(far) if with_far else ()
    return pl.pallas_call(
        functools.partial(attend_kernel, chunk=chunk, with_far=with_far),
        grid_spec=pltpu.PrefetchScalarGridSpec(
            num_scalar_prefetch=1,
            grid=(chunks,),
            in_specs=[pl.BlockSpec((rows, WIDTH), spot)] + [IN_HBM] * (3 + len(extra)),
            out_specs=out_specs,
            scratch_shapes=scratch,
        ),
        out_shape=out_shape,
        compiler_params=pltpu.CompilerParams(vmem_limit_bytes=VMEM_LIMIT),
        cost_estimate=pl.CostEstimate(
            flops=chunks * CHUNK * HEADS * 17 * 4 * BLK * BLK * HD * 3,
            bytes_accessed=8 * 2**20,
            transcendentals=0,
        ),
    )(table, query, keys, values, halo, *extra)


def merge_kernel(table, q_ref, near_ref, level_ref, *rest, chunk):
    far_refs, (_, first_ref, last_ref, out_vm, far_vm, sems) = rest[:5], rest[5:]
    step = pl.program_id(0)

    @pl.when(step == 0)
    def _():
        copies = load_far(far_refs, far_vm, sems, 0)
        for copy in copies:
            copy.start()
        for copy in copies:
            copy.wait()

    first = table[ORDER, chunk + step] * CHUNK
    spot = {
        (unit, head): (
            slice(unit * BLK, unit * BLK + BLK),
            slice(head * HD, head * HD + HD),
        )
        for unit in range(CHUNK)
        for head in range(HEADS)
    }
    far = [far_block(far_vm, table, first + unit) for unit in range(CHUNK)]
    scores, peaks, sums = {}, {}, {}
    for p, (rows, cols) in spot.items():
        keys, _, used = far[p[0]]
        some = lax.dot_general(
            q_ref[rows, cols], keys[:, cols], NT, preferred_element_type=jnp.float32
        )
        scores[p] = jnp.where(used, some, -1e30) * LOG2_SCALE
    for p, (rows, cols) in spot.items():
        peaks[p] = jnp.maximum(jnp.max(scores[p], axis=1, keepdims=True), level_ref[rows, cols])
    for p, (rows, cols) in spot.items():
        weights = jnp.exp2(scores[p] - peaks[p]).astype(jnp.bfloat16)
        values = far[p[0]][1][:, cols]
        sums[p] = jnp.dot(weights, with_ones(values), preferred_element_type=jnp.float32)
    for p, (rows, cols) in spot.items():
        share = jnp.exp2(level_ref[rows, cols] - peaks[p])
        total = share + sums[p][:, HD:]
        mixed = near_ref[rows, cols].astype(jnp.float32) * share + sums[p][:, :HD]
        out_vm[step, rows, cols] = (mixed / total).astype(jnp.bfloat16)

    outs = [
        pltpu.make_async_copy(out_vm.at[n], ref, sems.at[5 + n])
        for n, ref in enumerate((first_ref, last_ref))
    ]

    @pl.when(step == 0)
    def _():
        outs[0].start()

    @pl.when(step == 1)
    def _():
        outs[1].start()
        for copy in outs:
            copy.wait()


def merge_far(table, query, state, far, chunk, after):
    rows = CHUNK * BLK
    return pl.pallas_call(
        functools.partial(merge_kernel, chunk=chunk),
        grid_spec=pltpu.PrefetchScalarGridSpec(
            num_scalar_prefetch=1,
            grid=(2,),
            in_specs=[pl.BlockSpec((rows, WIDTH), lambda i, s: (s[ORDER, chunk + i], 0))]
            + [pl.BlockSpec((rows, WIDTH), lambda i, s: (i, 0))] * 2
            + [IN_HBM] * 6,
            out_specs=[IN_HBM] * 2,
            scratch_shapes=[
                pltpu.VMEM((2, rows, WIDTH), jnp.bfloat16),
                pltpu.VMEM((FAR_ROWS, WIDTH), jnp.bfloat16),
                pltpu.SemaphoreType.DMA((7,)),
            ],
        ),
        out_shape=[jax.ShapeDtypeStruct((rows, WIDTH), jnp.bfloat16)] * 2,
        compiler_params=pltpu.CompilerParams(vmem_limit_bytes=VMEM_LIMIT),
        cost_estimate=pl.CostEstimate(
            flops=2 * CHUNK * HEADS * 4 * BLK * BLK * HD * 6,
            bytes_accessed=8 * 2**20,
            transcendentals=0,
        ),
    )(table, query, *state, *far, after)


def index_kernel(scalars, steps, far_ref, near_ref, picks_ref, table_ref):
    t = scalars[0]
    core, x, z = t & 1, (t >> 1) & 3, t >> 3
    lane = lax.broadcasted_iota(jnp.int32, (1, BLK), 1)
    group = (lane * 2731) >> 16
    within = lane - group * BLOCKS
    valid = lane < NX * BLOCKS

    source = ((z * NX + ((x - group) & 3)) * NC + core) * BLOCKS + within
    source = jnp.where(valid, source, -1)
    present = []
    for dz in range(NZ):
        for dc in range(NC):
            receiver = (((z + dz) & 3) * NX + x) * NC + (core ^ dc)
            listed = far_ref[pl.ds(pl.multiple_of(receiver * BLOCKS, 8), BLOCKS), :]
            found = jnp.zeros((BLOCKS, BLK), jnp.float32)
            for j in range(KFAR):
                found = jnp.where(listed[:, j : j + 1] == source, 1.0, found)
            present.append(jnp.max(found, axis=0, keepdims=True))

    mine = far_ref[pl.ds(pl.multiple_of(t * BLOCKS, 8), BLOCKS), :]
    ids = [jnp.where(valid, row * NX * BLOCKS + lane, -1) for row in range(NTM // NX)]
    found = [jnp.zeros((BLOCKS, BLK), jnp.float32) for _ in ids]
    for j in range(KFAR):
        column = jnp.broadcast_to(mine[:, j : j + 1], (BLOCKS, BLK))
        found = [jnp.where(column == i, 1.0, f) for i, f in zip(ids, found)]
    present += [jnp.max(f, axis=0, keepdims=True) for f in found]
    present = jnp.concatenate(present, axis=0)

    a = lax.broadcasted_iota(jnp.int32, (BLK, BLK), 0)
    b = lax.broadcasted_iota(jnp.int32, (BLK, BLK), 1)
    group_a, group_b = (a * 2731) >> 16, (b * 2731) >> 16
    before = jnp.where((group_a == group_b) & (a < b), 1.0, 0.0).astype(jnp.bfloat16)
    rank = jnp.dot(present.astype(jnp.bfloat16), before, preferred_element_type=jnp.float32)

    receivers = NZ * NC
    chosen = [
        jnp.where((present[:receivers] > 0) & (rank[:receivers] == k), within.astype(jnp.float32), 0.0)
        for k in range(CAP)
    ]
    gather = jnp.where(group_a == b, 1.0, 0.0).astype(jnp.bfloat16)
    picks = jnp.dot(
        jnp.concatenate(chosen, axis=0).astype(jnp.bfloat16),
        gather,
        preferred_element_type=jnp.float32,
    )
    picks_ref[...] = picks.astype(jnp.int32)

    lies = []
    for row in range(NTM // NX):
        device = row * NX + group
        dz = (z - (device >> 3)) & 3
        dx = (x - (device >> 1)) & 3
        dc = core ^ (device & 1)
        start = ((dc * NZ + dz) * NX + dx) * CAP
        lies.append(start.astype(jnp.float32) + rank[receivers + row : receivers + row + 1])
    entry = lax.broadcasted_iota(jnp.int32, (BLOCKS, KFAR), 1)
    slots = jnp.zeros((BLOCKS, KFAR), jnp.float32)
    for j in range(KFAR):
        column = jnp.broadcast_to(mine[:, j : j + 1], (BLOCKS, BLK))
        at = jnp.zeros((BLOCKS, BLK), jnp.float32)
        for i, where in zip(ids, lies):
            at = jnp.where(column == i, where, at)
        slots = jnp.where(entry == j, jnp.sum(at, axis=1, keepdims=True), slots)

    row = lax.broadcasted_iota(jnp.int32, (BLOCKS, KFAR), 0)
    frame = t * (BLOCKS // FRAME_BLK) + jnp.where(row >= FRAME_BLK, 1, 0)
    distance = jnp.abs(frame - ((mine * 5462) >> 16))
    strides = jnp.zeros((BLOCKS, KFAR), jnp.int32)
    for d in range(steps.shape[0]):
        strides = jnp.where(distance == d, steps[d], strides)

    local = near_ref[...] - t * BLOCKS
    local = jnp.where(local < 0, local + FRAME_BLK + BLOCKS, local)
    rest = jnp.zeros((BLOCKS, BLK - KNEAR - 2 * KFAR), jnp.int32)
    table_ref[:BLOCKS, :] = jnp.concatenate(
        [local, slots.astype(jnp.int32), strides, rest], axis=1
    )

    h = scalars[1]
    order = jnp.zeros((8, BLK), jnp.int32)
    column = lax.broadcasted_iota(jnp.int32, (8, BLK), 1)
    for at, half in ((FAST_FIRST, 1 - core), (SLOW_FIRST, core)):
        inside = (h >> 1) == half
        order = jnp.where(column == at, jnp.where(inside, h ^ 1, h ^ 2), order)
        order = jnp.where(column == at + 1, jnp.where(inside, h, h ^ 3), order)
    table_ref[BLOCKS:, :] = order


def index_work(scalars, steps, far_list, near_list):
    whole = lambda shape: pl.BlockSpec(shape, lambda i, *_: (0, 0))
    shapes = [(NZ * NC * CAP, BLK), (BLOCKS + 8, BLK)]
    return pl.pallas_call(
        index_kernel,
        grid_spec=pltpu.PrefetchScalarGridSpec(
            num_scalar_prefetch=2,
            grid=(1,),
            in_specs=[whole(far_list.shape), whole(near_list.shape)],
            out_specs=[whole(shape) for shape in shapes],
        ),
        out_shape=[jax.ShapeDtypeStruct(shape, jnp.int32) for shape in shapes],
        cost_estimate=pl.CostEstimate(flops=2**20, bytes_accessed=2**22, transcendentals=0),
    )(scalars, steps, far_list, near_list)


def halo_kernel(scalars, k_fast, v_fast, k_slow, v_slow, after, fast_ref, slow_ref):
    fast_ref[0] = k_fast[...]
    fast_ref[1] = v_fast[...]
    slow_ref[0] = k_slow[...]
    slow_ref[1] = v_slow[...]


def pack_halos(scalars, keys, values, after):
    parts = 4
    rows = FRAME // parts
    fast = pl.BlockSpec((rows, WIDTH), lambda i, s: ((1 - (s[0] & 1)) * parts + i, 0))
    slow = pl.BlockSpec((rows, WIDTH), lambda i, s: ((s[0] & 1) * parts + i, 0))
    shape = jax.ShapeDtypeStruct((2, FRAME, WIDTH), jnp.bfloat16)
    outs = pl.pallas_call(
        halo_kernel,
        grid_spec=pltpu.PrefetchScalarGridSpec(
            num_scalar_prefetch=1,
            grid=(parts,),
            in_specs=[fast, fast, slow, slow, IN_HBM],
            out_specs=[pl.BlockSpec((2, rows, WIDTH), lambda i, s: (0, i, 0))] * 2,
        ),
        out_shape=[shape] * 2,
        cost_estimate=pl.CostEstimate(flops=0, bytes_accessed=10 * 2**20, transcendentals=0),
    )(scalars, keys, values, keys, values, after)
    return [out.reshape(2 * FRAME, WIDTH) for out in outs]


def pass_kernel(a, b, c, d, after, out_ref):
    rows = a.shape[0]
    for n, ref in enumerate((a, b, c, d)):
        out_ref[n * rows : n * rows + rows, :] = ref[...]


def pack_passed(arrived, after):
    rows = arrived[0].shape[0] // 2
    return pl.pallas_call(
        pass_kernel,
        grid=(1,),
        in_specs=[pl.BlockSpec((rows, WIDTH), lambda i: (1, 0))] * NZ + [IN_HBM],
        out_specs=pl.BlockSpec((NZ * rows, WIDTH), lambda i: (0, 0)),
        out_shape=jax.ShapeDtypeStruct((NZ * rows, WIDTH), jnp.bfloat16),
        cost_estimate=pl.CostEstimate(flops=0, bytes_accessed=2 * 2**20, transcendentals=0),
    )(*arrived, after)


def select_kernel(picks, *refs):
    sources, outs = refs[:NX], refs[NX:]
    for dz, out in enumerate(outs):
        for dc in range(NC):
            for s in range(NX):
                for k in range(CAP):
                    block = picks[k * NZ * NC + dz * NC + dc, s]
                    at = pl.ds(pl.multiple_of(block * 2 * THIN, 2 * THIN), 2 * THIN)
                    to = ((dc * NX + s) * CAP + k) * 2 * THIN
                    out[to : to + 2 * THIN, :] = sources[s][at, :]


def select(picks, sources):
    shape = jax.ShapeDtypeStruct((NC * NX * CAP * 2 * THIN, WIDTH), jnp.bfloat16)
    whole = lambda a: pl.BlockSpec(a.shape, lambda i, *_: (0, 0))
    return pl.pallas_call(
        select_kernel,
        grid_spec=pltpu.PrefetchScalarGridSpec(
            num_scalar_prefetch=1,
            grid=(1,),
            in_specs=[whole(s) for s in sources],
            out_specs=[whole(shape)] * NZ,
        ),
        out_shape=[shape] * NZ,
        compiler_params=pltpu.CompilerParams(vmem_limit_bytes=VMEM_LIMIT),
        cost_estimate=pl.CostEstimate(flops=0, bytes_accessed=4 * 2**20, transcendentals=0),
    )(picks, *sources)


TILES = 4


def project_kernel(scalars, *refs):
    fast, slow, weight, w_one, w_two, w_swap, out_ref, a_vm, w_vm, sems = (
        refs[:4],
        refs[4:8],
        *refs[8:],
    )
    t, h = scalars[0], scalars[1]
    core = t & 1
    step = pl.program_id(0)
    rows, cols = a_vm.shape[0], w_vm.shape[2]
    gets_fast = (h >> 1) == 1 - core

    def part_copies(refs):
        return [
            pltpu.make_async_copy(
                ref, a_vm.at[:, pl.ds(e * WIDTH, WIDTH)], sems.at[TILES, e]
            )
            for e, ref in enumerate(refs)
        ]

    def weight_copies(tile, direct):
        per_half = TILES // NC
        at = pl.ds((tile % per_half) * cols, cols)
        span = lambda n, count=1: pl.ds(n * WIDTH, count * WIDTH)
        to = w_vm.at[tile]
        pairs = [(weight.at[:, pl.ds(tile * cols, cols)], to.at[span(0)])]
        if direct:
            pairs += [
                (w_one.at[:, at], to.at[span(1)]),
                (w_two.at[span(0), at], to.at[span(3)]),
                (w_two.at[span(1), at], to.at[span(2)]),
            ]
        else:
            pairs += [
                (w_swap.at[span(0), at], to.at[span(1)]),
                (w_swap.at[span(1), at], to.at[span(3)]),
                (w_swap.at[span(2), at], to.at[span(2)]),
            ]
        return [pltpu.make_async_copy(a, b, sems.at[tile, n]) for n, (a, b) in enumerate(pairs)]

    @pl.when(step == 0)
    def _():
        @pl.when(gets_fast)
        def _():
            for copy in part_copies(fast):
                copy.start()

        @pl.when(jnp.logical_not(gets_fast))
        def _():
            for copy in part_copies(slow):
                copy.start()

        for tile in range(TILES):
            half = tile // (TILES // NC)
            for direct in (True, False):

                @pl.when((core == half) == direct)
                def _(tile=tile, direct=direct):
                    for copy in weight_copies(tile, direct):
                        copy.start()

        for copy in part_copies(fast):
            copy.wait()

    for tile in range(TILES):

        @pl.when(step == tile)
        def _(tile=tile):
            for copy in weight_copies(tile, True):
                copy.wait()

    out_ref[...] = jnp.dot(
        a_vm[...], w_vm[step], preferred_element_type=jnp.float32
    ).astype(jnp.bfloat16)


def project(scalars, fast, slow, weight, w_one, w_two, w_swap):
    anywhere = IN_HBM
    rows, width = CHUNK * BLK, weight.shape[1]
    depth = NHEAD * WIDTH
    inputs = (*fast, *slow, weight, w_one, w_two, w_swap)
    return pl.pallas_call(
        project_kernel,
        grid_spec=pltpu.PrefetchScalarGridSpec(
            num_scalar_prefetch=1,
            grid=(TILES,),
            in_specs=[anywhere] * len(inputs),
            out_specs=pl.BlockSpec((rows, width // TILES), lambda i, s: (0, i)),
            scratch_shapes=[
                pltpu.VMEM((rows, depth), jnp.bfloat16),
                pltpu.VMEM((TILES, depth, width // TILES), jnp.bfloat16),
                pltpu.SemaphoreType.DMA((TILES + 1, NHEAD)),
            ],
        ),
        out_shape=jax.ShapeDtypeStruct((rows, width), jnp.bfloat16),
        compiler_params=pltpu.CompilerParams(vmem_limit_bytes=VMEM_LIMIT),
        cost_estimate=pl.CostEstimate(
            flops=2 * rows * depth * width, bytes_accessed=10 * 2**20, transcendentals=0
        ),
    )(scalars, *inputs)


def per_device(query, keys, values, out_weight, near_list, far_list, stride_table):
    t = lax.axis_index("tm")
    h = lax.axis_index("head")
    core = t % NC
    coords = [(zz, xx, cc) for zz in range(NZ) for xx in range(NX) for cc in range(NC)]
    swap = [(i, i ^ 1) for i in range(NTM)]
    across = [(i, i + 1) for i in range(1, NTM - 1, 2)]
    across = across + [(j, i) for i, j in across]
    place = jnp.stack([t, h]).astype(jnp.int32)

    def thin(a):
        return a.reshape(BLOCKS, THIN, MINSTRIDE, WIDTH)[:, :, 0]

    thinned = jnp.concatenate([thin(keys), thin(values)], axis=1).reshape(-1, WIDTH)
    along_x = [
        lax.ppermute(
            thinned, "tm", [(tm_index(*p), tm_index(p[0], p[1] + d, p[2])) for p in coords]
        )
        for d in range(1, NX)
    ]

    fast_part, slow_part = pack_halos(place, keys, values, thinned)
    halo_fast = lax.ppermute(fast_part, "tm", swap)
    halo_slow = lax.ppermute(slow_part, "tm", across)

    cols = out_weight.shape[1] // NC
    half = lax.dynamic_slice_in_dim(out_weight, core * cols, cols, 1)
    half, *along_x = lax.optimization_barrier((half, *along_x))
    w_one = lax.ppermute(half, "head", [(g, g ^ 1) for g in range(NHEAD)])

    picks, table = index_work(place, stride_table, far_list, near_list)

    packs = select(picks, [thinned] + along_x)
    arrived = [packs[0]]
    for d in range(1, NZ):
        pairs = [(tm_index(*p), tm_index(p[0] + d, p[1], p[2])) for p in coords]
        arrived.append(lax.ppermute(packs[d], "tm", pairs))
    w_two = lax.ppermute(
        jnp.concatenate([half, w_one], axis=0), "head", [(g, g ^ 3) for g in range(NHEAD)]
    )
    near_fast = attend(table, query, keys, values, halo_fast, None, FAST_FIRST, 2)
    halo_slow, near_fast = lax.optimization_barrier((halo_slow, near_fast))
    near_slow = attend(table, query, keys, values, halo_slow, None, SLOW_FIRST, 2)
    passed = lax.ppermute(pack_passed(arrived, near_slow[1]), "tm", swap)
    far = [*arrived, passed]
    w_swap = lax.ppermute(jnp.concatenate([w_one, w_two], axis=0), "tm", swap)
    first_fast, last_fast = merge_far(table, query, near_fast, far, FAST_FIRST, w_two)
    near_slow, first_fast = lax.optimization_barrier((near_slow, first_fast))
    first_slow, last_slow = merge_far(table, query, near_slow, far, SLOW_FIRST, w_swap)

    def exchange(chunk, e, fast):
        pairs = []
        for i in range(NTM):
            frame = (1 - i % NC) if fast else i % NC
            for g in range(NHEAD):
                if (e >= 2) == (g // 2 != frame):
                    pairs.append((i * NHEAD + g, i * NHEAD + (g ^ e)))
        return lax.ppermute(chunk, ("tm", "head"), pairs)

    fast = [last_fast, *(exchange(first_fast, e, True) for e in (1, 2)), exchange(last_fast, 3, True)]
    slow = [
        last_slow,
        *(exchange(first_slow, e, False) for e in (1, 2)),
        exchange(last_slow, 3, False),
    ]
    return project(place, fast, slow, out_weight, w_one, w_two, w_swap)


def solution(mesh):
    placed = (
        P("tm", "head"),
        P("tm", "head"),
        P("tm", "head"),
        P("head", None),
        P("tm", None),
        P(),
        P(),
    )
    return jax.shard_map(
        per_device, mesh=mesh, in_specs=placed, out_specs=P(("tm", "head"), None), check_vma=False
    )
```

time: 531 us -> 156 us (0.29)
  local copies, waits for them, and re-layouts: 230 us -> 8.85 us
  waiting for transfers between devices: 146 us -> 31.2 us
  matrix products: 91.7 us -> 0 us
  Pallas kernels: 0 us -> 79.7 us
  other arithmetic: 38.7 us -> 2.57 us
  starting transfers between devices: 4.08 us -> 32.7 us
  between operations: 13.5 us -> 0.46 us
    gather x14 -> x0, local copies, waits for them, and re-layouts: 118 us -> none  [the longest x12 105 us: group_step(): near_pair = extended[:, :, chosen].reshape(2, heads, 4, KNEAR * BLK, HD)]
    dot_general x13 -> x0, matrix products: 91.7 us -> none  [the longest x6 46.1 us: attend_group(): jnp.einsum('hgqd,hgkd->hgqk', queries, key_rows, preferred_element_type=j...]
    reduce_scatter x1 -> x0, waiting for transfers between devices: 88.5 us -> none  [per_device(): lax.psum_scatter(jnp.dot(attended, out_weight, preferred_element_type=jnp...]
    pallas_call x0 -> x9, Pallas kernels: none -> 79.7 us  [the longest x2 39.6 us: attend(): pl.pallas_call(functools.partial(attend_kernel, chunk=chunk, with_far=wit...]
    all_gather x1 -> x0, waiting for transfers between devices: 57.3 us -> none  [per_device(): everything = lax.all_gather(thinned, 'tm', axis=2, tiled=True)]
    ppermute x2 -> x18, waiting for transfers between devices: 0.01 us -> 31.2 us  [the longest x6 18.3 us: exchange(): return lax.ppermute(chunk, ('tm', 'head'), pairs)]
    ppermute x2 -> x18, starting transfers between devices: 4.04 us -> 32.7 us  [the longest x6 11.7 us: exchange(): return lax.ppermute(chunk, ('tm', 'head'), pairs)]
    slice x6 -> x2, local copies, waits for them, and re-layouts: 31 us -> 2.85 us  [thin(): return a.reshape(BLOCKS, THIN, MINSTRIDE, WIDTH)[:, :, 0]]
  transfers between devices with their start and end apart: 4 -> 18, of which waited for: 2 -> 6; matrix products, arithmetic and copies ran while one was open for 8% -> 2% of each run, Pallas kernels for 0% -> 42%
where the time goes in v2:
time: 156 us; the launch traced here: 155 us
  Pallas kernels  79.7 us (51%)
  starting transfers between devices  32.7 us (21%)
  waiting for transfers between devices  31.2 us (20%)
  local copies, waits for them, and re-layouts  8.85 us (6%)
  other arithmetic  2.57 us (2%)
    pallas_call x2, Pallas kernels, attend(): pl.pallas_call(functools.partial(attend_kernel, chunk=chunk, with_far=wit...  39.6 us
    ppermute x6, waiting for transfers between devices, exchange(): return lax.ppermute(chunk, ('tm', 'head'), pairs)  18.3 us
    pallas_call x2, Pallas kernels, merge_far(): pl.pallas_call(functools.partial(merge_kernel, chunk=chunk), grid_spec=pl...  15.1 us
    ppermute x6, starting transfers between devices, exchange(): return lax.ppermute(chunk, ('tm', 'head'), pairs)  11.7 us
    ppermute x3, waiting for transfers between devices, per_device(): lax.ppermute(thinned, 'tm', [(tm_index(*p), tm_index(p[0], p[1] + d, p[2]...  10.6 us
    pallas_call x1, Pallas kernels, project(): pl.pallas_call(project_kernel, grid_spec=pltpu.PrefetchScalarGridSpec(num...  9.25 us
    ppermute x3, starting transfers between devices, per_device(): arrived.append(lax.ppermute(packs[d], 'tm', pairs))  7.84 us
    unnamed x42, local copies, waits for them, and re-layouts  5.91 us
  transfers between devices with their start and end apart: 18, of which 6 were waited for; matrix products, arithmetic and copies ran while one was open for 2% of the time, Pallas kernels for 42%

profile of v2, /device:TPU:0, one launch (start us, length us, event | category | flops | bytes accessed | tf_op | source)
XLA Modules:
  0.0 155.5 jit_solution(11623242192503372479)
XLA Ops:
  0.0 1.4 slice.8
  1.4 1.4 slice.9
  4.3 5.8 %shard_map.74 = (bf16[2,1536,384]{2,1,0:T(8,128)(2,1)}, bf16[2,1536,384]{2,1,0:T(8,128)(2,1)}) custom-call(s32[2]{0:T(128)} %pad_add_fusion.scalars, bf16[3072,384]{1,0:T(8,128)(2,1)} %k_ref.3, bf16[3072,384]{1,0:T(8,128)(2,1)} %v_ref.3, bf16[3072,384]{1,0:T(8,128)(2,1)} %k_ref.3, bf16[3072,384]{1,0:T(8,128)(2,1)} %v_ref.3, bf16[384,384]{1,0:T(8,128)(2,1)} %bitcast.13), custom_call_target="tpu_custom_call" | custom-call | bytes 10485760 | tf_op jit(solution)/shard_map/pallas_call | solution.py:435
  10.1 1.6 %collective-permute-start.2 = (bf16[384,384]{1,0:T(8,128)(2,1)S(1)}, bf16[384,384]{1,0:T(8,128)(2,1)S(1)}, u32[]{:S(2)}, u32[]{:S(2)}) collective-permute-start(bf16[384,384]{1,0:T(8,128)(2,1)S(1)} %bitcast.15), channel_id=1, source_target_pairs={{0,8},{4,12},{8,16},{12,20},{16,24},{20,28},{24,0},{28,4},{32,40},... | collective-permute-start | bytes 884744 | tf_op jit(solution)/shard_map/ppermute | solution.py:616
  11.7 2.7 %collective-permute-start.3 = (bf16[384,384]{1,0:T(8,128)(2,1)S(1)}, bf16[384,384]{1,0:T(8,128)(2,1)S(1)}, u32[]{:S(2)}, u32[]{:S(2)}) collective-permute-start(bf16[384,384]{1,0:T(8,128)(2,1)S(1)} %bitcast.16), channel_id=1, source_target_pairs={{0,16},{4,20},{8,24},{12,28},{16,0},{20,4},{24,8},{28,12},{32,48},... | collective-permute-start | bytes 884744 | tf_op jit(solution)/shard_map/ppermute | solution.py:616
  14.5 1.4 collective-permute-start.4
  15.9 2.1 %collective-permute-start = (bf16[3072,384]{1,0:T(8,128)(2,1)}, bf16[3072,384]{1,0:T(8,128)(2,1)}, u32[]{:S(2)}, u32[]{:S(2)}) collective-permute-start(bf16[3072,384]{1,0:T(8,128)(2,1)} %bitcast.18), channel_id=1, source_target_pairs={{4,8},{12,16},{20,24},{28,32},{36,40},{44,48},{52,56},{60,64},{68,... | collective-permute-start | bytes 7077896 | tf_op jit(solution)/shard_map/ppermute | solution.py:624
  18.1 2.7 %collective-permute-done.2.refs_1_ = bf16[384,384]{1,0:T(8,128)(2,1)S(1)} collective-permute-done((bf16[384,384]{1,0:T(8,128)(2,1)S(1)}, bf16[384,384]{1,0:T(8,128)(2,1)S(1)}, u32[]{:S(2)}, u32[]{:S(2)}) %collective-permute-start.2) | collective-permute-done | bytes 294944 | tf_op jit(solution)/shard_map/ppermute | solution.py:616
  20.7 7.9 %collective-permute-done.3.refs_2_ = bf16[384,384]{1,0:T(8,128)(2,1)S(1)} collective-permute-done((bf16[384,384]{1,0:T(8,128)(2,1)S(1)}, bf16[384,384]{1,0:T(8,128)(2,1)S(1)}, u32[]{:S(2)}, u32[]{:S(2)}) %collective-permute-start.3) | collective-permute-done | bytes 294944 | tf_op jit(solution)/shard_map/ppermute | solution.py:616
  28.6 1.7 %collective-permute-start.9 = (bf16[384,768]{1,0:T(8,128)(2,1)S(1)}, bf16[384,768]{1,0:T(8,128)(2,1)S(1)}, u32[]{:S(2)}, u32[]{:S(2)}) collective-permute-start(bf16[384,768]{1,0:T(8,128)(2,1)S(1)} %constant_dynamic-slice_fusion), channel_id=1, source_target_pairs={{0,1},{1,0},{2,3},{3,2},{4,5},{5,4},{6,7},{7,6},{8,9},{9,8},{10,11... | collective-permute-start | bytes 1769480 | tf_op jit(solution)/shard_map/ppermute | solution.py:629
  31.9 3.4 %shard_map.73 = (s32[48,128]{1,0:T(8,128)}, s32[32,128]{1,0:T(8,128)}) custom-call(s32[2]{0:T(128)} %pad_add_fusion.scalars, s32[64]{0:T(128)} %steps.1, s32[768,16]{1,0:T(8,128)} %copy.8.far_ref, s32[24,16]{1,0:T(8,128)} %copy.9.near_ref), custom_call_target="tpu_custom_call" | custom-call | flops 1048576 | bytes 4194304 | tf_op jit(solution)/shard_map/pallas_call | solution.py:409
  35.3 4.1 %shard_map.76 = (bf16[768,384]{1,0:T(8,128)(2,1)}, bf16[768,384]{1,0:T(8,128)(2,1)}, bf16[768,384]{1,0:T(8,128)(2,1)}, bf16[768,384]{1,0:T(8,128)(2,1)}) custom-call(s32[48,128]{1,0:T(8,128)} %get-tuple-element.38.picks, bf16[384,384]{1,0:T(8,128)(2,1)} %bitcast.14, bf16[384,384]{1,0:T(8,128)(2,1)} %copy-done.9, bf16[384,384]{1,0:T(8,128)(2,1)} %copy-done.10, ...), custom_call_target="tpu_custom_call" | custom-call | bytes 4194304 | tf_op jit(solution)/shard_map/pallas_call | solution.py:482
  39.4 1.9 %collective-permute-start.5 = (bf16[768,384]{1,0:T(8,128)(2,1)}, bf16[768,384]{1,0:T(8,128)(2,1)S(1)}, u32[]{:S(2)}, u32[]{:S(2)}) collective-permute-start(bf16[768,384]{1,0:T(8,128)(2,1)} %get-tuple-element.43), channel_id=1, source_target_pairs={{0,32},{4,36},{8,40},{12,44},{16,48},{20,52},{24,56},{28,60},{32,6... | collective-permute-start | bytes 1769480 | tf_op jit(solution)/shard_map/ppermute | solution.py:637
  41.3 3.5 %collective-permute-start.6 = (bf16[768,384]{1,0:T(8,128)(2,1)}, bf16[768,384]{1,0:T(8,128)(2,1)S(1)}, u32[]{:S(2)}, u32[]{:S(2)}) collective-permute-start(bf16[768,384]{1,0:T(8,128)(2,1)} %get-tuple-element.44), channel_id=1, source_target_pairs={{0,64},{4,68},{8,72},{12,76},{16,80},{20,84},{24,88},{28,92},{32,9... | collective-permute-start | bytes 1769480 | tf_op jit(solution)/shard_map/ppermute | solution.py:637
  44.8 2.4 %collective-permute-start.7 = (bf16[768,384]{1,0:T(8,128)(2,1)}, bf16[768,384]{1,0:T(8,128)(2,1)S(1)}, u32[]{:S(2)}, u32[]{:S(2)}) collective-permute-start(bf16[768,384]{1,0:T(8,128)(2,1)} %get-tuple-element.45), channel_id=1, source_target_pairs={{0,96},{4,100},{8,104},{12,108},{16,112},{20,116},{24,120},{28,124... | collective-permute-start | bytes 1769480 | tf_op jit(solution)/shard_map/ppermute | solution.py:637
  48.3 3.0 %collective-permute-start.10 = (bf16[768,768]{1,0:T(8,128)(2,1)}, bf16[768,768]{1,0:T(8,128)(2,1)S(1)}, u32[]{:S(2)}, u32[]{:S(2)}) collective-permute-start(bf16[768,768]{1,0:T(8,128)(2,1)} %pad_maximum_fusion.1), channel_id=1, source_target_pairs={{0,3},{1,2},{2,1},{3,0},{4,7},{5,6},{6,5},{7,4},{8,11},{9,10},{10,... | collective-permute-start | bytes 3538952 | tf_op jit(solution)/shard_map/ppermute | solution.py:638
  51.4 19.8 %shard_map.75 = (bf16[1536,384]{1,0:T(8,128)(2,1)}, f32[1536,384]{1,0:T(8,128)}) custom-call(s32[32,128]{1,0:T(8,128)} %get-tuple-element.31.table, bf16[3072,384]{1,0:T(8,128)(2,1)} %q_ref.7, bf16[3072,384]{1,0:T(8,128)(2,1)} %k_ref.3, bf16[3072,384]{1,0:T(8,128)(2,1)} %v_ref.3, bf16[3072,384]{1,0:T(8,128)(2,1)} %collective-permute-done.1.halo_ref), custom_call_target="tpu_custom_call" | custom-call | flops 15401484288 | bytes 8388608 | tf_op jit(solution)/shard_map/pallas_call | solution.py:214
  71.2 19.8 %shard_map.77 = (bf16[1536,384]{1,0:T(8,128)(2,1)}, f32[1536,384]{1,0:T(8,128)}) custom-call(s32[32,128]{1,0:T(8,128)} %get-tuple-element.31.table, bf16[3072,384]{1,0:T(8,128)(2,1)} %q_ref.7, bf16[3072,384]{1,0:T(8,128)(2,1)} %k_ref.3, bf16[3072,384]{1,0:T(8,128)(2,1)} %v_ref.3, bf16[3072,384]{1,0:T(8,128)(2,1)} %collective-permute-done.halo_ref), custom_call_target="tpu_custom_call" | custom-call | flops 15401484288 | bytes 8388608 | tf_op jit(solution)/shard_map/pallas_call | solution.py:214
  92.3 2.4 %shard_map.78 = bf16[1536,384]{1,0:T(8,128)(2,1)} custom-call(bf16[768,384]{1,0:T(8,128)(2,1)} %get-tuple-element.42.a.rest_0_, bf16[768,384]{1,0:T(8,128)(2,1)} %copy-done, bf16[768,384]{1,0:T(8,128)(2,1)} %copy-done.1, bf16[768,384]{1,0:T(8,128)(2,1)} %copy-done.2, f32[1536,384]{1,0:T(8,128)} %get-tuple-element.54.after.level_ref), custom_call_target="tpu_custom_call" | custom-call | bytes 2097152 | tf_op jit(solution)/shard_map/pallas_call | solution.py:457
  95.4 2.3 %collective-permute-done.8.rest_4_ = bf16[1536,384]{1,0:T(8,128)(2,1)S(1)} collective-permute-done((bf16[1536,384]{1,0:T(8,128)(2,1)}, bf16[1536,384]{1,0:T(8,128)(2,1)S(1)}, u32[]{:S(2)}, u32[]{:S(2)}) %collective-permute-start.8) | collective-permute-done | bytes 1179680 | tf_op jit(solution)/shard_map/ppermute | solution.py:644
  98.7 7.6 %shard_map.79 = (bf16[768,384]{1,0:T(8,128)(2,1)}, bf16[768,384]{1,0:T(8,128)(2,1)}) custom-call(s32[32,128]{1,0:T(8,128)} %get-tuple-element.31.table, bf16[3072,384]{1,0:T(8,128)(2,1)} %q_ref.7, bf16[1536,384]{1,0:T(8,128)(2,1)} %get-tuple-element.36.near_ref, f32[1536,384]{1,0:T(8,128)} %get-tuple-element.37.level_ref, ...), custom_call_target="tpu_custom_call" | custom-call | flops 1811939328 | bytes 8388608 | tf_op jit(solution)/shard_map/pallas_call | solution.py:292
  107.0 4.8 %collective-permute-start.12 = (bf16[768,384]{1,0:T(8,128)(2,1)}, bf16[768,384]{1,0:T(8,128)(2,1)S(1)}, u32[]{:S(2)}, u32[]{:S(2)}) collective-permute-start(bf16[768,384]{1,0:T(8,128)(2,1)} %get-tuple-element.52), channel_id=1, source_target_pairs={{0,2},{1,3},{6,4},{7,5},{8,10},{9,11},{14,12},{15,13},{16,18},{17,... | collective-permute-start | bytes 1769480 | tf_op jit(solution)/shard_map/ppermute | solution.py:658
  111.9 1.3 collective-permute-start.13
  113.2 1.2 copy-done.7
  114.4 7.6 %shard_map.80 = (bf16[768,384]{1,0:T(8,128)(2,1)}, bf16[768,384]{1,0:T(8,128)(2,1)}) custom-call(s32[32,128]{1,0:T(8,128)} %get-tuple-element.31.table, bf16[3072,384]{1,0:T(8,128)(2,1)} %q_ref.7, bf16[1536,384]{1,0:T(8,128)(2,1)} %get-tuple-element.53.near_ref, f32[1536,384]{1,0:T(8,128)} %get-tuple-element.54.after.level_ref, ...), custom_call_target="tpu_custom_call" | custom-call | flops 1811939328 | bytes 8388608 | tf_op jit(solution)/shard_map/pallas_call | solution.py:292
  122.0 2.3 %collective-permute-start.15 = (bf16[768,384]{1,0:T(8,128)(2,1)}, bf16[768,384]{1,0:T(8,128)(2,1)S(1)}, u32[]{:S(2)}, u32[]{:S(2)}) collective-permute-start(bf16[768,384]{1,0:T(8,128)(2,1)} %get-tuple-element.56), channel_id=1, source_target_pairs={{0,1},{1,0},{6,7},{7,6},{8,9},{9,8},{14,15},{15,14},{16,17},{17,16... | collective-permute-start | bytes 1769480 | tf_op jit(solution)/shard_map/ppermute | solution.py:658
  124.3 1.3 collective-permute-start.16
  125.6 1.3 collective-permute-start.17
  127.0 10.9 %collective-permute-done.15.refs_5_ = bf16[768,384]{1,0:T(8,128)(2,1)S(1)} collective-permute-done((bf16[768,384]{1,0:T(8,128)(2,1)}, bf16[768,384]{1,0:T(8,128)(2,1)S(1)}, u32[]{:S(2)}, u32[]{:S(2)}) %collective-permute-start.15) | collective-permute-done | bytes 589856 | tf_op jit(solution)/shard_map/ppermute | solution.py:658
  137.9 3.6 %collective-permute-done.16.refs_6_ = bf16[768,384]{1,0:T(8,128)(2,1)S(1)} collective-permute-done((bf16[768,384]{1,0:T(8,128)(2,1)}, bf16[768,384]{1,0:T(8,128)(2,1)S(1)}, u32[]{:S(2)}, u32[]{:S(2)}) %collective-permute-start.16) | collective-permute-done | bytes 589856 | tf_op jit(solution)/shard_map/ppermute | solution.py:658
  141.5 3.7 %collective-permute-done.17.refs_7_ = bf16[768,384]{1,0:T(8,128)(2,1)S(1)} collective-permute-done((bf16[768,384]{1,0:T(8,128)(2,1)}, bf16[768,384]{1,0:T(8,128)(2,1)S(1)}, u32[]{:S(2)}, u32[]{:S(2)}) %collective-permute-start.17) | collective-permute-done | bytes 589856 | tf_op jit(solution)/shard_map/ppermute | solution.py:658
  146.1 9.2 %shard_map.81 = bf16[768,1536]{1,0:T(8,128)(2,1)} custom-call(s32[2]{0:T(128)} %pad_add_fusion.scalars, bf16[768,384]{1,0:T(8,128)(2,1)} %get-tuple-element.49.refs_0_, bf16[768,384]{1,0:T(8,128)(2,1)} %copy-done.14, bf16[768,384]{1,0:T(8,128)(2,1)} %copy-done.15, bf16[768,384]{1,0:T(8,128)(2,1)} %copy-done.16, bf16[768,384]{1,0:T(8,128)(2,1)} %get-tuple-element.55.refs_4_, ...), custom_call_target="tpu_custom_call" | custom-call | flops 3623878656 | bytes 10485760 | tf_op jit(solution)/shard_map/pallas_call | solution.py:580
  (63 shorter events, 8.6 us)
Async XLA Ops:
  4.3 5.8 %copy-start.5 = (bf16[24,16,384]{2,1,0:T(8,128)(2,1)S(1)}, bf16[24,16,384]{2,1,0:T(8,128)(2,1)}, u32[]{:S(2)}) copy-start(bf16[24,16,384]{2,1,0:T(8,128)(2,1)} %pad_maximum_fusion.2) | copy-start | bytes 884740
  4.3 13.8 %copy-start.8 = (bf16[384,1536]{1,0:T(8,128)(2,1)S(1)}, bf16[384,1536]{1,0:T(8,128)(2,1)}, u32[]{:S(2)}) copy-start(bf16[384,1536]{1,0:T(8,128)(2,1)} %refs_8_.1) | copy-start | bytes 3538948
  4.3 26.0 %copy-start.12 = (s32[768,16]{0,1:T(8,128)S(1)}, s32[768,16]{0,1:T(8,128)}, u32[]{:S(2)}) copy-start(s32[768,16]{0,1:T(8,128)} %param.12) | copy-start | bytes 147460
  4.3 27.0 %copy-start.13 = (s32[24,16]{0,1:T(8,128)S(1)}, s32[24,16]{0,1:T(8,128)}, u32[]{:S(2)}) copy-start(s32[24,16]{0,1:T(8,128)} %param.11) | copy-start | bytes 4612
  10.1 38.2 %collective-permute-start.1 = (bf16[3072,384]{1,0:T(8,128)(2,1)}, bf16[3072,384]{1,0:T(8,128)(2,1)}, u32[]{:S(2)}, u32[]{:S(2)}) collective-permute-start(bf16[3072,384]{1,0:T(8,128)(2,1)} %bitcast.19), channel_id=1, source_target_pairs={{0,4},{4,0},{8,12},{12,8},{16,20},{20,16},{24,28},{28,24},{32,36},... | collective-permute-start | bytes 7077896 | tf_op jit(solution)/shard_map/ppermute | solution.py:623
  10.1 10.6 %collective-permute-start.2 = (bf16[384,384]{1,0:T(8,128)(2,1)S(1)}, bf16[384,384]{1,0:T(8,128)(2,1)S(1)}, u32[]{:S(2)}, u32[]{:S(2)}) collective-permute-start(bf16[384,384]{1,0:T(8,128)(2,1)S(1)} %bitcast.15), channel_id=1, source_target_pairs={{0,8},{4,12},{8,16},{12,20},{16,24},{20,28},{24,0},{28,4},{32,40},... | collective-permute-start | bytes 884744 | tf_op jit(solution)/shard_map/ppermute | solution.py:616
  11.7 16.9 %collective-permute-start.3 = (bf16[384,384]{1,0:T(8,128)(2,1)S(1)}, bf16[384,384]{1,0:T(8,128)(2,1)S(1)}, u32[]{:S(2)}, u32[]{:S(2)}) collective-permute-start(bf16[384,384]{1,0:T(8,128)(2,1)S(1)} %bitcast.16), channel_id=1, source_target_pairs={{0,16},{4,20},{8,24},{12,28},{16,0},{20,4},{24,8},{28,12},{32,48},... | collective-permute-start | bytes 884744 | tf_op jit(solution)/shard_map/ppermute | solution.py:616
  14.5 14.2 %collective-permute-start.4 = (bf16[384,384]{1,0:T(8,128)(2,1)S(1)}, bf16[384,384]{1,0:T(8,128)(2,1)S(1)}, u32[]{:S(2)}, u32[]{:S(2)}) collective-permute-start(bf16[384,384]{1,0:T(8,128)(2,1)S(1)} %bitcast.17), channel_id=1, source_target_pairs={{0,24},{4,28},{8,0},{12,4},{16,8},{20,12},{24,16},{28,20},{32,56},... | collective-permute-start | bytes 884744 | tf_op jit(solution)/shard_map/ppermute | solution.py:616
  15.9 55.3 %collective-permute-start = (bf16[3072,384]{1,0:T(8,128)(2,1)}, bf16[3072,384]{1,0:T(8,128)(2,1)}, u32[]{:S(2)}, u32[]{:S(2)}) collective-permute-start(bf16[3072,384]{1,0:T(8,128)(2,1)} %bitcast.18), channel_id=1, source_target_pairs={{4,8},{12,16},{20,24},{28,32},{36,40},{44,48},{52,56},{60,64},{68,... | collective-permute-start | bytes 7077896 | tf_op jit(solution)/shard_map/ppermute | solution.py:624
  20.7 14.6 %copy-start.9 = (bf16[384,384]{1,0:T(8,128)(2,1)}, bf16[384,384]{1,0:T(8,128)(2,1)S(1)}, u32[]{:S(2)}) copy-start(bf16[384,384]{1,0:T(8,128)(2,1)S(1)} %collective-permute-done.2.refs_1_) | copy-start | bytes 884740
  28.6 6.7 %copy-start.10 = (bf16[384,384]{1,0:T(8,128)(2,1)}, bf16[384,384]{1,0:T(8,128)(2,1)S(1)}, u32[]{:S(2)}) copy-start(bf16[384,384]{1,0:T(8,128)(2,1)S(1)} %collective-permute-done.3.refs_2_) | copy-start | bytes 884740
  28.6 6.7 %copy-start.11 = (bf16[384,384]{1,0:T(8,128)(2,1)}, bf16[384,384]{1,0:T(8,128)(2,1)S(1)}, u32[]{:S(2)}) copy-start(bf16[384,384]{1,0:T(8,128)(2,1)S(1)} %collective-permute-done.4.refs_3_) | copy-start | bytes 884740
  28.6 16.2 %collective-permute-start.9 = (bf16[384,768]{1,0:T(8,128)(2,1)S(1)}, bf16[384,768]{1,0:T(8,128)(2,1)S(1)}, u32[]{:S(2)}, u32[]{:S(2)}) collective-permute-start(bf16[384,768]{1,0:T(8,128)(2,1)S(1)} %constant_dynamic-slice_fusion), channel_id=1, source_target_pairs={{0,1},{1,0},{2,3},{3,2},{4,5},{5,4},{6,7},{7,6},{8,9},{9,8},{10,11... | collective-permute-start | bytes 1769480 | tf_op jit(solution)/shard_map/ppermute | solution.py:629
  39.4 51.6 %collective-permute-start.5 = (bf16[768,384]{1,0:T(8,128)(2,1)}, bf16[768,384]{1,0:T(8,128)(2,1)S(1)}, u32[]{:S(2)}, u32[]{:S(2)}) collective-permute-start(bf16[768,384]{1,0:T(8,128)(2,1)} %get-tuple-element.43), channel_id=1, source_target_pairs={{0,32},{4,36},{8,40},{12,44},{16,48},{20,52},{24,56},{28,60},{32,6... | collective-permute-start | bytes 1769480 | tf_op jit(solution)/shard_map/ppermute | solution.py:637
  41.3 49.7 %collective-permute-start.6 = (bf16[768,384]{1,0:T(8,128)(2,1)}, bf16[768,384]{1,0:T(8,128)(2,1)S(1)}, u32[]{:S(2)}, u32[]{:S(2)}) collective-permute-start(bf16[768,384]{1,0:T(8,128)(2,1)} %get-tuple-element.44), channel_id=1, source_target_pairs={{0,64},{4,68},{8,72},{12,76},{16,80},{20,84},{24,88},{28,92},{32,9... | collective-permute-start | bytes 1769480 | tf_op jit(solution)/shard_map/ppermute | solution.py:637
  44.8 49.8 %copy-start.6 = (bf16[384,768]{1,0:T(8,128)(2,1)}, bf16[384,768]{1,0:T(8,128)(2,1)S(1)}, u32[]{:S(2)}) copy-start(bf16[384,768]{1,0:T(8,128)(2,1)S(1)} %collective-permute-done.9.refs_9_) | copy-start | bytes 1769476
  44.8 46.2 %collective-permute-start.7 = (bf16[768,384]{1,0:T(8,128)(2,1)}, bf16[768,384]{1,0:T(8,128)(2,1)S(1)}, u32[]{:S(2)}, u32[]{:S(2)}) collective-permute-start(bf16[768,384]{1,0:T(8,128)(2,1)} %get-tuple-element.45), channel_id=1, source_target_pairs={{0,96},{4,100},{8,104},{12,108},{16,112},{20,116},{24,120},{28,124... | collective-permute-start | bytes 1769480 | tf_op jit(solution)/shard_map/ppermute | solution.py:637
  48.3 46.3 %collective-permute-start.10 = (bf16[768,768]{1,0:T(8,128)(2,1)}, bf16[768,768]{1,0:T(8,128)(2,1)S(1)}, u32[]{:S(2)}, u32[]{:S(2)}) collective-permute-start(bf16[768,768]{1,0:T(8,128)(2,1)} %pad_maximum_fusion.1), channel_id=1, source_target_pairs={{0,3},{1,2},{2,1},{3,0},{4,7},{5,6},{6,5},{7,4},{8,11},{9,10},{10,... | collective-permute-start | bytes 3538952 | tf_op jit(solution)/shard_map/ppermute | solution.py:638
  94.6 3.1 %collective-permute-start.8 = (bf16[1536,384]{1,0:T(8,128)(2,1)}, bf16[1536,384]{1,0:T(8,128)(2,1)S(1)}, u32[]{:S(2)}, u32[]{:S(2)}) collective-permute-start(bf16[1536,384]{1,0:T(8,128)(2,1)} %shard_map.78), channel_id=1, source_target_pairs={{0,4},{4,0},{8,12},{12,8},{16,20},{20,16},{24,28},{28,24},{32,36},... | collective-permute-start | bytes 3538952 | tf_op jit(solution)/shard_map/ppermute | solution.py:644
  94.7 3.0 %copy-start.3 = (bf16[768,768]{1,0:T(8,128)(2,1)}, bf16[768,768]{1,0:T(8,128)(2,1)S(1)}, u32[]{:S(2)}) copy-start(bf16[768,768]{1,0:T(8,128)(2,1)S(1)} %collective-permute-done.10.rest_5_.refs_10_) | copy-start | bytes 3538948
  94.8 18.4 %collective-permute-start.14 = (bf16[1152,768]{1,0:T(8,128)(2,1)S(1)}, bf16[1152,768]{1,0:T(8,128)(2,1)S(1)}, u32[]{:S(2)}, u32[]{:S(2)}) collective-permute-start(bf16[1152,768]{1,0:T(8,128)(2,1)S(1)} %pad_maximum_fusion), channel_id=1, source_target_pairs={{0,4},{4,0},{8,12},{12,8},{16,20},{20,16},{24,28},{28,24},{32,36},... | collective-permute-start | bytes 5308424 | tf_op jit(solution)/shard_map/ppermute | solution.py:646
  106.3 19.3 %collective-permute-start.11 = (bf16[768,384]{1,0:T(8,128)(2,1)}, bf16[768,384]{1,0:T(8,128)(2,1)S(1)}, u32[]{:S(2)}, u32[]{:S(2)}) collective-permute-start(bf16[768,384]{1,0:T(8,128)(2,1)} %get-tuple-element.52), channel_id=1, source_target_pairs={{2,3},{3,2},{4,5},{5,4},{10,11},{11,10},{12,13},{13,12},{18,19},{1... | collective-permute-start | bytes 1769480 | tf_op jit(solution)/shard_map/ppermute | solution.py:658
  107.0 19.9 %collective-permute-start.12 = (bf16[768,384]{1,0:T(8,128)(2,1)}, bf16[768,384]{1,0:T(8,128)(2,1)S(1)}, u32[]{:S(2)}, u32[]{:S(2)}) collective-permute-start(bf16[768,384]{1,0:T(8,128)(2,1)} %get-tuple-element.52), channel_id=1, source_target_pairs={{0,2},{1,3},{6,4},{7,5},{8,10},{9,11},{14,12},{15,13},{16,18},{17,... | collective-permute-start | bytes 1769480 | tf_op jit(solution)/shard_map/ppermute | solution.py:658
  111.9 15.1 %collective-permute-start.13 = (bf16[768,384]{1,0:T(8,128)(2,1)}, bf16[768,384]{1,0:T(8,128)(2,1)S(1)}, u32[]{:S(2)}, u32[]{:S(2)}) collective-permute-start(bf16[768,384]{1,0:T(8,128)(2,1)} %get-tuple-element.49.refs_0_), channel_id=1, source_target_pairs={{0,3},{1,2},{6,5},{7,4},{8,11},{9,10},{14,13},{15,12},{16,19},{17,... | collective-permute-start | bytes 1769480 | tf_op jit(solution)/shard_map/ppermute | solution.py:658
  122.0 15.9 %collective-permute-start.15 = (bf16[768,384]{1,0:T(8,128)(2,1)}, bf16[768,384]{1,0:T(8,128)(2,1)S(1)}, u32[]{:S(2)}, u32[]{:S(2)}) collective-permute-start(bf16[768,384]{1,0:T(8,128)(2,1)} %get-tuple-element.56), channel_id=1, source_target_pairs={{0,1},{1,0},{6,7},{7,6},{8,9},{9,8},{14,15},{15,14},{16,17},{17,16... | collective-permute-start | bytes 1769480 | tf_op jit(solution)/shard_map/ppermute | solution.py:658
  124.3 17.2 %collective-permute-start.16 = (bf16[768,384]{1,0:T(8,128)(2,1)}, bf16[768,384]{1,0:T(8,128)(2,1)S(1)}, u32[]{:S(2)}, u32[]{:S(2)}) collective-permute-start(bf16[768,384]{1,0:T(8,128)(2,1)} %get-tuple-element.56), channel_id=1, source_target_pairs={{2,0},{3,1},{4,6},{5,7},{10,8},{11,9},{12,14},{13,15},{18,16},{19,... | collective-permute-start | bytes 1769480 | tf_op jit(solution)/shard_map/ppermute | solution.py:658
  125.6 19.6 %copy-start.14 = (bf16[768,384]{1,0:T(8,128)(2,1)}, bf16[768,384]{1,0:T(8,128)(2,1)S(1)}, u32[]{:S(2)}) copy-start(bf16[768,384]{1,0:T(8,128)(2,1)S(1)} %collective-permute-done.11.refs_1_) | copy-start | bytes 1769476
  125.6 19.6 %collective-permute-start.17 = (bf16[768,384]{1,0:T(8,128)(2,1)}, bf16[768,384]{1,0:T(8,128)(2,1)S(1)}, u32[]{:S(2)}, u32[]{:S(2)}) collective-permute-start(bf16[768,384]{1,0:T(8,128)(2,1)} %get-tuple-element.55.refs_4_), channel_id=1, source_target_pairs={{2,1},{3,0},{4,7},{5,6},{10,9},{11,8},{12,15},{13,14},{18,17},{19,... | collective-permute-start | bytes 1769480 | tf_op jit(solution)/shard_map/ppermute | solution.py:658
  126.9 18.3 %copy-start.15 = (bf16[768,384]{1,0:T(8,128)(2,1)}, bf16[768,384]{1,0:T(8,128)(2,1)S(1)}, u32[]{:S(2)}) copy-start(bf16[768,384]{1,0:T(8,128)(2,1)S(1)} %collective-permute-done.12.refs_2_) | copy-start | bytes 1769476
  126.9 18.3 %copy-start.16 = (bf16[768,384]{1,0:T(8,128)(2,1)}, bf16[768,384]{1,0:T(8,128)(2,1)S(1)}, u32[]{:S(2)}) copy-start(bf16[768,384]{1,0:T(8,128)(2,1)S(1)} %collective-permute-done.13.refs_3_) | copy-start | bytes 1769476
  137.9 7.4 %copy-start.17 = (bf16[768,384]{1,0:T(8,128)(2,1)}, bf16[768,384]{1,0:T(8,128)(2,1)S(1)}, u32[]{:S(2)}) copy-start(bf16[768,384]{1,0:T(8,128)(2,1)S(1)} %collective-permute-done.15.refs_5_) | copy-start | bytes 1769476
  141.5 3.8 %copy-start.18 = (bf16[768,384]{1,0:T(8,128)(2,1)}, bf16[768,384]{1,0:T(8,128)(2,1)S(1)}, u32[]{:S(2)}) copy-start(bf16[768,384]{1,0:T(8,128)(2,1)S(1)} %collective-permute-done.16.refs_6_) | copy-start | bytes 1769476
  (6 other events, 6.2 us)

commit v3 on v2

--- a/solution.py
+++ b/solution.py
@@ -32,6 +32,8 @@
 SLOT, STRIDE, ORDER = KNEAR, KNEAR + KFAR, BLOCKS
 FAST_FIRST, FAST_LAST, SLOW_FIRST, SLOW_LAST = range(4)
 IN_HBM = pl.BlockSpec(memory_space=pltpu.HBM)
+ANYWHERE = pl.BlockSpec(memory_space=pl.ANY)
+IN_VMEM = pl.BlockSpec(memory_space=pltpu.VMEM)
 
 
 def tm_index(z, x, c):
@@ -72,7 +74,8 @@
     return jnp.concatenate([values, jnp.ones((values.shape[0], HD), jnp.bfloat16)], axis=1)
 
 
-def attend_kernel(table, q_ref, k_ref, v_ref, halo_ref, *rest, chunk, with_far):
+def attend_kernel(table, q_ref, k_ref, v_ref, halo_ref, *rest, chunk, with_far, ordering):
+    rest = rest[ordering:]
     if with_far:
         far_refs, (out_ref, k_vm, v_vm, s_vm, far_vm, sems) = rest[:5], rest[5:]
     else:
@@ -192,7 +195,7 @@
     lax.fori_loop(0, units, body, 0)
 
 
-def attend(table, query, keys, values, halo, far, chunk, chunks):
+def attend(table, query, keys, values, halo, far, chunk, chunks, after=()):
     with_far = far is not None
     spot = lambda i, s: (s[ORDER, chunk + i], 0)
     same = lambda i, s: (i, 0)
@@ -212,11 +215,13 @@
     scratch.append(pltpu.SemaphoreType.DMA((9,)))
     extra = tuple(far) if with_far else ()
     return pl.pallas_call(
-        functools.partial(attend_kernel, chunk=chunk, with_far=with_far),
+        functools.partial(
+            attend_kernel, chunk=chunk, with_far=with_far, ordering=len(after)
+        ),
         grid_spec=pltpu.PrefetchScalarGridSpec(
             num_scalar_prefetch=1,
             grid=(chunks,),
-            in_specs=[pl.BlockSpec((rows, WIDTH), spot)] + [IN_HBM] * (3 + len(extra)),
+            in_specs=[pl.BlockSpec((rows, WIDTH), spot)] + [IN_HBM] * 3 + [ANYWHERE] * len(after + extra),
             out_specs=out_specs,
             scratch_shapes=scratch,
         ),
@@ -227,7 +232,7 @@
             bytes_accessed=8 * 2**20,
             transcendentals=0,
         ),
-    )(table, query, keys, values, halo, *extra)
+    )(table, query, keys, values, halo, *after, *extra)
 
 
 def merge_kernel(table, q_ref, near_ref, level_ref, *rest, chunk):
@@ -296,7 +301,7 @@
             grid=(2,),
             in_specs=[pl.BlockSpec((rows, WIDTH), lambda i, s: (s[ORDER, chunk + i], 0))]
             + [pl.BlockSpec((rows, WIDTH), lambda i, s: (i, 0))] * 2
-            + [IN_HBM] * 6,
+            + [ANYWHERE] * 6,
             out_specs=[IN_HBM] * 2,
             scratch_shapes=[
                 pltpu.VMEM((2, rows, WIDTH), jnp.bfloat16),
@@ -437,7 +442,7 @@
         grid_spec=pltpu.PrefetchScalarGridSpec(
             num_scalar_prefetch=1,
             grid=(parts,),
-            in_specs=[fast, fast, slow, slow, IN_HBM],
+            in_specs=[fast, fast, slow, slow, ANYWHERE],
             out_specs=[pl.BlockSpec((2, rows, WIDTH), lambda i, s: (0, i, 0))] * 2,
         ),
         out_shape=[shape] * 2,
@@ -457,7 +462,7 @@
     return pl.pallas_call(
         pass_kernel,
         grid=(1,),
-        in_specs=[pl.BlockSpec((rows, WIDTH), lambda i: (1, 0))] * NZ + [IN_HBM],
+        in_specs=[pl.BlockSpec((rows, WIDTH), lambda i: (1, 0))] * NZ + [ANYWHERE],
         out_specs=pl.BlockSpec((NZ * rows, WIDTH), lambda i: (0, 0)),
         out_shape=jax.ShapeDtypeStruct((NZ * rows, WIDTH), jnp.bfloat16),
         cost_estimate=pl.CostEstimate(flops=0, bytes_accessed=2 * 2**20, transcendentals=0),
@@ -465,7 +470,7 @@
 
 
 def select_kernel(picks, *refs):
-    sources, outs = refs[:NX], refs[NX:]
+    sources, outs = refs[:NX], refs[NX + 1 :]
     for dz, out in enumerate(outs):
         for dc in range(NC):
             for s in range(NX):
@@ -476,7 +481,7 @@
                     out[to : to + 2 * THIN, :] = sources[s][at, :]
 
 
-def select(picks, sources):
+def select(picks, sources, after):
     shape = jax.ShapeDtypeStruct((NC * NX * CAP * 2 * THIN, WIDTH), jnp.bfloat16)
     whole = lambda a: pl.BlockSpec(a.shape, lambda i, *_: (0, 0))
     return pl.pallas_call(
@@ -484,124 +489,87 @@
         grid_spec=pltpu.PrefetchScalarGridSpec(
             num_scalar_prefetch=1,
             grid=(1,),
-            in_specs=[whole(s) for s in sources],
+            in_specs=[whole(s) for s in sources] + [ANYWHERE],
             out_specs=[whole(shape)] * NZ,
         ),
         out_shape=[shape] * NZ,
         compiler_params=pltpu.CompilerParams(vmem_limit_bytes=VMEM_LIMIT),
         cost_estimate=pl.CostEstimate(flops=0, bytes_accessed=4 * 2**20, transcendentals=0),
-    )(picks, *sources)
-
-
-TILES = 4
-
-
-def project_kernel(scalars, *refs):
-    fast, slow, weight, w_one, w_two, w_swap, out_ref, a_vm, w_vm, sems = (
-        refs[:4],
-        refs[4:8],
-        *refs[8:],
-    )
-    t, h = scalars[0], scalars[1]
-    core = t & 1
-    step = pl.program_id(0)
-    rows, cols = a_vm.shape[0], w_vm.shape[2]
+    )(picks, *sources, after)
+
+
+ROW_TILE = 256
+
+
+def project_kernel(scalars, *refs, wanted_fast, held):
+    parts, (weight, w_one, w_two, w_swap) = refs[:4], refs[4:8]
+    out_ref, out_vm, sems = refs[8 + held :]
+    core, h = scalars[0] & 1, scalars[1]
     gets_fast = (h >> 1) == 1 - core
-
-    def part_copies(refs):
-        return [
-            pltpu.make_async_copy(
-                ref, a_vm.at[:, pl.ds(e * WIDTH, WIDTH)], sems.at[TILES, e]
-            )
-            for e, ref in enumerate(refs)
-        ]
-
-    def weight_copies(tile, direct):
-        per_half = TILES // NC
-        at = pl.ds((tile % per_half) * cols, cols)
-        span = lambda n, count=1: pl.ds(n * WIDTH, count * WIDTH)
-        to = w_vm.at[tile]
-        pairs = [(weight.at[:, pl.ds(tile * cols, cols)], to.at[span(0)])]
-        if direct:
-            pairs += [
-                (w_one.at[:, at], to.at[span(1)]),
-                (w_two.at[span(0), at], to.at[span(3)]),
-                (w_two.at[span(1), at], to.at[span(2)]),
-            ]
-        else:
-            pairs += [
-                (w_swap.at[span(0), at], to.at[span(1)]),
-                (w_swap.at[span(1), at], to.at[span(3)]),
-                (w_swap.at[span(2), at], to.at[span(2)]),
-            ]
-        return [pltpu.make_async_copy(a, b, sems.at[tile, n]) for n, (a, b) in enumerate(pairs)]
-
-    @pl.when(step == 0)
-    def _():
-        @pl.when(gets_fast)
-        def _():
-            for copy in part_copies(fast):
-                copy.start()
-
-        @pl.when(jnp.logical_not(gets_fast))
-        def _():
-            for copy in part_copies(slow):
-                copy.start()
-
-        for tile in range(TILES):
-            half = tile // (TILES // NC)
-            for direct in (True, False):
-
-                @pl.when((core == half) == direct)
-                def _(tile=tile, direct=direct):
-                    for copy in weight_copies(tile, direct):
-                        copy.start()
-
-        for copy in part_copies(fast):
-            copy.wait()
-
-    for tile in range(TILES):
-
-        @pl.when(step == tile)
-        def _(tile=tile):
-            for copy in weight_copies(tile, True):
-                copy.wait()
-
-    out_ref[...] = jnp.dot(
-        a_vm[...], w_vm[step], preferred_element_type=jnp.float32
-    ).astype(jnp.bfloat16)
-
-
-def project(scalars, fast, slow, weight, w_one, w_two, w_swap):
-    anywhere = IN_HBM
-    rows, width = CHUNK * BLK, weight.shape[1]
-    depth = NHEAD * WIDTH
-    inputs = (*fast, *slow, weight, w_one, w_two, w_swap)
+    tiles = out_vm.shape[0] // ROW_TILE
+    width = out_vm.shape[1] // NC
+
+    def copy_of(i):
+        rows = pl.ds(pl.multiple_of(i * ROW_TILE, ROW_TILE), ROW_TILE)
+        return pltpu.make_async_copy(out_vm.at[rows], out_ref.at[rows], sems.at[i])
+
+    def group(n):
+        return pl.ds(n * WIDTH, WIDTH)
+
+    for mine in range(NC):
+
+        @pl.when((core == mine) & (gets_fast == wanted_fast))
+        def _(mine=mine):
+            def step(i, _):
+                rows = pl.ds(pl.multiple_of(i * ROW_TILE, ROW_TILE), ROW_TILE)
+                attended = jnp.concatenate([part[rows, :] for part in parts], axis=1)
+                for half in range(NC):
+                    cols = pl.ds(half * width, width)
+                    if half == mine:
+                        others = w_one[...], w_two[group(1), :], w_two[group(0), :]
+                    else:
+                        others = w_swap[group(0), :], w_swap[group(2), :], w_swap[group(1), :]
+                    out_vm[rows, cols] = jnp.dot(
+                        attended,
+                        jnp.concatenate([weight[:, cols], *others], axis=0),
+                        preferred_element_type=jnp.float32,
+                    ).astype(jnp.bfloat16)
+                copy_of(i).start()
+                return 0
+
+            lax.fori_loop(0, tiles, step, 0)
+            for i in range(tiles):
+                copy_of(i).wait()
+
+
+def project(scalars, parts, weights, wanted_fast, held=None):
+    rows, width = CHUNK * BLK, weights[0].shape[1]
+    inputs = (*parts, *weights)
+    extra = () if held is None else (held,)
     return pl.pallas_call(
-        project_kernel,
+        functools.partial(project_kernel, wanted_fast=wanted_fast, held=len(extra)),
         grid_spec=pltpu.PrefetchScalarGridSpec(
             num_scalar_prefetch=1,
-            grid=(TILES,),
-            in_specs=[anywhere] * len(inputs),
-            out_specs=pl.BlockSpec((rows, width // TILES), lambda i, s: (0, i)),
+            grid=(1,),
+            in_specs=[IN_VMEM] * len(inputs) + [IN_HBM] * len(extra),
+            out_specs=IN_HBM,
             scratch_shapes=[
-                pltpu.VMEM((rows, depth), jnp.bfloat16),
-                pltpu.VMEM((TILES, depth, width // TILES), jnp.bfloat16),
-                pltpu.SemaphoreType.DMA((TILES + 1, NHEAD)),
+                pltpu.VMEM((rows, width), jnp.bfloat16),
+                pltpu.SemaphoreType.DMA((rows // ROW_TILE,)),
             ],
         ),
         out_shape=jax.ShapeDtypeStruct((rows, width), jnp.bfloat16),
-        compiler_params=pltpu.CompilerParams(vmem_limit_bytes=VMEM_LIMIT),
+        input_output_aliases={} if held is None else {1 + len(inputs): 0},
+        compiler_params=pltpu.CompilerParams(vmem_limit_bytes=24 * 2**20),
         cost_estimate=pl.CostEstimate(
-            flops=2 * rows * depth * width, bytes_accessed=10 * 2**20, transcendentals=0
-        ),
-    )(scalars, *inputs)
+            flops=2 * rows * NHEAD * WIDTH * width, bytes_accessed=10 * 2**20, transcendentals=0
+        ),
+    )(scalars, *inputs, *extra)
 
 
 def per_device(query, keys, values, out_weight, near_list, far_list, stride_table):
     t = lax.axis_index("tm")
     h = lax.axis_index("head")
-    core = t % NC
     coords = [(zz, xx, cc) for zz in range(NZ) for xx in range(NX) for cc in range(NC)]
     swap = [(i, i ^ 1) for i in range(NTM)]
     across = [(i, i + 1) for i in range(1, NTM - 1, 2)]
@@ -621,30 +589,33 @@
 
     fast_part, slow_part = pack_halos(place, keys, values, thinned)
     halo_fast = lax.ppermute(fast_part, "tm", swap)
+    picks, table = index_work(place, stride_table, far_list, near_list)
+    slow_part, table, *along_x = lax.optimization_barrier((slow_part, table, *along_x))
     halo_slow = lax.ppermute(slow_part, "tm", across)
 
-    cols = out_weight.shape[1] // NC
-    half = lax.dynamic_slice_in_dim(out_weight, core * cols, cols, 1)
-    half, *along_x = lax.optimization_barrier((half, *along_x))
-    w_one = lax.ppermute(half, "head", [(g, g ^ 1) for g in range(NHEAD)])
-
-    picks, table = index_work(place, stride_table, far_list, near_list)
-
-    packs = select(picks, [thinned] + along_x)
+    near_fast = attend(table, query, keys, values, halo_fast, None, FAST_FIRST, 2)
+    packs = select(picks, [thinned] + along_x, near_fast[1])
     arrived = [packs[0]]
     for d in range(1, NZ):
         pairs = [(tm_index(*p), tm_index(p[0] + d, p[1], p[2])) for p in coords]
         arrived.append(lax.ppermute(packs[d], "tm", pairs))
+
+    cols = out_weight.shape[1] // NC
+    half = lax.dynamic_slice_in_dim(out_weight, (t % NC) * cols, cols, 1)
+    half, _ = lax.optimization_barrier((half, table))
+    w_one = lax.ppermute(half, "head", [(g, g ^ 1) for g in range(NHEAD)])
+    half, w_one, _ = lax.optimization_barrier((half, w_one, packs[0]))
     w_two = lax.ppermute(
         jnp.concatenate([half, w_one], axis=0), "head", [(g, g ^ 3) for g in range(NHEAD)]
     )
-    near_fast = attend(table, query, keys, values, halo_fast, None, FAST_FIRST, 2)
-    halo_slow, near_fast = lax.optimization_barrier((halo_slow, near_fast))
-    near_slow = attend(table, query, keys, values, halo_slow, None, SLOW_FIRST, 2)
+
+    near_slow = attend(
+        table, query, keys, values, halo_slow, None, SLOW_FIRST, 2, (packs[0],)
+    )
     passed = lax.ppermute(pack_passed(arrived, near_slow[1]), "tm", swap)
     far = [*arrived, passed]
     w_swap = lax.ppermute(jnp.concatenate([w_one, w_two], axis=0), "tm", swap)
-    first_fast, last_fast = merge_far(table, query, near_fast, far, FAST_FIRST, w_two)
+    first_fast, last_fast = merge_far(table, query, near_fast, far, FAST_FIRST, near_slow[1])
     near_slow, first_fast = lax.optimization_barrier((near_slow, first_fast))
     first_slow, last_slow = merge_far(table, query, near_slow, far, SLOW_FIRST, w_swap)
 
@@ -657,13 +628,17 @@
                     pairs.append((i * NHEAD + g, i * NHEAD + (g ^ e)))
         return lax.ppermute(chunk, ("tm", "head"), pairs)
 
-    fast = [last_fast, *(exchange(first_fast, e, True) for e in (1, 2)), exchange(last_fast, 3, True)]
-    slow = [
-        last_slow,
-        *(exchange(first_slow, e, False) for e in (1, 2)),
-        exchange(last_slow, 3, False),
-    ]
-    return project(place, fast, slow, out_weight, w_one, w_two, w_swap)
+    def received(first, last, fast):
+        two, one, three = [
+            exchange(chunk, e, fast) for e, chunk in ((2, first), (1, first), (3, last))
+        ]
+        return last, one, two, three
+
+    weights = (out_weight, w_one, w_two, w_swap)
+    fast = received(first_fast, last_fast, True)
+    slow = received(first_slow, last_slow, False)
+    held = project(place, fast, weights, True)
+    return project(place, slow, weights, False, held)
 
 
 def solution(mesh):

time: 156 us -> 152 us (0.974)
  waiting for transfers between devices: 31.2 us -> 28 us
  Pallas kernels: 79.7 us -> 76.7 us
    ppermute x3, waiting for transfers between devices: 10.6 us -> 7.19 us  [per_device(): lax.ppermute(thinned, 'tm', [(tm_index(*p), tm_index(p[0], p[1] + d, p[2]...]
    pallas_call x1 -> x2, Pallas kernels: 9.25 us -> 6.26 us  [project(): pl.pallas_call(functools.partial(project_kernel, wanted_fast=wanted_fast,...]
    ppermute x3, waiting for transfers between devices: 0.01 us -> 2.82 us  [per_device(): arrived.append(lax.ppermute(packs[d], 'tm', pairs))]
    ppermute x6, starting transfers between devices: 11.7 us -> 14.4 us  [exchange(): return lax.ppermute(chunk, ('tm', 'head'), pairs)]
    ppermute x6, waiting for transfers between devices: 18.3 us -> 16.2 us  [exchange(): return lax.ppermute(chunk, ('tm', 'head'), pairs)]
    unnamed x42 -> x30, local copies, waits for them, and re-layouts: 5.91 us -> 5.4 us
  transfers between devices with their start and end apart: 18 -> 18, of which waited for: 6 -> 6; matrix products, arithmetic and copies ran while one was open for 2% -> 3% of each run, Pallas kernels for 42% -> 43%
where the time goes in v3:
time: 152 us; the launch traced here: 151 us
  Pallas kernels  76.7 us (50%)
  starting transfers between devices  33.9 us (22%)
  waiting for transfers between devices  28 us (18%)
  local copies, waits for them, and re-layouts  8.34 us (5%)
  other arithmetic  3.77 us (2%)
    pallas_call x2, Pallas kernels, attend(): pl.pallas_call(functools.partial(attend_kernel, chunk=chunk, with_far=wit...  39.6 us
    ppermute x6, waiting for transfers between devices, exchange(): return lax.ppermute(chunk, ('tm', 'head'), pairs)  16.2 us
    pallas_call x2, Pallas kernels, merge_far(): pl.pallas_call(functools.partial(merge_kernel, chunk=chunk), grid_spec=pl...  15.1 us
    ppermute x6, starting transfers between devices, exchange(): return lax.ppermute(chunk, ('tm', 'head'), pairs)  14.4 us
    ppermute x3, starting transfers between devices, per_device(): arrived.append(lax.ppermute(packs[d], 'tm', pairs))  7.76 us
    ppermute x3, waiting for transfers between devices, per_device(): lax.ppermute(thinned, 'tm', [(tm_index(*p), tm_index(p[0], p[1] + d, p[2]...  7.19 us
    pallas_call x2, Pallas kernels, project(): pl.pallas_call(functools.partial(project_kernel, wanted_fast=wanted_fast,...  6.26 us
    pallas_call x1, Pallas kernels, pack_halos(): pl.pallas_call(halo_kernel, grid_spec=pltpu.PrefetchScalarGridSpec(num_sc...  5.84 us
  transfers between devices with their start and end apart: 18, of which 6 were waited for; matrix products, arithmetic and copies ran while one was open for 3% of the time, Pallas kernels for 43%

profile of v3, /device:TPU:0, one launch (start us, length us, event | category | flops | bytes accessed | tf_op | source)
XLA Modules:
  0.0 151.1 jit_solution(1579425369232639873)
XLA Ops:
  0.0 1.4 slice.9
  1.4 1.4 slice.8
  4.3 5.8 %shard_map.73 = (bf16[2,1536,384]{2,1,0:T(8,128)(2,1)}, bf16[2,1536,384]{2,1,0:T(8,128)(2,1)}) custom-call(s32[2]{0:T(128)} %pad_add_fusion.scalars, bf16[3072,384]{1,0:T(8,128)(2,1)} %k_ref.3, bf16[3072,384]{1,0:T(8,128)(2,1)} %v_ref.3, bf16[3072,384]{1,0:T(8,128)(2,1)} %k_ref.3, bf16[3072,384]{1,0:T(8,128)(2,1)} %v_ref.3, bf16[384,384]{1,0:T(8,128)(2,1)} %bitcast.13), custom_call_target="tpu_custom_call" | custom-call | bytes 10485760 | tf_op jit(solution)/shard_map/pallas_call | solution.py:440
  10.1 1.6 %collective-permute-start = (bf16[384,384]{1,0:T(8,128)(2,1)S(1)}, bf16[384,384]{1,0:T(8,128)(2,1)S(1)}, u32[]{:S(2)}, u32[]{:S(2)}) collective-permute-start(bf16[384,384]{1,0:T(8,128)(2,1)S(1)} %bitcast.15), channel_id=1, source_target_pairs={{0,8},{4,12},{8,16},{12,20},{16,24},{20,28},{24,0},{28,4},{32,40},... | collective-permute-start | bytes 884744 | tf_op jit(solution)/shard_map/ppermute | solution.py:584
  11.8 2.7 %collective-permute-start.1 = (bf16[384,384]{1,0:T(8,128)(2,1)S(1)}, bf16[384,384]{1,0:T(8,128)(2,1)S(1)}, u32[]{:S(2)}, u32[]{:S(2)}) collective-permute-start(bf16[384,384]{1,0:T(8,128)(2,1)S(1)} %bitcast.16), channel_id=1, source_target_pairs={{0,16},{4,20},{8,24},{12,28},{16,0},{20,4},{24,8},{28,12},{32,48},... | collective-permute-start | bytes 884744 | tf_op jit(solution)/shard_map/ppermute | solution.py:584
  14.5 1.4 collective-permute-start.2
  17.5 3.4 %shard_map.74 = (s32[48,128]{1,0:T(8,128)}, s32[32,128]{1,0:T(8,128)}) custom-call(s32[2]{0:T(128)} %pad_add_fusion.scalars, s32[64]{0:T(128)} %steps.1, s32[768,16]{1,0:T(8,128)} %copy.11.far_ref, s32[24,16]{1,0:T(8,128)} %copy.12.near_ref), custom_call_target="tpu_custom_call" | custom-call | flops 1048576 | bytes 4194304 | tf_op jit(solution)/shard_map/pallas_call | solution.py:414
  21.0 7.2 %collective-permute-done.1.refs_2_ = bf16[384,384]{1,0:T(8,128)(2,1)S(1)} collective-permute-done((bf16[384,384]{1,0:T(8,128)(2,1)S(1)}, bf16[384,384]{1,0:T(8,128)(2,1)S(1)}, u32[]{:S(2)}, u32[]{:S(2)}) %collective-permute-start.1) | collective-permute-done | bytes 294944 | tf_op jit(solution)/shard_map/ppermute | solution.py:584
  28.2 2.1 %collective-permute-start.3 = (bf16[3072,384]{1,0:T(8,128)(2,1)}, bf16[3072,384]{1,0:T(8,128)(2,1)}, u32[]{:S(2)}, u32[]{:S(2)}) collective-permute-start(bf16[3072,384]{1,0:T(8,128)(2,1)} %bitcast.18), channel_id=1, source_target_pairs={{4,8},{12,16},{20,24},{28,32},{36,40},{44,48},{52,56},{60,64},{68,... | collective-permute-start | bytes 7077896 | tf_op jit(solution)/shard_map/ppermute | solution.py:594
  30.3 1.7 %collective-permute-start.9 = (bf16[384,768]{1,0:T(8,128)(2,1)S(1)}, bf16[384,768]{1,0:T(8,128)(2,1)S(1)}, u32[]{:S(2)}, u32[]{:S(2)}) collective-permute-start(bf16[384,768]{1,0:T(8,128)(2,1)S(1)} %constant_dynamic-slice_fusion), channel_id=1, source_target_pairs={{0,1},{1,0},{2,3},{3,2},{4,5},{5,4},{6,7},{7,6},{8,9},{9,8},{10,11... | collective-permute-start | bytes 1769480 | tf_op jit(solution)/shard_map/ppermute | solution.py:606
  32.0 19.8 %shard_map.75 = (bf16[1536,384]{1,0:T(8,128)(2,1)}, f32[1536,384]{1,0:T(8,128)}) custom-call(s32[32,128]{1,0:T(8,128)} %get-tuple-element.34.table, bf16[3072,384]{1,0:T(8,128)(2,1)} %q_ref.7, bf16[3072,384]{1,0:T(8,128)(2,1)} %k_ref.3, bf16[3072,384]{1,0:T(8,128)(2,1)} %v_ref.3, bf16[3072,384]{1,0:T(8,128)(2,1)} %collective-permute-done.4.halo_ref), custom_call_target="tpu_custom_call" | custom-call | flops 15401484288 | bytes 8388608 | tf_op jit(solution)/shard_map/pallas_call | solution.py:217
  51.8 4.0 %shard_map.76 = (bf16[768,384]{1,0:T(8,128)(2,1)}, bf16[768,384]{1,0:T(8,128)(2,1)}, bf16[768,384]{1,0:T(8,128)(2,1)}, bf16[768,384]{1,0:T(8,128)(2,1)}) custom-call(s32[48,128]{1,0:T(8,128)} %get-tuple-element.36.picks, bf16[384,384]{1,0:T(8,128)(2,1)} %bitcast.14, bf16[384,384]{1,0:T(8,128)(2,1)} %copy-done.9, bf16[384,384]{1,0:T(8,128)(2,1)} %copy-done.10, ...), custom_call_target="tpu_custom_call" | custom-call | bytes 4194304 | tf_op jit(solution)/shard_map/pallas_call | solution.py:487
  55.8 3.2 %collective-permute-start.5 = (bf16[768,384]{1,0:T(8,128)(2,1)}, bf16[768,384]{1,0:T(8,128)(2,1)S(1)}, u32[]{:S(2)}, u32[]{:S(2)}) collective-permute-start(bf16[768,384]{1,0:T(8,128)(2,1)} %get-tuple-element.46), channel_id=1, source_target_pairs={{0,32},{4,36},{8,40},{12,44},{16,48},{20,52},{24,56},{28,60},{32,6... | collective-permute-start | bytes 1769480 | tf_op jit(solution)/shard_map/ppermute | solution.py:601
  59.0 3.9 %collective-permute-start.6 = (bf16[768,384]{1,0:T(8,128)(2,1)}, bf16[768,384]{1,0:T(8,128)(2,1)}, u32[]{:S(2)}, u32[]{:S(2)}) collective-permute-start(bf16[768,384]{1,0:T(8,128)(2,1)} %get-tuple-element.47), channel_id=1, source_target_pairs={{0,64},{4,68},{8,72},{12,76},{16,80},{20,84},{24,88},{28,92},{32,9... | collective-permute-start | bytes 1769480 | tf_op jit(solution)/shard_map/ppermute | solution.py:601
  64.7 2.2 %collective-permute-start.10 = (bf16[768,768]{1,0:T(8,128)(2,1)}, bf16[768,768]{1,0:T(8,128)(2,1)S(1)}, u32[]{:S(2)}, u32[]{:S(2)}) collective-permute-start(bf16[768,768]{1,0:T(8,128)(2,1)} %pad_maximum_fusion.1), channel_id=1, source_target_pairs={{0,3},{1,2},{2,1},{3,0},{4,7},{5,6},{6,5},{7,4},{8,11},{9,10},{10,... | collective-permute-start | bytes 3538952 | tf_op jit(solution)/shard_map/ppermute | solution.py:608
  66.9 19.8 %shard_map.77 = (bf16[1536,384]{1,0:T(8,128)(2,1)}, f32[1536,384]{1,0:T(8,128)}) custom-call(s32[32,128]{1,0:T(8,128)} %get-tuple-element.34.table, bf16[3072,384]{1,0:T(8,128)(2,1)} %q_ref.7, bf16[3072,384]{1,0:T(8,128)(2,1)} %k_ref.3, bf16[3072,384]{1,0:T(8,128)(2,1)} %v_ref.3, bf16[3072,384]{1,0:T(8,128)(2,1)} %collective-permute-done.3.halo_ref, ...), custom_call_target="tpu_custom_call" | custom-call | flops 15401484288 | bytes 8388608 | tf_op jit(solution)/shard_map/pallas_call | solution.py:217
  86.7 2.8 %collective-permute-done.6.c.rest_2_ = bf16[768,384]{1,0:T(8,128)(2,1)} collective-permute-done((bf16[768,384]{1,0:T(8,128)(2,1)}, bf16[768,384]{1,0:T(8,128)(2,1)}, u32[]{:S(2)}, u32[]{:S(2)}) %collective-permute-start.6) | collective-permute-done | bytes 589856 | tf_op jit(solution)/shard_map/ppermute | solution.py:601
  89.5 2.5 %shard_map.78 = bf16[1536,384]{1,0:T(8,128)(2,1)} custom-call(bf16[768,384]{1,0:T(8,128)(2,1)} %get-tuple-element.42.rest_0_.a, bf16[768,384]{1,0:T(8,128)(2,1)} %copy-done.6, bf16[768,384]{1,0:T(8,128)(2,1)} %collective-permute-done.6.c.rest_2_, bf16[768,384]{1,0:T(8,128)(2,1)} %collective-permute-done.7.d.rest_3_, ...), custom_call_target="tpu_custom_call" | custom-call | bytes 2097152 | tf_op jit(solution)/shard_map/pallas_call | solution.py:462
  92.9 1.3 pad_maximum_fusion
  95.0 1.1 copy-done.7
  96.1 7.6 %shard_map.79 = (bf16[768,384]{1,0:T(8,128)(2,1)}, bf16[768,384]{1,0:T(8,128)(2,1)}) custom-call(s32[32,128]{1,0:T(8,128)} %get-tuple-element.34.table, bf16[3072,384]{1,0:T(8,128)(2,1)} %q_ref.7, bf16[1536,384]{1,0:T(8,128)(2,1)} %get-tuple-element.45.near_ref, f32[1536,384]{1,0:T(8,128)} %get-tuple-element.41.refs_4_.level_ref, ...), custom_call_target="tpu_custom_call" | custom-call | flops 1811939328 | bytes 8388608 | tf_op jit(solution)/shard_map/pallas_call | solution.py:297
  104.4 7.6 %collective-permute-start.16 = (bf16[768,384]{1,0:T(8,128)(2,1)}, bf16[768,384]{1,0:T(8,128)(2,1)S(1)}, u32[]{:S(2)}, u32[]{:S(2)}) collective-permute-start(bf16[768,384]{1,0:T(8,128)(2,1)} %get-tuple-element.58), channel_id=1, source_target_pairs={{0,2},{1,3},{6,4},{7,5},{8,10},{9,11},{14,12},{15,13},{16,18},{17,... | collective-permute-start | bytes 1769480 | tf_op jit(solution)/shard_map/ppermute | solution.py:629
  112.0 1.5 collective-permute-start.17
  113.5 1.2 copy-done
  114.7 7.6 %shard_map.80 = (bf16[768,384]{1,0:T(8,128)(2,1)}, bf16[768,384]{1,0:T(8,128)(2,1)}) custom-call(s32[32,128]{1,0:T(8,128)} %get-tuple-element.34.table, bf16[3072,384]{1,0:T(8,128)(2,1)} %q_ref.7, bf16[1536,384]{1,0:T(8,128)(2,1)} %get-tuple-element.50.near_ref, f32[1536,384]{1,0:T(8,128)} %get-tuple-element.51.after.rest_5_.level_ref, ...), custom_call_target="tpu_custom_call" | custom-call | flops 1811939328 | bytes 8388608 | tf_op jit(solution)/shard_map/pallas_call | solution.py:297
  122.3 2.0 %collective-permute-start.12 = (bf16[768,384]{1,0:T(8,128)(2,1)}, bf16[768,384]{1,0:T(8,128)(2,1)S(1)}, u32[]{:S(2)}, u32[]{:S(2)}) collective-permute-start(bf16[768,384]{1,0:T(8,128)(2,1)} %get-tuple-element.56), channel_id=1, source_target_pairs={{0,1},{1,0},{6,7},{7,6},{8,9},{9,8},{14,15},{15,14},{16,17},{17,16... | collective-permute-start | bytes 1769480 | tf_op jit(solution)/shard_map/ppermute | solution.py:629
  124.4 1.3 collective-permute-start.13
  125.7 1.3 collective-permute-start.14
  127.0 1.5 copy-done.1
  129.1 11.3 %collective-permute-done.12.refs_1_ = bf16[768,384]{1,0:T(8,128)(2,1)S(1)} collective-permute-done((bf16[768,384]{1,0:T(8,128)(2,1)}, bf16[768,384]{1,0:T(8,128)(2,1)S(1)}, u32[]{:S(2)}, u32[]{:S(2)}) %collective-permute-start.12) | collective-permute-done | bytes 589856 | tf_op jit(solution)/shard_map/ppermute | solution.py:629
  140.3 4.9 %collective-permute-done.14.refs_3_ = bf16[768,384]{1,0:T(8,128)(2,1)S(1)} collective-permute-done((bf16[768,384]{1,0:T(8,128)(2,1)}, bf16[768,384]{1,0:T(8,128)(2,1)S(1)}, u32[]{:S(2)}, u32[]{:S(2)}) %collective-permute-start.14) | collective-permute-done | bytes 589856 | tf_op jit(solution)/shard_map/ppermute | solution.py:629
  145.3 5.7 %shard_map.82 = bf16[768,1536]{1,0:T(8,128)(2,1)} custom-call(s32[2]{0:T(128)S(1)} %copy-done.3, bf16[768,384]{1,0:T(8,128)(2,1)S(1)} %copy-done.5, bf16[768,384]{1,0:T(8,128)(2,1)S(1)} %collective-permute-done.12.refs_1_, bf16[768,384]{1,0:T(8,128)(2,1)S(1)} %collective-permute-done.13.refs_2_, ...), custom_call_target="tpu_custom_call", output_to_operand_aliasing={{}: (9, {})} | custom-call | flops 3623878656 | bytes 10485760 | tf_op jit(solution)/shard_map/pallas_call | solution.py:549
  (52 shorter events, 7.9 us)
Async XLA Ops:
  4.3 5.9 %copy-start.8 = (bf16[24,16,384]{2,1,0:T(8,128)(2,1)S(1)}, bf16[24,16,384]{2,1,0:T(8,128)(2,1)}, u32[]{:S(2)}) copy-start(bf16[24,16,384]{2,1,0:T(8,128)(2,1)} %pad_maximum_fusion.2) | copy-start | bytes 884740
  4.3 11.7 %copy-start.12 = (s32[768,16]{0,1:T(8,128)S(1)}, s32[768,16]{0,1:T(8,128)}, u32[]{:S(2)}) copy-start(s32[768,16]{0,1:T(8,128)} %param.12) | copy-start | bytes 147460
  4.3 12.6 %copy-start.13 = (s32[24,16]{0,1:T(8,128)S(1)}, s32[24,16]{0,1:T(8,128)}, u32[]{:S(2)}) copy-start(s32[24,16]{0,1:T(8,128)} %param.11) | copy-start | bytes 4612
  4.3 26.0 %copy-start.2 = (bf16[384,1536]{1,0:T(8,128)(2,1)S(1)}, bf16[384,1536]{1,0:T(8,128)(2,1)}, u32[]{:S(2)}) copy-start(bf16[384,1536]{1,0:T(8,128)(2,1)} %refs_4_.3) | copy-start | bytes 3538948
  10.1 21.9 %collective-permute-start.4 = (bf16[3072,384]{1,0:T(8,128)(2,1)}, bf16[3072,384]{1,0:T(8,128)(2,1)}, u32[]{:S(2)}, u32[]{:S(2)}) collective-permute-start(bf16[3072,384]{1,0:T(8,128)(2,1)} %bitcast.19), channel_id=1, source_target_pairs={{0,4},{4,0},{8,12},{12,8},{16,20},{20,16},{24,28},{28,24},{32,36},... | collective-permute-start | bytes 7077896 | tf_op jit(solution)/shard_map/ppermute | solution.py:591
  10.1 10.8 %collective-permute-start = (bf16[384,384]{1,0:T(8,128)(2,1)S(1)}, bf16[384,384]{1,0:T(8,128)(2,1)S(1)}, u32[]{:S(2)}, u32[]{:S(2)}) collective-permute-start(bf16[384,384]{1,0:T(8,128)(2,1)S(1)} %bitcast.15), channel_id=1, source_target_pairs={{0,8},{4,12},{8,16},{12,20},{16,24},{20,28},{24,0},{28,4},{32,40},... | collective-permute-start | bytes 884744 | tf_op jit(solution)/shard_map/ppermute | solution.py:584
  11.8 16.4 %collective-permute-start.1 = (bf16[384,384]{1,0:T(8,128)(2,1)S(1)}, bf16[384,384]{1,0:T(8,128)(2,1)S(1)}, u32[]{:S(2)}, u32[]{:S(2)}) collective-permute-start(bf16[384,384]{1,0:T(8,128)(2,1)S(1)} %bitcast.16), channel_id=1, source_target_pairs={{0,16},{4,20},{8,24},{12,28},{16,0},{20,4},{24,8},{28,12},{32,48},... | collective-permute-start | bytes 884744 | tf_op jit(solution)/shard_map/ppermute | solution.py:584
  14.5 13.6 %collective-permute-start.2 = (bf16[384,384]{1,0:T(8,128)(2,1)S(1)}, bf16[384,384]{1,0:T(8,128)(2,1)S(1)}, u32[]{:S(2)}, u32[]{:S(2)}) collective-permute-start(bf16[384,384]{1,0:T(8,128)(2,1)S(1)} %bitcast.17), channel_id=1, source_target_pairs={{0,24},{4,28},{8,0},{12,4},{16,8},{20,12},{24,16},{28,20},{32,56},... | collective-permute-start | bytes 884744 | tf_op jit(solution)/shard_map/ppermute | solution.py:584
  21.0 30.9 %copy-start.9 = (bf16[384,384]{1,0:T(8,128)(2,1)}, bf16[384,384]{1,0:T(8,128)(2,1)S(1)}, u32[]{:S(2)}) copy-start(bf16[384,384]{1,0:T(8,128)(2,1)S(1)} %collective-permute-done.refs_1_) | copy-start | bytes 884740
  28.1 23.7 %copy-start.10 = (bf16[384,384]{1,0:T(8,128)(2,1)}, bf16[384,384]{1,0:T(8,128)(2,1)S(1)}, u32[]{:S(2)}) copy-start(bf16[384,384]{1,0:T(8,128)(2,1)S(1)} %collective-permute-done.1.refs_2_) | copy-start | bytes 884740
  28.2 23.7 %copy-start.11 = (bf16[384,384]{1,0:T(8,128)(2,1)}, bf16[384,384]{1,0:T(8,128)(2,1)S(1)}, u32[]{:S(2)}) copy-start(bf16[384,384]{1,0:T(8,128)(2,1)S(1)} %collective-permute-done.2.refs_3_) | copy-start | bytes 884740
  28.2 38.7 %collective-permute-start.3 = (bf16[3072,384]{1,0:T(8,128)(2,1)}, bf16[3072,384]{1,0:T(8,128)(2,1)}, u32[]{:S(2)}, u32[]{:S(2)}) collective-permute-start(bf16[3072,384]{1,0:T(8,128)(2,1)} %bitcast.18), channel_id=1, source_target_pairs={{4,8},{12,16},{20,24},{28,32},{36,40},{44,48},{52,56},{60,64},{68,... | collective-permute-start | bytes 7077896 | tf_op jit(solution)/shard_map/ppermute | solution.py:594
  30.3 33.3 %collective-permute-start.9 = (bf16[384,768]{1,0:T(8,128)(2,1)S(1)}, bf16[384,768]{1,0:T(8,128)(2,1)S(1)}, u32[]{:S(2)}, u32[]{:S(2)}) collective-permute-start(bf16[384,768]{1,0:T(8,128)(2,1)S(1)} %constant_dynamic-slice_fusion), channel_id=1, source_target_pairs={{0,1},{1,0},{2,3},{3,2},{4,5},{5,4},{6,7},{7,6},{8,9},{9,8},{10,11... | collective-permute-start | bytes 1769480 | tf_op jit(solution)/shard_map/ppermute | solution.py:606
  55.8 30.8 %collective-permute-start.5 = (bf16[768,384]{1,0:T(8,128)(2,1)}, bf16[768,384]{1,0:T(8,128)(2,1)S(1)}, u32[]{:S(2)}, u32[]{:S(2)}) collective-permute-start(bf16[768,384]{1,0:T(8,128)(2,1)} %get-tuple-element.46), channel_id=1, source_target_pairs={{0,32},{4,36},{8,40},{12,44},{16,48},{20,52},{24,56},{28,60},{32,6... | collective-permute-start | bytes 1769480 | tf_op jit(solution)/shard_map/ppermute | solution.py:601
  59.0 30.5 %collective-permute-start.6 = (bf16[768,384]{1,0:T(8,128)(2,1)}, bf16[768,384]{1,0:T(8,128)(2,1)}, u32[]{:S(2)}, u32[]{:S(2)}) collective-permute-start(bf16[768,384]{1,0:T(8,128)(2,1)} %get-tuple-element.47), channel_id=1, source_target_pairs={{0,64},{4,68},{8,72},{12,76},{16,80},{20,84},{24,88},{28,92},{32,9... | collective-permute-start | bytes 1769480 | tf_op jit(solution)/shard_map/ppermute | solution.py:601
  62.9 26.6 %collective-permute-start.7 = (bf16[768,384]{1,0:T(8,128)(2,1)}, bf16[768,384]{1,0:T(8,128)(2,1)}, u32[]{:S(2)}, u32[]{:S(2)}) collective-permute-start(bf16[768,384]{1,0:T(8,128)(2,1)} %get-tuple-element.48), channel_id=1, source_target_pairs={{0,96},{4,100},{8,104},{12,108},{16,112},{20,116},{24,120},{28,124... | collective-permute-start | bytes 1769480 | tf_op jit(solution)/shard_map/ppermute | solution.py:601
  64.7 28.2 %collective-permute-start.10 = (bf16[768,768]{1,0:T(8,128)(2,1)}, bf16[768,768]{1,0:T(8,128)(2,1)S(1)}, u32[]{:S(2)}, u32[]{:S(2)}) collective-permute-start(bf16[768,768]{1,0:T(8,128)(2,1)} %pad_maximum_fusion.1), channel_id=1, source_target_pairs={{0,3},{1,2},{2,1},{3,0},{4,7},{5,6},{6,5},{7,4},{8,11},{9,10},{10,... | collective-permute-start | bytes 3538952 | tf_op jit(solution)/shard_map/ppermute | solution.py:608
  86.7 2.8 %copy-start.6 = (bf16[768,384]{1,0:T(8,128)(2,1)}, bf16[768,384]{1,0:T(8,128)(2,1)S(1)}, u32[]{:S(2)}) copy-start(bf16[768,384]{1,0:T(8,128)(2,1)S(1)} %collective-permute-done.5.b.rest_1_) | copy-start | bytes 1769476
  91.9 3.1 %collective-permute-start.8 = (bf16[1536,384]{1,0:T(8,128)(2,1)}, bf16[1536,384]{1,0:T(8,128)(2,1)S(1)}, u32[]{:S(2)}, u32[]{:S(2)}) collective-permute-start(bf16[1536,384]{1,0:T(8,128)(2,1)} %shard_map.78), channel_id=1, source_target_pairs={{0,4},{4,0},{8,12},{12,8},{16,20},{20,16},{24,28},{28,24},{32,36},... | collective-permute-start | bytes 3538952 | tf_op jit(solution)/shard_map/ppermute | solution.py:615
  94.2 19.3 %collective-permute-start.11 = (bf16[1152,768]{1,0:T(8,128)(2,1)}, bf16[1152,768]{1,0:T(8,128)(2,1)S(1)}, u32[]{:S(2)}, u32[]{:S(2)}) collective-permute-start(bf16[1152,768]{1,0:T(8,128)(2,1)} %pad_maximum_fusion), channel_id=1, source_target_pairs={{0,4},{4,0},{8,12},{12,8},{16,20},{20,16},{24,28},{28,24},{32,36},... | collective-permute-start | bytes 5308424 | tf_op jit(solution)/shard_map/ppermute | solution.py:617
  95.0 1.1 copy-start.7
  103.7 22.0 %collective-permute-start.15 = (bf16[768,384]{1,0:T(8,128)(2,1)}, bf16[768,384]{1,0:T(8,128)(2,1)S(1)}, u32[]{:S(2)}, u32[]{:S(2)}) collective-permute-start(bf16[768,384]{1,0:T(8,128)(2,1)} %get-tuple-element.58), channel_id=1, source_target_pairs={{2,3},{3,2},{4,5},{5,4},{10,11},{11,10},{12,13},{13,12},{18,19},{1... | collective-permute-start | bytes 1769480 | tf_op jit(solution)/shard_map/ppermute | solution.py:629
  104.4 22.6 %collective-permute-start.16 = (bf16[768,384]{1,0:T(8,128)(2,1)}, bf16[768,384]{1,0:T(8,128)(2,1)S(1)}, u32[]{:S(2)}, u32[]{:S(2)}) collective-permute-start(bf16[768,384]{1,0:T(8,128)(2,1)} %get-tuple-element.58), channel_id=1, source_target_pairs={{0,2},{1,3},{6,4},{7,5},{8,10},{9,11},{14,12},{15,13},{16,18},{17,... | collective-permute-start | bytes 1769480 | tf_op jit(solution)/shard_map/ppermute | solution.py:629
  112.0 15.0 %copy-start.3 = (s32[2]{0:T(128)S(1)}, s32[2]{0:T(128)}, u32[]{:S(2)}) copy-start(s32[2]{0:T(128)} %pad_add_fusion.scalars) | copy-start | bytes 28
  112.0 15.0 %copy-start.4 = (bf16[768,384]{1,0:T(8,128)(2,1)S(1)}, bf16[768,384]{1,0:T(8,128)(2,1)}, u32[]{:S(2)}) copy-start(bf16[768,384]{1,0:T(8,128)(2,1)} %get-tuple-element.57.refs_0_) | copy-start | bytes 1769476
  112.0 14.9 %collective-permute-start.17 = (bf16[768,384]{1,0:T(8,128)(2,1)}, bf16[768,384]{1,0:T(8,128)(2,1)S(1)}, u32[]{:S(2)}, u32[]{:S(2)}) collective-permute-start(bf16[768,384]{1,0:T(8,128)(2,1)} %get-tuple-element.57.refs_0_), channel_id=1, source_target_pairs={{0,3},{1,2},{6,5},{7,4},{8,11},{9,10},{14,13},{15,12},{16,19},{17,... | collective-permute-start | bytes 1769480 | tf_op jit(solution)/shard_map/ppermute | solution.py:629
  113.5 1.2 copy-start
  122.3 18.0 %collective-permute-start.12 = (bf16[768,384]{1,0:T(8,128)(2,1)}, bf16[768,384]{1,0:T(8,128)(2,1)S(1)}, u32[]{:S(2)}, u32[]{:S(2)}) collective-permute-start(bf16[768,384]{1,0:T(8,128)(2,1)} %get-tuple-element.56), channel_id=1, source_target_pairs={{0,1},{1,0},{6,7},{7,6},{8,9},{9,8},{14,15},{15,14},{16,17},{17,16... | collective-permute-start | bytes 1769480 | tf_op jit(solution)/shard_map/ppermute | solution.py:629
  124.4 16.0 %collective-permute-start.13 = (bf16[768,384]{1,0:T(8,128)(2,1)}, bf16[768,384]{1,0:T(8,128)(2,1)S(1)}, u32[]{:S(2)}, u32[]{:S(2)}) collective-permute-start(bf16[768,384]{1,0:T(8,128)(2,1)} %get-tuple-element.56), channel_id=1, source_target_pairs={{2,0},{3,1},{4,6},{5,7},{10,8},{11,9},{12,14},{13,15},{18,16},{19,... | collective-permute-start | bytes 1769480 | tf_op jit(solution)/shard_map/ppermute | solution.py:629
  125.7 19.6 %collective-permute-start.14 = (bf16[768,384]{1,0:T(8,128)(2,1)}, bf16[768,384]{1,0:T(8,128)(2,1)S(1)}, u32[]{:S(2)}, u32[]{:S(2)}) collective-permute-start(bf16[768,384]{1,0:T(8,128)(2,1)} %get-tuple-element.55.refs_0_), channel_id=1, source_target_pairs={{2,1},{3,0},{4,7},{5,6},{10,9},{11,8},{12,15},{13,14},{18,17},{19,... | collective-permute-start | bytes 1769480 | tf_op jit(solution)/shard_map/ppermute | solution.py:629
  127.0 1.5 copy-start.1
  128.5 16.8 %copy-start.5 = (bf16[768,384]{1,0:T(8,128)(2,1)S(1)}, bf16[768,384]{1,0:T(8,128)(2,1)}, u32[]{:S(2)}) copy-start(bf16[768,384]{1,0:T(8,128)(2,1)} %get-tuple-element.55.refs_0_) | copy-start | bytes 1769476

commit v4 on v3

--- a/solution.py
+++ b/solution.py
@@ -424,31 +424,47 @@
     )(scalars, steps, far_list, near_list)
 
 
-def halo_kernel(scalars, k_fast, v_fast, k_slow, v_slow, after, fast_ref, slow_ref):
-    fast_ref[0] = k_fast[...]
-    fast_ref[1] = v_fast[...]
-    slow_ref[0] = k_slow[...]
-    slow_ref[1] = v_slow[...]
-
-
-def pack_halos(scalars, keys, values, after):
+def pack_kernel(scalars, k_fast, v_fast, k_slow, v_slow, thin_ref, fast_ref, slow_ref):
+    core, step = scalars[0] & 1, pl.program_id(0)
+    blocks = k_fast.shape[0] // BLK
+
+    def thin(ref):
+        rows = ref[...].astype(jnp.float32).reshape(blocks * THIN, MINSTRIDE, WIDTH)
+        return rows[:, 0, :]
+
+    for out, frame, k_part, v_part in (
+        (fast_ref, 1 - core, k_fast, v_fast),
+        (slow_ref, core, k_slow, v_slow),
+    ):
+        out[0] = k_part[...]
+        out[1] = v_part[...]
+        keys, values = thin(k_part), thin(v_part)
+        pairs = [a[b * THIN : b * THIN + THIN] for b in range(blocks) for a in (keys, values)]
+        first = (frame * FRAME_BLK + step * blocks) * 2 * THIN
+        rows = pl.ds(pl.multiple_of(first, 2 * THIN), blocks * 2 * THIN)
+        thin_ref[rows, :] = jnp.concatenate(pairs, axis=0).astype(jnp.bfloat16)
+
+
+def pack(scalars, keys, values):
     parts = 4
     rows = FRAME // parts
     fast = pl.BlockSpec((rows, WIDTH), lambda i, s: ((1 - (s[0] & 1)) * parts + i, 0))
     slow = pl.BlockSpec((rows, WIDTH), lambda i, s: ((s[0] & 1) * parts + i, 0))
-    shape = jax.ShapeDtypeStruct((2, FRAME, WIDTH), jnp.bfloat16)
-    outs = pl.pallas_call(
-        halo_kernel,
+    frame = jax.ShapeDtypeStruct((2, FRAME, WIDTH), jnp.bfloat16)
+    thinned = jax.ShapeDtypeStruct((BLOCKS * 2 * THIN, WIDTH), jnp.bfloat16)
+    thinned, *frames = pl.pallas_call(
+        pack_kernel,
         grid_spec=pltpu.PrefetchScalarGridSpec(
             num_scalar_prefetch=1,
             grid=(parts,),
-            in_specs=[fast, fast, slow, slow, ANYWHERE],
-            out_specs=[pl.BlockSpec((2, rows, WIDTH), lambda i, s: (0, i, 0))] * 2,
-        ),
-        out_shape=[shape] * 2,
+            in_specs=[fast, fast, slow, slow],
+            out_specs=[pl.BlockSpec(thinned.shape, lambda i, s: (0, 0))]
+            + [pl.BlockSpec((2, rows, WIDTH), lambda i, s: (0, i, 0))] * 2,
+        ),
+        out_shape=[thinned, frame, frame],
         cost_estimate=pl.CostEstimate(flops=0, bytes_accessed=10 * 2**20, transcendentals=0),
-    )(scalars, keys, values, keys, values, after)
-    return [out.reshape(2 * FRAME, WIDTH) for out in outs]
+    )(scalars, keys, values, keys, values)
+    return thinned, *(f.reshape(2 * FRAME, WIDTH) for f in frames)
 
 
 def pass_kernel(a, b, c, d, after, out_ref):
@@ -576,10 +592,7 @@
     across = across + [(j, i) for i, j in across]
     place = jnp.stack([t, h]).astype(jnp.int32)
 
-    def thin(a):
-        return a.reshape(BLOCKS, THIN, MINSTRIDE, WIDTH)[:, :, 0]
-
-    thinned = jnp.concatenate([thin(keys), thin(values)], axis=1).reshape(-1, WIDTH)
+    thinned, fast_part, slow_part = pack(place, keys, values)
     along_x = [
         lax.ppermute(
             thinned, "tm", [(tm_index(*p), tm_index(p[0], p[1] + d, p[2])) for p in coords]
@@ -587,7 +600,6 @@
         for d in range(1, NX)
     ]
 
-    fast_part, slow_part = pack_halos(place, keys, values, thinned)
     halo_fast = lax.ppermute(fast_part, "tm", swap)
     picks, table = index_work(place, stride_table, far_list, near_list)
     slow_part, table, *along_x = lax.optimization_barrier((slow_part, table, *along_x))
@@ -629,8 +641,8 @@
         return lax.ppermute(chunk, ("tm", "head"), pairs)
 
     def received(first, last, fast):
-        two, one, three = [
-            exchange(chunk, e, fast) for e, chunk in ((2, first), (1, first), (3, last))
+        one, two, three = [
+            exchange(chunk, e, fast) for e, chunk in ((1, first), (2, first), (3, last))
         ]
         return last, one, two, three
 

time: 152 us -> 149 us (0.980)
  local copies, waits for them, and re-layouts: 8.34 us -> 5.45 us
    slice x2 -> x0, local copies, waits for them, and re-layouts: 2.85 us -> none  [thin(): return a.reshape(BLOCKS, THIN, MINSTRIDE, WIDTH)[:, :, 0]]
    unnamed x30 -> x28, local copies, waits for them, and re-layouts: 5.4 us -> 5.41 us
  transfers between devices with their start and end apart: 18 -> 18, of which waited for: 6 -> 6; matrix products, arithmetic and copies ran while one was open for 3% -> 3% of each run, Pallas kernels for 43% -> 44%
where the time goes in v4:
time: 149 us; the launch traced here: 148 us
  Pallas kernels  76.9 us (52%)
  starting transfers between devices  33.9 us (23%)
  waiting for transfers between devices  28.2 us (19%)
  local copies, waits for them, and re-layouts  5.45 us (4%)
  other arithmetic  3.05 us (2%)
    pallas_call x2, Pallas kernels, attend(): pl.pallas_call(functools.partial(attend_kernel, chunk=chunk, with_far=wit...  39.6 us
    ppermute x6, waiting for transfers between devices, exchange(): return lax.ppermute(chunk, ('tm', 'head'), pairs)  16.2 us
    pallas_call x2, Pallas kernels, merge_far(): pl.pallas_call(functools.partial(merge_kernel, chunk=chunk), grid_spec=pl...  15.1 us
    ppermute x6, starting transfers between devices, exchange(): return lax.ppermute(chunk, ('tm', 'head'), pairs)  14.4 us
    ppermute x3, starting transfers between devices, per_device(): arrived.append(lax.ppermute(packs[d], 'tm', pairs))  7.74 us
    ppermute x3, waiting for transfers between devices, per_device(): lax.ppermute(thinned, 'tm', [(tm_index(*p), tm_index(p[0], p[1] + d, p[2]...  7.4 us
    pallas_call x2, Pallas kernels, project(): pl.pallas_call(functools.partial(project_kernel, wanted_fast=wanted_fast,...  6.26 us
    pallas_call x1, Pallas kernels, pack(): pl.pallas_call(pack_kernel, grid_spec=pltpu.PrefetchScalarGridSpec(num_sc...  6.03 us
  transfers between devices with their start and end apart: 18, of which 6 were waited for; matrix products, arithmetic and copies ran while one was open for 3% of the time, Pallas kernels for 44%

profile of v4, /device:TPU:0, one launch (start us, length us, event | category | flops | bytes accessed | tf_op | source)
XLA Modules:
  0.0 147.9 jit_solution(7022292066633874503)
XLA Ops:
  0.7 6.0 %shard_map.73 = (bf16[384,384]{1,0:T(8,128)(2,1)}, bf16[2,1536,384]{2,1,0:T(8,128)(2,1)}, bf16[2,1536,384]{2,1,0:T(8,128)(2,1)}) custom-call(s32[2]{0:T(128)} %pad_add_fusion.scalars, bf16[3072,384]{1,0:T(8,128)(2,1)} %k_ref.3, bf16[3072,384]{1,0:T(8,128)(2,1)} %v_ref.3, bf16[3072,384]{1,0:T(8,128)(2,1)} %k_ref.3, bf16[3072,384]{1,0:T(8,128)(2,1)} %v_ref.3), custom_call_target="tpu_custom_call" | custom-call | bytes 10485760 | tf_op jit(solution)/shard_map/pallas_call | solution.py:455
  6.7 1.6 %collective-permute-start = (bf16[384,384]{1,0:T(8,128)(2,1)}, bf16[384,384]{1,0:T(8,128)(2,1)S(1)}, u32[]{:S(2)}, u32[]{:S(2)}) collective-permute-start(bf16[384,384]{1,0:T(8,128)(2,1)} %get-tuple-element.35.refs_0_), channel_id=1, source_target_pairs={{0,8},{4,12},{8,16},{12,20},{16,24},{20,28},{24,0},{28,4},{32,40},... | collective-permute-start | bytes 884744 | tf_op jit(solution)/shard_map/ppermute | solution.py:597
  8.3 2.7 %collective-permute-start.1 = (bf16[384,384]{1,0:T(8,128)(2,1)}, bf16[384,384]{1,0:T(8,128)(2,1)S(1)}, u32[]{:S(2)}, u32[]{:S(2)}) collective-permute-start(bf16[384,384]{1,0:T(8,128)(2,1)} %get-tuple-element.35.refs_0_), channel_id=1, source_target_pairs={{0,16},{4,20},{8,24},{12,28},{16,0},{20,4},{24,8},{28,12},{32,48},... | collective-permute-start | bytes 884744 | tf_op jit(solution)/shard_map/ppermute | solution.py:597
  11.1 1.4 collective-permute-start.2
  14.1 3.4 %shard_map.74 = (s32[48,128]{1,0:T(8,128)}, s32[32,128]{1,0:T(8,128)}) custom-call(s32[2]{0:T(128)} %pad_add_fusion.scalars, s32[64]{0:T(128)} %steps.1, s32[768,16]{1,0:T(8,128)} %copy.9.far_ref, s32[24,16]{1,0:T(8,128)} %copy.10.near_ref), custom_call_target="tpu_custom_call" | custom-call | flops 1048576 | bytes 4194304 | tf_op jit(solution)/shard_map/pallas_call | solution.py:414
  17.5 7.4 %collective-permute-done.1.refs_2_ = bf16[384,384]{1,0:T(8,128)(2,1)S(1)} collective-permute-done((bf16[384,384]{1,0:T(8,128)(2,1)}, bf16[384,384]{1,0:T(8,128)(2,1)S(1)}, u32[]{:S(2)}, u32[]{:S(2)}) %collective-permute-start.1) | collective-permute-done | bytes 294944 | tf_op jit(solution)/shard_map/ppermute | solution.py:597
  24.9 2.1 %collective-permute-start.3 = (bf16[3072,384]{1,0:T(8,128)(2,1)}, bf16[3072,384]{1,0:T(8,128)(2,1)}, u32[]{:S(2)}, u32[]{:S(2)}) collective-permute-start(bf16[3072,384]{1,0:T(8,128)(2,1)} %bitcast.4), channel_id=1, source_target_pairs={{4,8},{12,16},{20,24},{28,32},{36,40},{44,48},{52,56},{60,64},{68,... | collective-permute-start | bytes 7077896 | tf_op jit(solution)/shard_map/ppermute | solution.py:606
  27.1 1.7 %collective-permute-start.9 = (bf16[384,768]{1,0:T(8,128)(2,1)S(1)}, bf16[384,768]{1,0:T(8,128)(2,1)S(1)}, u32[]{:S(2)}, u32[]{:S(2)}) collective-permute-start(bf16[384,768]{1,0:T(8,128)(2,1)S(1)} %constant_dynamic-slice_fusion), channel_id=1, source_target_pairs={{0,1},{1,0},{2,3},{3,2},{4,5},{5,4},{6,7},{7,6},{8,9},{9,8},{10,11... | collective-permute-start | bytes 1769480 | tf_op jit(solution)/shard_map/ppermute | solution.py:618
  28.8 19.8 %shard_map.75 = (bf16[1536,384]{1,0:T(8,128)(2,1)}, f32[1536,384]{1,0:T(8,128)}) custom-call(s32[32,128]{1,0:T(8,128)} %get-tuple-element.36.table, bf16[3072,384]{1,0:T(8,128)(2,1)} %q_ref.7, bf16[3072,384]{1,0:T(8,128)(2,1)} %k_ref.3, bf16[3072,384]{1,0:T(8,128)(2,1)} %v_ref.3, bf16[3072,384]{1,0:T(8,128)(2,1)} %collective-permute-done.4.halo_ref), custom_call_target="tpu_custom_call" | custom-call | flops 15401484288 | bytes 8388608 | tf_op jit(solution)/shard_map/pallas_call | solution.py:217
  48.6 4.0 %shard_map.76 = (bf16[768,384]{1,0:T(8,128)(2,1)}, bf16[768,384]{1,0:T(8,128)(2,1)}, bf16[768,384]{1,0:T(8,128)(2,1)}, bf16[768,384]{1,0:T(8,128)(2,1)}) custom-call(s32[48,128]{1,0:T(8,128)} %get-tuple-element.38.picks, bf16[384,384]{1,0:T(8,128)(2,1)} %get-tuple-element.35.refs_0_, bf16[384,384]{1,0:T(8,128)(2,1)} %copy-done.8, ...), custom_call_target="tpu_custom_call" | custom-call | bytes 4194304 | tf_op jit(solution)/shard_map/pallas_call | solution.py:503
  52.6 3.2 %collective-permute-start.5 = (bf16[768,384]{1,0:T(8,128)(2,1)}, bf16[768,384]{1,0:T(8,128)(2,1)S(1)}, u32[]{:S(2)}, u32[]{:S(2)}) collective-permute-start(bf16[768,384]{1,0:T(8,128)(2,1)} %get-tuple-element.48), channel_id=1, source_target_pairs={{0,32},{4,36},{8,40},{12,44},{16,48},{20,52},{24,56},{28,60},{32,6... | collective-permute-start | bytes 1769480 | tf_op jit(solution)/shard_map/ppermute | solution.py:613
  55.8 3.9 %collective-permute-start.6 = (bf16[768,384]{1,0:T(8,128)(2,1)}, bf16[768,384]{1,0:T(8,128)(2,1)}, u32[]{:S(2)}, u32[]{:S(2)}) collective-permute-start(bf16[768,384]{1,0:T(8,128)(2,1)} %get-tuple-element.49), channel_id=1, source_target_pairs={{0,64},{4,68},{8,72},{12,76},{16,80},{20,84},{24,88},{28,92},{32,9... | collective-permute-start | bytes 1769480 | tf_op jit(solution)/shard_map/ppermute | solution.py:613
  60.4 1.1 pad_maximum_fusion.1
  61.5 2.2 %collective-permute-start.10 = (bf16[768,768]{1,0:T(8,128)(2,1)}, bf16[768,768]{1,0:T(8,128)(2,1)S(1)}, u32[]{:S(2)}, u32[]{:S(2)}) collective-permute-start(bf16[768,768]{1,0:T(8,128)(2,1)} %pad_maximum_fusion.1), channel_id=1, source_target_pairs={{0,3},{1,2},{2,1},{3,0},{4,7},{5,6},{6,5},{7,4},{8,11},{9,10},{10,... | collective-permute-start | bytes 3538952 | tf_op jit(solution)/shard_map/ppermute | solution.py:620
  63.7 19.8 %shard_map.77 = (bf16[1536,384]{1,0:T(8,128)(2,1)}, f32[1536,384]{1,0:T(8,128)}) custom-call(s32[32,128]{1,0:T(8,128)} %get-tuple-element.36.table, bf16[3072,384]{1,0:T(8,128)(2,1)} %q_ref.7, bf16[3072,384]{1,0:T(8,128)(2,1)} %k_ref.3, bf16[3072,384]{1,0:T(8,128)(2,1)} %v_ref.3, bf16[3072,384]{1,0:T(8,128)(2,1)} %collective-permute-done.3.halo_ref, ...), custom_call_target="tpu_custom_call" | custom-call | flops 15401484288 | bytes 8388608 | tf_op jit(solution)/shard_map/pallas_call | solution.py:217
  83.5 2.8 %collective-permute-done.6.c.rest_2_ = bf16[768,384]{1,0:T(8,128)(2,1)} collective-permute-done((bf16[768,384]{1,0:T(8,128)(2,1)}, bf16[768,384]{1,0:T(8,128)(2,1)}, u32[]{:S(2)}, u32[]{:S(2)}) %collective-permute-start.6) | collective-permute-done | bytes 589856 | tf_op jit(solution)/shard_map/ppermute | solution.py:613
  86.3 2.4 %shard_map.78 = bf16[1536,384]{1,0:T(8,128)(2,1)} custom-call(bf16[768,384]{1,0:T(8,128)(2,1)} %get-tuple-element.44.rest_0_.a, bf16[768,384]{1,0:T(8,128)(2,1)} %copy-done.6, bf16[768,384]{1,0:T(8,128)(2,1)} %collective-permute-done.6.c.rest_2_, bf16[768,384]{1,0:T(8,128)(2,1)} %collective-permute-done.7.d.rest_3_, ...), custom_call_target="tpu_custom_call" | custom-call | bytes 2097152 | tf_op jit(solution)/shard_map/pallas_call | solution.py:478
  88.7 0.9 collective-permute-done.10.refs_6_
  89.7 1.3 pad_maximum_fusion
  91.8 1.1 copy-done.7
  92.9 7.5 %shard_map.79 = (bf16[768,384]{1,0:T(8,128)(2,1)}, bf16[768,384]{1,0:T(8,128)(2,1)}) custom-call(s32[32,128]{1,0:T(8,128)} %get-tuple-element.36.table, bf16[3072,384]{1,0:T(8,128)(2,1)} %q_ref.7, bf16[1536,384]{1,0:T(8,128)(2,1)} %get-tuple-element.47.near_ref, f32[1536,384]{1,0:T(8,128)} %get-tuple-element.43.refs_4_.level_ref, ...), custom_call_target="tpu_custom_call" | custom-call | flops 1811939328 | bytes 8388608 | tf_op jit(solution)/shard_map/pallas_call | solution.py:297
  101.1 7.6 %collective-permute-start.16 = (bf16[768,384]{1,0:T(8,128)(2,1)}, bf16[768,384]{1,0:T(8,128)(2,1)S(1)}, u32[]{:S(2)}, u32[]{:S(2)}) collective-permute-start(bf16[768,384]{1,0:T(8,128)(2,1)} %get-tuple-element.60), channel_id=1, source_target_pairs={{0,2},{1,3},{6,4},{7,5},{8,10},{9,11},{14,12},{15,13},{16,18},{17,... | collective-permute-start | bytes 1769480 | tf_op jit(solution)/shard_map/ppermute | solution.py:641
  108.8 1.5 collective-permute-start.17
  110.3 1.2 copy-done
  111.5 7.6 %shard_map.80 = (bf16[768,384]{1,0:T(8,128)(2,1)}, bf16[768,384]{1,0:T(8,128)(2,1)}) custom-call(s32[32,128]{1,0:T(8,128)} %get-tuple-element.36.table, bf16[3072,384]{1,0:T(8,128)(2,1)} %q_ref.7, bf16[1536,384]{1,0:T(8,128)(2,1)} %get-tuple-element.52.near_ref, f32[1536,384]{1,0:T(8,128)} %get-tuple-element.53.after.rest_5_.level_ref, ...), custom_call_target="tpu_custom_call" | custom-call | flops 1811939328 | bytes 8388608 | tf_op jit(solution)/shard_map/pallas_call | solution.py:297
  119.1 2.0 %collective-permute-start.12 = (bf16[768,384]{1,0:T(8,128)(2,1)}, bf16[768,384]{1,0:T(8,128)(2,1)S(1)}, u32[]{:S(2)}, u32[]{:S(2)}) collective-permute-start(bf16[768,384]{1,0:T(8,128)(2,1)} %get-tuple-element.58), channel_id=1, source_target_pairs={{0,1},{1,0},{6,7},{7,6},{8,9},{9,8},{14,15},{15,14},{16,17},{17,16... | collective-permute-start | bytes 1769480 | tf_op jit(solution)/shard_map/ppermute | solution.py:641
  121.1 1.3 collective-permute-start.13
  122.4 1.3 collective-permute-start.14
  123.8 1.5 copy-done.1
  125.9 11.3 %collective-permute-done.12.refs_1_ = bf16[768,384]{1,0:T(8,128)(2,1)S(1)} collective-permute-done((bf16[768,384]{1,0:T(8,128)(2,1)}, bf16[768,384]{1,0:T(8,128)(2,1)S(1)}, u32[]{:S(2)}, u32[]{:S(2)}) %collective-permute-start.12) | collective-permute-done | bytes 589856 | tf_op jit(solution)/shard_map/ppermute | solution.py:641
  137.1 4.9 %collective-permute-done.14.refs_3_ = bf16[768,384]{1,0:T(8,128)(2,1)S(1)} collective-permute-done((bf16[768,384]{1,0:T(8,128)(2,1)}, bf16[768,384]{1,0:T(8,128)(2,1)S(1)}, u32[]{:S(2)}, u32[]{:S(2)}) %collective-permute-start.14) | collective-permute-done | bytes 589856 | tf_op jit(solution)/shard_map/ppermute | solution.py:641
  142.1 5.7 %shard_map.82 = bf16[768,1536]{1,0:T(8,128)(2,1)} custom-call(s32[2]{0:T(128)S(1)} %copy-done.3, bf16[768,384]{1,0:T(8,128)(2,1)S(1)} %copy-done.5, bf16[768,384]{1,0:T(8,128)(2,1)S(1)} %collective-permute-done.12.refs_1_, bf16[768,384]{1,0:T(8,128)(2,1)S(1)} %collective-permute-done.13.refs_2_, ...), custom_call_target="tpu_custom_call", output_to_operand_aliasing={{}: (9, {})} | custom-call | flops 3623878656 | bytes 10485760 | tf_op jit(solution)/shard_map/pallas_call | solution.py:565
  (46 shorter events, 5.2 us)
Async XLA Ops:
  0.7 11.9 %copy-start.11 = (s32[768,16]{0,1:T(8,128)S(1)}, s32[768,16]{0,1:T(8,128)}, u32[]{:S(2)}) copy-start(s32[768,16]{0,1:T(8,128)} %param.12) | copy-start | bytes 147460
  0.7 12.8 %copy-start.12 = (s32[24,16]{0,1:T(8,128)S(1)}, s32[24,16]{0,1:T(8,128)}, u32[]{:S(2)}) copy-start(s32[24,16]{0,1:T(8,128)} %param.11) | copy-start | bytes 4612
  0.7 26.4 %copy-start.2 = (bf16[384,1536]{1,0:T(8,128)(2,1)S(1)}, bf16[384,1536]{1,0:T(8,128)(2,1)}, u32[]{:S(2)}) copy-start(bf16[384,1536]{1,0:T(8,128)(2,1)} %refs_4_.3) | copy-start | bytes 3538948
  6.7 22.1 %collective-permute-start.4 = (bf16[3072,384]{1,0:T(8,128)(2,1)}, bf16[3072,384]{1,0:T(8,128)(2,1)}, u32[]{:S(2)}, u32[]{:S(2)}) collective-permute-start(bf16[3072,384]{1,0:T(8,128)(2,1)} %bitcast.5), channel_id=1, source_target_pairs={{0,4},{4,0},{8,12},{12,8},{16,20},{20,16},{24,28},{28,24},{32,36},... | collective-permute-start | bytes 7077896 | tf_op jit(solution)/shard_map/ppermute | solution.py:603
  6.7 10.8 %collective-permute-start = (bf16[384,384]{1,0:T(8,128)(2,1)}, bf16[384,384]{1,0:T(8,128)(2,1)S(1)}, u32[]{:S(2)}, u32[]{:S(2)}) collective-permute-start(bf16[384,384]{1,0:T(8,128)(2,1)} %get-tuple-element.35.refs_0_), channel_id=1, source_target_pairs={{0,8},{4,12},{8,16},{12,20},{16,24},{20,28},{24,0},{28,4},{32,40},... | collective-permute-start | bytes 884744 | tf_op jit(solution)/shard_map/ppermute | solution.py:597
  8.3 16.6 %collective-permute-start.1 = (bf16[384,384]{1,0:T(8,128)(2,1)}, bf16[384,384]{1,0:T(8,128)(2,1)S(1)}, u32[]{:S(2)}, u32[]{:S(2)}) collective-permute-start(bf16[384,384]{1,0:T(8,128)(2,1)} %get-tuple-element.35.refs_0_), channel_id=1, source_target_pairs={{0,16},{4,20},{8,24},{12,28},{16,0},{20,4},{24,8},{28,12},{32,48},... | collective-permute-start | bytes 884744 | tf_op jit(solution)/shard_map/ppermute | solution.py:597
  11.1 13.9 %collective-permute-start.2 = (bf16[384,384]{1,0:T(8,128)(2,1)}, bf16[384,384]{1,0:T(8,128)(2,1)S(1)}, u32[]{:S(2)}, u32[]{:S(2)}) collective-permute-start(bf16[384,384]{1,0:T(8,128)(2,1)} %get-tuple-element.35.refs_0_), channel_id=1, source_target_pairs={{0,24},{4,28},{8,0},{12,4},{16,8},{20,12},{24,16},{28,20},{32,56},... | collective-permute-start | bytes 884744 | tf_op jit(solution)/shard_map/ppermute | solution.py:597
  17.5 31.1 %copy-start.8 = (bf16[384,384]{1,0:T(8,128)(2,1)}, bf16[384,384]{1,0:T(8,128)(2,1)S(1)}, u32[]{:S(2)}) copy-start(bf16[384,384]{1,0:T(8,128)(2,1)S(1)} %collective-permute-done.refs_1_) | copy-start | bytes 884740
  24.9 23.7 %copy-start.9 = (bf16[384,384]{1,0:T(8,128)(2,1)}, bf16[384,384]{1,0:T(8,128)(2,1)S(1)}, u32[]{:S(2)}) copy-start(bf16[384,384]{1,0:T(8,128)(2,1)S(1)} %collective-permute-done.1.refs_2_) | copy-start | bytes 884740
  24.9 23.7 %copy-start.10 = (bf16[384,384]{1,0:T(8,128)(2,1)}, bf16[384,384]{1,0:T(8,128)(2,1)S(1)}, u32[]{:S(2)}) copy-start(bf16[384,384]{1,0:T(8,128)(2,1)S(1)} %collective-permute-done.2.refs_3_) | copy-start | bytes 884740
  24.9 38.7 %collective-permute-start.3 = (bf16[3072,384]{1,0:T(8,128)(2,1)}, bf16[3072,384]{1,0:T(8,128)(2,1)}, u32[]{:S(2)}, u32[]{:S(2)}) collective-permute-start(bf16[3072,384]{1,0:T(8,128)(2,1)} %bitcast.4), channel_id=1, source_target_pairs={{4,8},{12,16},{20,24},{28,32},{36,40},{44,48},{52,56},{60,64},{68,... | collective-permute-start | bytes 7077896 | tf_op jit(solution)/shard_map/ppermute | solution.py:606
  27.1 33.3 %collective-permute-start.9 = (bf16[384,768]{1,0:T(8,128)(2,1)S(1)}, bf16[384,768]{1,0:T(8,128)(2,1)S(1)}, u32[]{:S(2)}, u32[]{:S(2)}) collective-permute-start(bf16[384,768]{1,0:T(8,128)(2,1)S(1)} %constant_dynamic-slice_fusion), channel_id=1, source_target_pairs={{0,1},{1,0},{2,3},{3,2},{4,5},{5,4},{6,7},{7,6},{8,9},{9,8},{10,11... | collective-permute-start | bytes 1769480 | tf_op jit(solution)/shard_map/ppermute | solution.py:618
  52.6 30.8 %collective-permute-start.5 = (bf16[768,384]{1,0:T(8,128)(2,1)}, bf16[768,384]{1,0:T(8,128)(2,1)S(1)}, u32[]{:S(2)}, u32[]{:S(2)}) collective-permute-start(bf16[768,384]{1,0:T(8,128)(2,1)} %get-tuple-element.48), channel_id=1, source_target_pairs={{0,32},{4,36},{8,40},{12,44},{16,48},{20,52},{24,56},{28,60},{32,6... | collective-permute-start | bytes 1769480 | tf_op jit(solution)/shard_map/ppermute | solution.py:613
  55.8 30.5 %collective-permute-start.6 = (bf16[768,384]{1,0:T(8,128)(2,1)}, bf16[768,384]{1,0:T(8,128)(2,1)}, u32[]{:S(2)}, u32[]{:S(2)}) collective-permute-start(bf16[768,384]{1,0:T(8,128)(2,1)} %get-tuple-element.49), channel_id=1, source_target_pairs={{0,64},{4,68},{8,72},{12,76},{16,80},{20,84},{24,88},{28,92},{32,9... | collective-permute-start | bytes 1769480 | tf_op jit(solution)/shard_map/ppermute | solution.py:613
  59.7 26.6 %collective-permute-start.7 = (bf16[768,384]{1,0:T(8,128)(2,1)}, bf16[768,384]{1,0:T(8,128)(2,1)}, u32[]{:S(2)}, u32[]{:S(2)}) collective-permute-start(bf16[768,384]{1,0:T(8,128)(2,1)} %get-tuple-element.50), channel_id=1, source_target_pairs={{0,96},{4,100},{8,104},{12,108},{16,112},{20,116},{24,120},{28,124... | collective-permute-start | bytes 1769480 | tf_op jit(solution)/shard_map/ppermute | solution.py:613
  61.5 28.2 %collective-permute-start.10 = (bf16[768,768]{1,0:T(8,128)(2,1)}, bf16[768,768]{1,0:T(8,128)(2,1)S(1)}, u32[]{:S(2)}, u32[]{:S(2)}) collective-permute-start(bf16[768,768]{1,0:T(8,128)(2,1)} %pad_maximum_fusion.1), channel_id=1, source_target_pairs={{0,3},{1,2},{2,1},{3,0},{4,7},{5,6},{6,5},{7,4},{8,11},{9,10},{10,... | collective-permute-start | bytes 3538952 | tf_op jit(solution)/shard_map/ppermute | solution.py:620
  83.5 2.8 %copy-start.6 = (bf16[768,384]{1,0:T(8,128)(2,1)}, bf16[768,384]{1,0:T(8,128)(2,1)S(1)}, u32[]{:S(2)}) copy-start(bf16[768,384]{1,0:T(8,128)(2,1)S(1)} %collective-permute-done.5.b.rest_1_) | copy-start | bytes 1769476
  88.7 3.1 %collective-permute-start.8 = (bf16[1536,384]{1,0:T(8,128)(2,1)}, bf16[1536,384]{1,0:T(8,128)(2,1)S(1)}, u32[]{:S(2)}, u32[]{:S(2)}) collective-permute-start(bf16[1536,384]{1,0:T(8,128)(2,1)} %shard_map.78), channel_id=1, source_target_pairs={{0,4},{4,0},{8,12},{12,8},{16,20},{20,16},{24,28},{28,24},{32,36},... | collective-permute-start | bytes 3538952 | tf_op jit(solution)/shard_map/ppermute | solution.py:627
  91.0 19.3 %collective-permute-start.11 = (bf16[1152,768]{1,0:T(8,128)(2,1)}, bf16[1152,768]{1,0:T(8,128)(2,1)S(1)}, u32[]{:S(2)}, u32[]{:S(2)}) collective-permute-start(bf16[1152,768]{1,0:T(8,128)(2,1)} %pad_maximum_fusion), channel_id=1, source_target_pairs={{0,4},{4,0},{8,12},{12,8},{16,20},{20,16},{24,28},{28,24},{32,36},... | collective-permute-start | bytes 5308424 | tf_op jit(solution)/shard_map/ppermute | solution.py:629
  91.8 1.1 copy-start.7
  100.4 22.0 %collective-permute-start.15 = (bf16[768,384]{1,0:T(8,128)(2,1)}, bf16[768,384]{1,0:T(8,128)(2,1)S(1)}, u32[]{:S(2)}, u32[]{:S(2)}) collective-permute-start(bf16[768,384]{1,0:T(8,128)(2,1)} %get-tuple-element.60), channel_id=1, source_target_pairs={{2,3},{3,2},{4,5},{5,4},{10,11},{11,10},{12,13},{13,12},{18,19},{1... | collective-permute-start | bytes 1769480 | tf_op jit(solution)/shard_map/ppermute | solution.py:641
  101.1 22.6 %collective-permute-start.16 = (bf16[768,384]{1,0:T(8,128)(2,1)}, bf16[768,384]{1,0:T(8,128)(2,1)S(1)}, u32[]{:S(2)}, u32[]{:S(2)}) collective-permute-start(bf16[768,384]{1,0:T(8,128)(2,1)} %get-tuple-element.60), channel_id=1, source_target_pairs={{0,2},{1,3},{6,4},{7,5},{8,10},{9,11},{14,12},{15,13},{16,18},{17,... | collective-permute-start | bytes 1769480 | tf_op jit(solution)/shard_map/ppermute | solution.py:641
  108.8 15.0 %copy-start.3 = (s32[2]{0:T(128)S(1)}, s32[2]{0:T(128)}, u32[]{:S(2)}) copy-start(s32[2]{0:T(128)} %pad_add_fusion.scalars) | copy-start | bytes 28
  108.8 15.0 %copy-start.4 = (bf16[768,384]{1,0:T(8,128)(2,1)S(1)}, bf16[768,384]{1,0:T(8,128)(2,1)}, u32[]{:S(2)}) copy-start(bf16[768,384]{1,0:T(8,128)(2,1)} %get-tuple-element.59.refs_0_) | copy-start | bytes 1769476
  108.8 15.0 %collective-permute-start.17 = (bf16[768,384]{1,0:T(8,128)(2,1)}, bf16[768,384]{1,0:T(8,128)(2,1)S(1)}, u32[]{:S(2)}, u32[]{:S(2)}) collective-permute-start(bf16[768,384]{1,0:T(8,128)(2,1)} %get-tuple-element.59.refs_0_), channel_id=1, source_target_pairs={{0,3},{1,2},{6,5},{7,4},{8,11},{9,10},{14,13},{15,12},{16,19},{17,... | collective-permute-start | bytes 1769480 | tf_op jit(solution)/shard_map/ppermute | solution.py:641
  110.3 1.2 copy-start
  119.1 18.0 %collective-permute-start.12 = (bf16[768,384]{1,0:T(8,128)(2,1)}, bf16[768,384]{1,0:T(8,128)(2,1)S(1)}, u32[]{:S(2)}, u32[]{:S(2)}) collective-permute-start(bf16[768,384]{1,0:T(8,128)(2,1)} %get-tuple-element.58), channel_id=1, source_target_pairs={{0,1},{1,0},{6,7},{7,6},{8,9},{9,8},{14,15},{15,14},{16,17},{17,16... | collective-permute-start | bytes 1769480 | tf_op jit(solution)/shard_map/ppermute | solution.py:641
  121.1 16.0 %collective-permute-start.13 = (bf16[768,384]{1,0:T(8,128)(2,1)}, bf16[768,384]{1,0:T(8,128)(2,1)S(1)}, u32[]{:S(2)}, u32[]{:S(2)}) collective-permute-start(bf16[768,384]{1,0:T(8,128)(2,1)} %get-tuple-element.58), channel_id=1, source_target_pairs={{2,0},{3,1},{4,6},{5,7},{10,8},{11,9},{12,14},{13,15},{18,16},{19,... | collective-permute-start | bytes 1769480 | tf_op jit(solution)/shard_map/ppermute | solution.py:641
  122.4 19.6 %collective-permute-start.14 = (bf16[768,384]{1,0:T(8,128)(2,1)}, bf16[768,384]{1,0:T(8,128)(2,1)S(1)}, u32[]{:S(2)}, u32[]{:S(2)}) collective-permute-start(bf16[768,384]{1,0:T(8,128)(2,1)} %get-tuple-element.57.refs_0_), channel_id=1, source_target_pairs={{2,1},{3,0},{4,7},{5,6},{10,9},{11,8},{12,15},{13,14},{18,17},{19,... | collective-permute-start | bytes 1769480 | tf_op jit(solution)/shard_map/ppermute | solution.py:641
  123.8 1.5 %copy-start.1 = (bf16[1152,768]{1,0:T(8,128)(2,1)S(1)}, bf16[1152,768]{1,0:T(8,128)(2,1)}, u32[]{:S(2)}) copy-start(bf16[1152,768]{1,0:T(8,128)(2,1)} %copy-done) | copy-start | bytes 5308420
  125.3 16.8 %copy-start.5 = (bf16[768,384]{1,0:T(8,128)(2,1)S(1)}, bf16[768,384]{1,0:T(8,128)(2,1)}, u32[]{:S(2)}) copy-start(bf16[768,384]{1,0:T(8,128)(2,1)} %get-tuple-element.57.refs_0_) | copy-start | bytes 1769476

commit v5 on v4

--- a/solution.py
+++ b/solution.py
@@ -28,7 +28,7 @@
 LOG2_SCALE = math.log2(math.e) / math.sqrt(HD)
 NT = (((1,), (1,)), ((), ()))
 VMEM_LIMIT = 56 * 2**20
-UNROLL = 3
+UNROLL = 6
 SLOT, STRIDE, ORDER = KNEAR, KNEAR + KFAR, BLOCKS
 FAST_FIRST, FAST_LAST, SLOW_FIRST, SLOW_LAST = range(4)
 IN_HBM = pl.BlockSpec(memory_space=pltpu.HBM)
@@ -626,10 +626,12 @@
     )
     passed = lax.ppermute(pack_passed(arrived, near_slow[1]), "tm", swap)
     far = [*arrived, passed]
+    first_fast, last_fast = merge_far(table, query, near_fast, far, FAST_FIRST, near_slow[1])
+    near_slow, first_fast, w_one, w_two = lax.optimization_barrier(
+        (near_slow, first_fast, w_one, w_two)
+    )
     w_swap = lax.ppermute(jnp.concatenate([w_one, w_two], axis=0), "tm", swap)
-    first_fast, last_fast = merge_far(table, query, near_fast, far, FAST_FIRST, near_slow[1])
-    near_slow, first_fast = lax.optimization_barrier((near_slow, first_fast))
-    first_slow, last_slow = merge_far(table, query, near_slow, far, SLOW_FIRST, w_swap)
+    first_slow, last_slow = merge_far(table, query, near_slow, far, SLOW_FIRST, first_fast)
 
     def exchange(chunk, e, fast):
         pairs = []

time: 149 us -> 169 us (1.13)
  waiting for transfers between devices: 28.2 us -> 49.3 us
    ppermute x1, waiting for transfers between devices: 0.94 us -> 18 us  [per_device(): lax.ppermute(jnp.concatenate([half, w_one], axis=0), 'head', [(g, g ^ 3)...]
    ppermute x3, waiting for transfers between devices: 2.81 us -> 6.37 us  [per_device(): arrived.append(lax.ppermute(packs[d], 'tm', pairs))]
    unnamed x28 -> x30, local copies, waits for them, and re-layouts: 5.41 us -> 3.78 us
  transfers between devices with their start and end apart: 18 -> 18, of which waited for: 6 -> 6; matrix products, arithmetic and copies ran while one was open for 3% -> 2% of each run, Pallas kernels for 44% -> 38%
where the time goes in v5:
time: 169 us; the launch traced here: 168 us
  Pallas kernels  75.9 us (45%)
  waiting for transfers between devices  49.3 us (29%)
  starting transfers between devices  34.6 us (20%)
  local copies, waits for them, and re-layouts  4.63 us (3%)
  other arithmetic  3.04 us (2%)
    pallas_call x2, Pallas kernels, attend(): pl.pallas_call(functools.partial(attend_kernel, chunk=chunk, with_far=wit...  38.4 us
    ppermute x1, waiting for transfers between devices, per_device(): lax.ppermute(jnp.concatenate([half, w_one], axis=0), 'head', [(g, g ^ 3)...  18 us
    ppermute x6, waiting for transfers between devices, exchange(): return lax.ppermute(chunk, ('tm', 'head'), pairs)  17.6 us
    pallas_call x2, Pallas kernels, merge_far(): pl.pallas_call(functools.partial(merge_kernel, chunk=chunk), grid_spec=pl...  15.1 us
    ppermute x6, starting transfers between devices, exchange(): return lax.ppermute(chunk, ('tm', 'head'), pairs)  14.2 us
    ppermute x3, starting transfers between devices, per_device(): arrived.append(lax.ppermute(packs[d], 'tm', pairs))  7.74 us
    ppermute x3, waiting for transfers between devices, per_device(): lax.ppermute(thinned, 'tm', [(tm_index(*p), tm_index(p[0], p[1] + d, p[2]...  7.38 us
    pallas_call x2, Pallas kernels, project(): pl.pallas_call(functools.partial(project_kernel, wanted_fast=wanted_fast,...  6.43 us
  transfers between devices with their start and end apart: 18, of which 6 were waited for; matrix products, arithmetic and copies ran while one was open for 2% of the time, Pallas kernels for 38%

profile of v5, /device:TPU:0, one launch (start us, length us, event | category | flops | bytes accessed | tf_op | source)
XLA Modules:
  0.0 167.9 jit_solution(12407985964524485740)
XLA Ops:
  0.6 6.0 %shard_map.73 = (bf16[384,384]{1,0:T(8,128)(2,1)}, bf16[2,1536,384]{2,1,0:T(8,128)(2,1)}, bf16[2,1536,384]{2,1,0:T(8,128)(2,1)}) custom-call(s32[2]{0:T(128)} %pad_add_fusion.scalars, bf16[3072,384]{1,0:T(8,128)(2,1)} %k_ref.3, bf16[3072,384]{1,0:T(8,128)(2,1)} %v_ref.3, bf16[3072,384]{1,0:T(8,128)(2,1)} %k_ref.3, bf16[3072,384]{1,0:T(8,128)(2,1)} %v_ref.3), custom_call_target="tpu_custom_call" | custom-call | bytes 10485760 | tf_op jit(solution)/shard_map/pallas_call | solution.py:455
  6.6 1.6 collective-permute-start
  8.3 2.7 %collective-permute-start.1 = (bf16[384,384]{1,0:T(8,128)(2,1)}, bf16[384,384]{1,0:T(8,128)(2,1)S(1)}, u32[]{:S(2)}, u32[]{:S(2)}) collective-permute-start(bf16[384,384]{1,0:T(8,128)(2,1)} %get-tuple-element.37.refs_0_), channel_id=1, source_target_pairs={{0,16},{4,20},{8,24},{12,28},{16,0},{20,4},{24,8},{28,12},{32,48},... | collective-permute-start | bytes 884744 | tf_op jit(solution)/shard_map/ppermute | solution.py:597
  11.0 1.4 collective-permute-start.2
  12.4 0.9 copy.9.far_ref
  14.0 3.4 %shard_map.74 = (s32[48,128]{1,0:T(8,128)}, s32[32,128]{1,0:T(8,128)}) custom-call(s32[2]{0:T(128)} %pad_add_fusion.scalars, s32[64]{0:T(128)} %steps.1, s32[768,16]{1,0:T(8,128)} %copy.9.far_ref, s32[24,16]{1,0:T(8,128)} %copy.10.near_ref), custom_call_target="tpu_custom_call" | custom-call | flops 1048576 | bytes 4194304 | tf_op jit(solution)/shard_map/pallas_call | solution.py:414
  17.5 7.4 %collective-permute-done.1.refs_2_ = bf16[384,384]{1,0:T(8,128)(2,1)S(1)} collective-permute-done((bf16[384,384]{1,0:T(8,128)(2,1)}, bf16[384,384]{1,0:T(8,128)(2,1)S(1)}, u32[]{:S(2)}, u32[]{:S(2)}) %collective-permute-start.1) | collective-permute-done | bytes 294944 | tf_op jit(solution)/shard_map/ppermute | solution.py:597
  24.9 2.1 %collective-permute-start.3 = (bf16[3072,384]{1,0:T(8,128)(2,1)}, bf16[3072,384]{1,0:T(8,128)(2,1)}, u32[]{:S(2)}, u32[]{:S(2)}) collective-permute-start(bf16[3072,384]{1,0:T(8,128)(2,1)} %bitcast.4), channel_id=1, source_target_pairs={{4,8},{12,16},{20,24},{28,32},{36,40},{44,48},{52,56},{60,64},{68,... | collective-permute-start | bytes 7077896 | tf_op jit(solution)/shard_map/ppermute | solution.py:606
  27.0 0.8 constant_dynamic-slice_fusion
  27.8 1.6 collective-permute-start.9
  29.4 19.2 %shard_map.75 = (bf16[1536,384]{1,0:T(8,128)(2,1)}, f32[1536,384]{1,0:T(8,128)}) custom-call(s32[32,128]{1,0:T(8,128)} %get-tuple-element.38.table, bf16[3072,384]{1,0:T(8,128)(2,1)} %q_ref.7, bf16[3072,384]{1,0:T(8,128)(2,1)} %k_ref.3, bf16[3072,384]{1,0:T(8,128)(2,1)} %v_ref.3, bf16[3072,384]{1,0:T(8,128)(2,1)} %collective-permute-done.4.halo_ref), custom_call_target="tpu_custom_call" | custom-call | flops 15401484288 | bytes 8388608 | tf_op jit(solution)/shard_map/pallas_call | solution.py:217
  48.7 4.1 %shard_map.76 = (bf16[768,384]{1,0:T(8,128)(2,1)}, bf16[768,384]{1,0:T(8,128)(2,1)}, bf16[768,384]{1,0:T(8,128)(2,1)}, bf16[768,384]{1,0:T(8,128)(2,1)}) custom-call(s32[48,128]{1,0:T(8,128)} %get-tuple-element.40.picks, bf16[384,384]{1,0:T(8,128)(2,1)} %get-tuple-element.37.refs_0_, bf16[384,384]{1,0:T(8,128)(2,1)} %copy-done.9, ...), custom_call_target="tpu_custom_call" | custom-call | bytes 4194304 | tf_op jit(solution)/shard_map/pallas_call | solution.py:503
  52.8 3.1 %collective-permute-start.5 = (bf16[768,384]{1,0:T(8,128)(2,1)}, bf16[768,384]{1,0:T(8,128)(2,1)S(1)}, u32[]{:S(2)}, u32[]{:S(2)}) collective-permute-start(bf16[768,384]{1,0:T(8,128)(2,1)} %get-tuple-element.50), channel_id=1, source_target_pairs={{0,32},{4,36},{8,40},{12,44},{16,48},{20,52},{24,56},{28,60},{32,6... | collective-permute-start | bytes 1769480 | tf_op jit(solution)/shard_map/ppermute | solution.py:613
  55.9 3.9 %collective-permute-start.6 = (bf16[768,384]{1,0:T(8,128)(2,1)}, bf16[768,384]{1,0:T(8,128)(2,1)S(1)}, u32[]{:S(2)}, u32[]{:S(2)}) collective-permute-start(bf16[768,384]{1,0:T(8,128)(2,1)} %get-tuple-element.51), channel_id=1, source_target_pairs={{0,64},{4,68},{8,72},{12,76},{16,80},{20,84},{24,88},{28,92},{32,9... | collective-permute-start | bytes 1769480 | tf_op jit(solution)/shard_map/ppermute | solution.py:613
  60.5 19.2 %shard_map.77 = (bf16[1536,384]{1,0:T(8,128)(2,1)}, f32[1536,384]{1,0:T(8,128)}) custom-call(s32[32,128]{1,0:T(8,128)} %get-tuple-element.38.table, bf16[3072,384]{1,0:T(8,128)(2,1)} %q_ref.7, bf16[3072,384]{1,0:T(8,128)(2,1)} %k_ref.3, bf16[3072,384]{1,0:T(8,128)(2,1)} %v_ref.3, bf16[3072,384]{1,0:T(8,128)(2,1)} %collective-permute-done.3.halo_ref, ...), custom_call_target="tpu_custom_call" | custom-call | flops 15401484288 | bytes 8388608 | tf_op jit(solution)/shard_map/pallas_call | solution.py:217
  79.7 6.4 %collective-permute-done.6.c.rest_2_ = bf16[768,384]{1,0:T(8,128)(2,1)S(1)} collective-permute-done((bf16[768,384]{1,0:T(8,128)(2,1)}, bf16[768,384]{1,0:T(8,128)(2,1)S(1)}, u32[]{:S(2)}, u32[]{:S(2)}) %collective-permute-start.6) | collective-permute-done | bytes 589856 | tf_op jit(solution)/shard_map/ppermute | solution.py:613
  87.1 2.4 %shard_map.78 = bf16[1536,384]{1,0:T(8,128)(2,1)} custom-call(bf16[768,384]{1,0:T(8,128)(2,1)} %get-tuple-element.46.rest_0_.a, bf16[768,384]{1,0:T(8,128)(2,1)} %copy-done.4, bf16[768,384]{1,0:T(8,128)(2,1)} %copy-done.5, bf16[768,384]{1,0:T(8,128)(2,1)} %copy-done.6, f32[1536,384]{1,0:T(8,128)} %get-tuple-element.58.after.rest_5_.level_ref), custom_call_target="tpu_custom_call" | custom-call | bytes 2097152 | tf_op jit(solution)/shard_map/pallas_call | solution.py:478
  89.6 1.1 pad_maximum_fusion.1
  90.7 3.1 %collective-permute-start.10 = (bf16[768,768]{1,0:T(8,128)(2,1)S(1)}, bf16[768,768]{1,0:T(8,128)(2,1)S(1)}, u32[]{:S(2)}, u32[]{:S(2)}) collective-permute-start(bf16[768,768]{1,0:T(8,128)(2,1)S(1)} %pad_maximum_fusion.1), channel_id=1, source_target_pairs={{0,3},{1,2},{2,1},{3,0},{4,7},{5,6},{6,5},{7,4},{8,11},{9,10},{10,... | collective-permute-start | bytes 3538952 | tf_op jit(solution)/shard_map/ppermute | solution.py:620
  93.8 1.1 copy-done.7
  94.9 7.5 %shard_map.79 = (bf16[768,384]{1,0:T(8,128)(2,1)}, bf16[768,384]{1,0:T(8,128)(2,1)}) custom-call(s32[32,128]{1,0:T(8,128)} %get-tuple-element.38.table, bf16[3072,384]{1,0:T(8,128)(2,1)} %q_ref.7, bf16[1536,384]{1,0:T(8,128)(2,1)} %get-tuple-element.49.near_ref, f32[1536,384]{1,0:T(8,128)} %get-tuple-element.45.refs_4_.level_ref, ...), custom_call_target="tpu_custom_call" | custom-call | flops 1811939328 | bytes 8388608 | tf_op jit(solution)/shard_map/pallas_call | solution.py:297
  102.5 18.0 %collective-permute-done.10.refs_6_ = bf16[768,768]{1,0:T(8,128)(2,1)S(1)} collective-permute-done((bf16[768,768]{1,0:T(8,128)(2,1)S(1)}, bf16[768,768]{1,0:T(8,128)(2,1)S(1)}, u32[]{:S(2)}, u32[]{:S(2)}) %collective-permute-start.10) | collective-permute-done | bytes 1179680 | tf_op jit(solution)/shard_map/ppermute | solution.py:620
  120.4 1.3 pad_maximum_fusion
  122.5 7.6 %collective-permute-start.16 = (bf16[768,384]{1,0:T(8,128)(2,1)S(1)}, bf16[768,384]{1,0:T(8,128)(2,1)S(1)}, u32[]{:S(2)}, u32[]{:S(2)}) collective-permute-start(bf16[768,384]{1,0:T(8,128)(2,1)S(1)} %copy-done.8), channel_id=1, source_target_pairs={{0,2},{1,3},{6,4},{7,5},{8,10},{9,11},{14,12},{15,13},{16,18},{17,... | collective-permute-start | bytes 1769480 | tf_op jit(solution)/shard_map/ppermute | solution.py:643
  130.1 1.3 collective-permute-start.17
  131.4 7.6 %shard_map.80 = (bf16[768,384]{1,0:T(8,128)(2,1)}, bf16[768,384]{1,0:T(8,128)(2,1)}) custom-call(s32[32,128]{1,0:T(8,128)} %get-tuple-element.38.table, bf16[3072,384]{1,0:T(8,128)(2,1)} %q_ref.7, bf16[1536,384]{1,0:T(8,128)(2,1)} %get-tuple-element.57.near_ref, f32[1536,384]{1,0:T(8,128)} %get-tuple-element.58.after.rest_5_.level_ref, ...), custom_call_target="tpu_custom_call" | custom-call | flops 1811939328 | bytes 8388608 | tf_op jit(solution)/shard_map/pallas_call | solution.py:297
  139.0 1.9 %collective-permute-start.11 = (bf16[768,384]{1,0:T(8,128)(2,1)}, bf16[768,384]{1,0:T(8,128)(2,1)S(1)}, u32[]{:S(2)}, u32[]{:S(2)}) collective-permute-start(bf16[768,384]{1,0:T(8,128)(2,1)} %get-tuple-element.61), channel_id=1, source_target_pairs={{0,1},{1,0},{6,7},{7,6},{8,9},{9,8},{14,15},{15,14},{16,17},{17,16... | collective-permute-start | bytes 1769480 | tf_op jit(solution)/shard_map/ppermute | solution.py:643
  140.9 1.3 collective-permute-start.12
  142.2 1.4 collective-permute-start.13
  144.7 12.6 %collective-permute-done.11.refs_1_ = bf16[768,384]{1,0:T(8,128)(2,1)S(1)} collective-permute-done((bf16[768,384]{1,0:T(8,128)(2,1)}, bf16[768,384]{1,0:T(8,128)(2,1)S(1)}, u32[]{:S(2)}, u32[]{:S(2)}) %collective-permute-start.11) | collective-permute-done | bytes 589856 | tf_op jit(solution)/shard_map/ppermute | solution.py:643
  157.3 4.8 %collective-permute-done.13.refs_3_ = bf16[768,384]{1,0:T(8,128)(2,1)S(1)} collective-permute-done((bf16[768,384]{1,0:T(8,128)(2,1)}, bf16[768,384]{1,0:T(8,128)(2,1)S(1)}, u32[]{:S(2)}, u32[]{:S(2)}) %collective-permute-start.13) | collective-permute-done | bytes 589856 | tf_op jit(solution)/shard_map/ppermute | solution.py:643
  162.1 5.6 %shard_map.82 = bf16[768,1536]{1,0:T(8,128)(2,1)} custom-call(s32[2]{0:T(128)S(1)} %copy-done.1, bf16[768,384]{1,0:T(8,128)(2,1)S(1)} %copy-done.3, bf16[768,384]{1,0:T(8,128)(2,1)S(1)} %collective-permute-done.11.refs_1_, bf16[768,384]{1,0:T(8,128)(2,1)S(1)} %collective-permute-done.12.refs_2_, ...), custom_call_target="tpu_custom_call", output_to_operand_aliasing={{}: (9, {})} | custom-call | flops 3623878656 | bytes 10485760 | tf_op jit(solution)/shard_map/pallas_call | solution.py:565
  (48 shorter events, 4.8 us)
Async XLA Ops:
  0.6 11.8 %copy-start.12 = (s32[768,16]{0,1:T(8,128)S(1)}, s32[768,16]{0,1:T(8,128)}, u32[]{:S(2)}) copy-start(s32[768,16]{0,1:T(8,128)} %param.12) | copy-start | bytes 147460
  0.6 12.8 %copy-start.13 = (s32[24,16]{0,1:T(8,128)S(1)}, s32[24,16]{0,1:T(8,128)}, u32[]{:S(2)}) copy-start(s32[24,16]{0,1:T(8,128)} %param.11) | copy-start | bytes 4612
  0.6 26.4 %copy-start = (bf16[384,1536]{1,0:T(8,128)(2,1)S(1)}, bf16[384,1536]{1,0:T(8,128)(2,1)}, u32[]{:S(2)}) copy-start(bf16[384,1536]{1,0:T(8,128)(2,1)} %refs_4_.3) | copy-start | bytes 3538948
  6.6 22.8 %collective-permute-start.4 = (bf16[3072,384]{1,0:T(8,128)(2,1)}, bf16[3072,384]{1,0:T(8,128)(2,1)}, u32[]{:S(2)}, u32[]{:S(2)}) collective-permute-start(bf16[3072,384]{1,0:T(8,128)(2,1)} %bitcast.5), channel_id=1, source_target_pairs={{0,4},{4,0},{8,12},{12,8},{16,20},{20,16},{24,28},{28,24},{32,36},... | collective-permute-start | bytes 7077896 | tf_op jit(solution)/shard_map/ppermute | solution.py:603
  6.6 10.8 %collective-permute-start = (bf16[384,384]{1,0:T(8,128)(2,1)}, bf16[384,384]{1,0:T(8,128)(2,1)S(1)}, u32[]{:S(2)}, u32[]{:S(2)}) collective-permute-start(bf16[384,384]{1,0:T(8,128)(2,1)} %get-tuple-element.37.refs_0_), channel_id=1, source_target_pairs={{0,8},{4,12},{8,16},{12,20},{16,24},{20,28},{24,0},{28,4},{32,40},... | collective-permute-start | bytes 884744 | tf_op jit(solution)/shard_map/ppermute | solution.py:597
  8.3 16.6 %collective-permute-start.1 = (bf16[384,384]{1,0:T(8,128)(2,1)}, bf16[384,384]{1,0:T(8,128)(2,1)S(1)}, u32[]{:S(2)}, u32[]{:S(2)}) collective-permute-start(bf16[384,384]{1,0:T(8,128)(2,1)} %get-tuple-element.37.refs_0_), channel_id=1, source_target_pairs={{0,16},{4,20},{8,24},{12,28},{16,0},{20,4},{24,8},{28,12},{32,48},... | collective-permute-start | bytes 884744 | tf_op jit(solution)/shard_map/ppermute | solution.py:597
  11.0 13.9 %collective-permute-start.2 = (bf16[384,384]{1,0:T(8,128)(2,1)}, bf16[384,384]{1,0:T(8,128)(2,1)S(1)}, u32[]{:S(2)}, u32[]{:S(2)}) collective-permute-start(bf16[384,384]{1,0:T(8,128)(2,1)} %get-tuple-element.37.refs_0_), channel_id=1, source_target_pairs={{0,24},{4,28},{8,0},{12,4},{16,8},{20,12},{24,16},{28,20},{32,56},... | collective-permute-start | bytes 884744 | tf_op jit(solution)/shard_map/ppermute | solution.py:597
  17.5 31.2 %copy-start.9 = (bf16[384,384]{1,0:T(8,128)(2,1)}, bf16[384,384]{1,0:T(8,128)(2,1)S(1)}, u32[]{:S(2)}) copy-start(bf16[384,384]{1,0:T(8,128)(2,1)S(1)} %collective-permute-done.refs_1_) | copy-start | bytes 884740
  24.8 23.8 %copy-start.10 = (bf16[384,384]{1,0:T(8,128)(2,1)}, bf16[384,384]{1,0:T(8,128)(2,1)S(1)}, u32[]{:S(2)}) copy-start(bf16[384,384]{1,0:T(8,128)(2,1)S(1)} %collective-permute-done.1.refs_2_) | copy-start | bytes 884740
  24.8 23.8 %copy-start.11 = (bf16[384,384]{1,0:T(8,128)(2,1)}, bf16[384,384]{1,0:T(8,128)(2,1)S(1)}, u32[]{:S(2)}) copy-start(bf16[384,384]{1,0:T(8,128)(2,1)S(1)} %collective-permute-done.2.refs_3_) | copy-start | bytes 884740
  24.9 35.7 %collective-permute-start.3 = (bf16[3072,384]{1,0:T(8,128)(2,1)}, bf16[3072,384]{1,0:T(8,128)(2,1)}, u32[]{:S(2)}, u32[]{:S(2)}) collective-permute-start(bf16[3072,384]{1,0:T(8,128)(2,1)} %bitcast.4), channel_id=1, source_target_pairs={{4,8},{12,16},{20,24},{28,32},{36,40},{44,48},{52,56},{60,64},{68,... | collective-permute-start | bytes 7077896 | tf_op jit(solution)/shard_map/ppermute | solution.py:606
  27.8 61.7 %collective-permute-start.9 = (bf16[384,768]{1,0:T(8,128)(2,1)}, bf16[384,768]{1,0:T(8,128)(2,1)S(1)}, u32[]{:S(2)}, u32[]{:S(2)}) collective-permute-start(bf16[384,768]{1,0:T(8,128)(2,1)} %constant_dynamic-slice_fusion), channel_id=1, source_target_pairs={{0,1},{1,0},{2,3},{3,2},{4,5},{5,4},{6,7},{7,6},{8,9},{9,8},{10,11... | collective-permute-start | bytes 1769480 | tf_op jit(solution)/shard_map/ppermute | solution.py:618
  52.8 26.9 %collective-permute-start.5 = (bf16[768,384]{1,0:T(8,128)(2,1)}, bf16[768,384]{1,0:T(8,128)(2,1)S(1)}, u32[]{:S(2)}, u32[]{:S(2)}) collective-permute-start(bf16[768,384]{1,0:T(8,128)(2,1)} %get-tuple-element.50), channel_id=1, source_target_pairs={{0,32},{4,36},{8,40},{12,44},{16,48},{20,52},{24,56},{28,60},{32,6... | collective-permute-start | bytes 1769480 | tf_op jit(solution)/shard_map/ppermute | solution.py:613
  55.9 30.2 %collective-permute-start.6 = (bf16[768,384]{1,0:T(8,128)(2,1)}, bf16[768,384]{1,0:T(8,128)(2,1)S(1)}, u32[]{:S(2)}, u32[]{:S(2)}) collective-permute-start(bf16[768,384]{1,0:T(8,128)(2,1)} %get-tuple-element.51), channel_id=1, source_target_pairs={{0,64},{4,68},{8,72},{12,76},{16,80},{20,84},{24,88},{28,92},{32,9... | collective-permute-start | bytes 1769480 | tf_op jit(solution)/shard_map/ppermute | solution.py:613
  59.8 26.3 %collective-permute-start.7 = (bf16[768,384]{1,0:T(8,128)(2,1)}, bf16[768,384]{1,0:T(8,128)(2,1)S(1)}, u32[]{:S(2)}, u32[]{:S(2)}) collective-permute-start(bf16[768,384]{1,0:T(8,128)(2,1)} %get-tuple-element.52), channel_id=1, source_target_pairs={{0,96},{4,100},{8,104},{12,108},{16,112},{20,116},{24,120},{28,124... | collective-permute-start | bytes 1769480 | tf_op jit(solution)/shard_map/ppermute | solution.py:613
  79.7 6.4 %copy-start.4 = (bf16[768,384]{1,0:T(8,128)(2,1)}, bf16[768,384]{1,0:T(8,128)(2,1)S(1)}, u32[]{:S(2)}) copy-start(bf16[768,384]{1,0:T(8,128)(2,1)S(1)} %collective-permute-done.5.b.rest_1_) | copy-start | bytes 1769476
  86.1 0.8 copy-start.5
  86.1 1.0 copy-start.6
  89.6 4.3 %collective-permute-start.8 = (bf16[1536,384]{1,0:T(8,128)(2,1)}, bf16[1536,384]{1,0:T(8,128)(2,1)S(1)}, u32[]{:S(2)}, u32[]{:S(2)}) collective-permute-start(bf16[1536,384]{1,0:T(8,128)(2,1)} %shard_map.78), channel_id=1, source_target_pairs={{0,4},{4,0},{8,12},{12,8},{16,20},{20,16},{24,28},{28,24},{32,36},... | collective-permute-start | bytes 3538952 | tf_op jit(solution)/shard_map/ppermute | solution.py:627
  90.7 29.7 %collective-permute-start.10 = (bf16[768,768]{1,0:T(8,128)(2,1)S(1)}, bf16[768,768]{1,0:T(8,128)(2,1)S(1)}, u32[]{:S(2)}, u32[]{:S(2)}) collective-permute-start(bf16[768,768]{1,0:T(8,128)(2,1)S(1)} %pad_maximum_fusion.1), channel_id=1, source_target_pairs={{0,3},{1,2},{2,1},{3,0},{4,7},{5,6},{6,5},{7,4},{8,11},{9,10},{10,... | collective-permute-start | bytes 3538952 | tf_op jit(solution)/shard_map/ppermute | solution.py:620
  93.8 1.1 copy-start.7
  102.5 19.3 %copy-start.8 = (bf16[768,384]{1,0:T(8,128)(2,1)S(1)}, bf16[768,384]{1,0:T(8,128)(2,1)}, u32[]{:S(2)}) copy-start(bf16[768,384]{1,0:T(8,128)(2,1)} %get-tuple-element.59.rest_5_) | copy-start | bytes 1769476
  102.5 27.6 %copy-start.2 = (bf16[768,384]{1,0:T(8,128)(2,1)S(1)}, bf16[768,384]{1,0:T(8,128)(2,1)}, u32[]{:S(2)}) copy-start(bf16[768,384]{1,0:T(8,128)(2,1)} %get-tuple-element.64.refs_0_) | copy-start | bytes 1769476
  121.8 22.1 %collective-permute-start.14 = (bf16[1152,768]{1,0:T(8,128)(2,1)}, bf16[1152,768]{1,0:T(8,128)(2,1)S(1)}, u32[]{:S(2)}, u32[]{:S(2)}) collective-permute-start(bf16[1152,768]{1,0:T(8,128)(2,1)} %pad_maximum_fusion), channel_id=1, source_target_pairs={{0,4},{4,0},{8,12},{12,8},{16,20},{20,16},{24,28},{28,24},{32,36},... | collective-permute-start | bytes 5308424 | tf_op jit(solution)/shard_map/ppermute | solution.py:633
  121.8 19.1 %collective-permute-start.15 = (bf16[768,384]{1,0:T(8,128)(2,1)S(1)}, bf16[768,384]{1,0:T(8,128)(2,1)S(1)}, u32[]{:S(2)}, u32[]{:S(2)}) collective-permute-start(bf16[768,384]{1,0:T(8,128)(2,1)S(1)} %copy-done.8), channel_id=1, source_target_pairs={{2,3},{3,2},{4,5},{5,4},{10,11},{11,10},{12,13},{13,12},{18,19},{1... | collective-permute-start | bytes 1769480 | tf_op jit(solution)/shard_map/ppermute | solution.py:643
  122.5 19.8 %collective-permute-start.16 = (bf16[768,384]{1,0:T(8,128)(2,1)S(1)}, bf16[768,384]{1,0:T(8,128)(2,1)S(1)}, u32[]{:S(2)}, u32[]{:S(2)}) collective-permute-start(bf16[768,384]{1,0:T(8,128)(2,1)S(1)} %copy-done.8), channel_id=1, source_target_pairs={{0,2},{1,3},{6,4},{7,5},{8,10},{9,11},{14,12},{15,13},{16,18},{17,... | collective-permute-start | bytes 1769480 | tf_op jit(solution)/shard_map/ppermute | solution.py:643
  130.0 13.8 %copy-start.1 = (s32[2]{0:T(128)S(1)}, s32[2]{0:T(128)}, u32[]{:S(2)}) copy-start(s32[2]{0:T(128)} %pad_add_fusion.scalars) | copy-start | bytes 28
  130.1 13.8 %collective-permute-start.17 = (bf16[768,384]{1,0:T(8,128)(2,1)S(1)}, bf16[768,384]{1,0:T(8,128)(2,1)S(1)}, u32[]{:S(2)}, u32[]{:S(2)}) collective-permute-start(bf16[768,384]{1,0:T(8,128)(2,1)S(1)} %copy-done.2), channel_id=1, source_target_pairs={{0,3},{1,2},{6,5},{7,4},{8,11},{9,10},{14,13},{15,12},{16,19},{17,... | collective-permute-start | bytes 1769480 | tf_op jit(solution)/shard_map/ppermute | solution.py:643
  139.0 18.3 %collective-permute-start.11 = (bf16[768,384]{1,0:T(8,128)(2,1)}, bf16[768,384]{1,0:T(8,128)(2,1)S(1)}, u32[]{:S(2)}, u32[]{:S(2)}) collective-permute-start(bf16[768,384]{1,0:T(8,128)(2,1)} %get-tuple-element.61), channel_id=1, source_target_pairs={{0,1},{1,0},{6,7},{7,6},{8,9},{9,8},{14,15},{15,14},{16,17},{17,16... | collective-permute-start | bytes 1769480 | tf_op jit(solution)/shard_map/ppermute | solution.py:643
  140.9 16.3 %collective-permute-start.12 = (bf16[768,384]{1,0:T(8,128)(2,1)}, bf16[768,384]{1,0:T(8,128)(2,1)S(1)}, u32[]{:S(2)}, u32[]{:S(2)}) collective-permute-start(bf16[768,384]{1,0:T(8,128)(2,1)} %get-tuple-element.61), channel_id=1, source_target_pairs={{2,0},{3,1},{4,6},{5,7},{10,8},{11,9},{12,14},{13,15},{18,16},{19,... | collective-permute-start | bytes 1769480 | tf_op jit(solution)/shard_map/ppermute | solution.py:643
  142.2 19.9 %copy-start.3 = (bf16[768,384]{1,0:T(8,128)(2,1)S(1)}, bf16[768,384]{1,0:T(8,128)(2,1)}, u32[]{:S(2)}) copy-start(bf16[768,384]{1,0:T(8,128)(2,1)} %get-tuple-element.60.refs_0_) | copy-start | bytes 1769476
  142.2 19.8 %collective-permute-start.13 = (bf16[768,384]{1,0:T(8,128)(2,1)}, bf16[768,384]{1,0:T(8,128)(2,1)S(1)}, u32[]{:S(2)}, u32[]{:S(2)}) collective-permute-start(bf16[768,384]{1,0:T(8,128)(2,1)} %get-tuple-element.60.refs_0_), channel_id=1, source_target_pairs={{2,1},{3,0},{4,7},{5,6},{10,9},{11,8},{12,15},{13,14},{18,17},{19,... | collective-permute-start | bytes 1769480 | tf_op jit(solution)/shard_map/ppermute | solution.py:643

commit v6 on v4

--- a/solution.py
+++ b/solution.py
@@ -28,7 +28,7 @@
 LOG2_SCALE = math.log2(math.e) / math.sqrt(HD)
 NT = (((1,), (1,)), ((), ()))
 VMEM_LIMIT = 56 * 2**20
-UNROLL = 3
+UNROLL = 6
 SLOT, STRIDE, ORDER = KNEAR, KNEAR + KFAR, BLOCKS
 FAST_FIRST, FAST_LAST, SLOW_FIRST, SLOW_LAST = range(4)
 IN_HBM = pl.BlockSpec(memory_space=pltpu.HBM)

time: 149 us -> 149 us (level)
  transfers between devices with their start and end apart: 18 -> 18, of which waited for: 6 -> 6; matrix products, arithmetic and copies ran while one was open for 3% -> 3% of each run, Pallas kernels for 44% -> 43%
where the time goes in v6:
time: 149 us; the launch traced here: 148 us
  Pallas kernels  75.9 us (51%)
  starting transfers between devices  34.1 us (23%)
  waiting for transfers between devices  29 us (19%)
  local copies, waits for them, and re-layouts  5.45 us (4%)
  other arithmetic  3.05 us (2%)
    pallas_call x2, Pallas kernels, attend(): pl.pallas_call(functools.partial(attend_kernel, chunk=chunk, with_far=wit...  38.4 us
    ppermute x6, waiting for transfers between devices, exchange(): return lax.ppermute(chunk, ('tm', 'head'), pairs)  16 us
    pallas_call x2, Pallas kernels, merge_far(): pl.pallas_call(functools.partial(merge_kernel, chunk=chunk), grid_spec=pl...  15.1 us
    ppermute x6, starting transfers between devices, exchange(): return lax.ppermute(chunk, ('tm', 'head'), pairs)  14.4 us
    ppermute x3, starting transfers between devices, per_device(): arrived.append(lax.ppermute(packs[d], 'tm', pairs))  7.75 us
    ppermute x3, waiting for transfers between devices, per_device(): lax.ppermute(thinned, 'tm', [(tm_index(*p), tm_index(p[0], p[1] + d, p[2]...  7.4 us
    pallas_call x2, Pallas kernels, project(): pl.pallas_call(functools.partial(project_kernel, wanted_fast=wanted_fast,...  6.48 us
    pallas_call x1, Pallas kernels, pack(): pl.pallas_call(pack_kernel, grid_spec=pltpu.PrefetchScalarGridSpec(num_sc...  6.03 us
  transfers between devices with their start and end apart: 18, of which 6 were waited for; matrix products, arithmetic and copies ran while one was open for 3% of the time, Pallas kernels for 43%

profile of v6, /device:TPU:0, one launch (start us, length us, event | category | flops | bytes accessed | tf_op | source)
XLA Modules:
  0.0 147.9 jit_solution(15456670279346287430)
XLA Ops:
  0.7 6.0 %shard_map.73 = (bf16[384,384]{1,0:T(8,128)(2,1)}, bf16[2,1536,384]{2,1,0:T(8,128)(2,1)}, bf16[2,1536,384]{2,1,0:T(8,128)(2,1)}) custom-call(s32[2]{0:T(128)} %pad_add_fusion.scalars, bf16[3072,384]{1,0:T(8,128)(2,1)} %k_ref.3, bf16[3072,384]{1,0:T(8,128)(2,1)} %v_ref.3, bf16[3072,384]{1,0:T(8,128)(2,1)} %k_ref.3, bf16[3072,384]{1,0:T(8,128)(2,1)} %v_ref.3), custom_call_target="tpu_custom_call" | custom-call | bytes 10485760 | tf_op jit(solution)/shard_map/pallas_call | solution.py:455
  6.7 1.6 %collective-permute-start = (bf16[384,384]{1,0:T(8,128)(2,1)}, bf16[384,384]{1,0:T(8,128)(2,1)S(1)}, u32[]{:S(2)}, u32[]{:S(2)}) collective-permute-start(bf16[384,384]{1,0:T(8,128)(2,1)} %get-tuple-element.35.refs_0_), channel_id=1, source_target_pairs={{0,8},{4,12},{8,16},{12,20},{16,24},{20,28},{24,0},{28,4},{32,40},... | collective-permute-start | bytes 884744 | tf_op jit(solution)/shard_map/ppermute | solution.py:597
  8.3 2.7 %collective-permute-start.1 = (bf16[384,384]{1,0:T(8,128)(2,1)}, bf16[384,384]{1,0:T(8,128)(2,1)S(1)}, u32[]{:S(2)}, u32[]{:S(2)}) collective-permute-start(bf16[384,384]{1,0:T(8,128)(2,1)} %get-tuple-element.35.refs_0_), channel_id=1, source_target_pairs={{0,16},{4,20},{8,24},{12,28},{16,0},{20,4},{24,8},{28,12},{32,48},... | collective-permute-start | bytes 884744 | tf_op jit(solution)/shard_map/ppermute | solution.py:597
  11.1 1.4 collective-permute-start.2
  14.1 3.4 %shard_map.74 = (s32[48,128]{1,0:T(8,128)}, s32[32,128]{1,0:T(8,128)}) custom-call(s32[2]{0:T(128)} %pad_add_fusion.scalars, s32[64]{0:T(128)} %steps.1, s32[768,16]{1,0:T(8,128)} %copy.9.far_ref, s32[24,16]{1,0:T(8,128)} %copy.10.near_ref), custom_call_target="tpu_custom_call" | custom-call | flops 1048576 | bytes 4194304 | tf_op jit(solution)/shard_map/pallas_call | solution.py:414
  17.5 7.4 %collective-permute-done.1.refs_2_ = bf16[384,384]{1,0:T(8,128)(2,1)S(1)} collective-permute-done((bf16[384,384]{1,0:T(8,128)(2,1)}, bf16[384,384]{1,0:T(8,128)(2,1)S(1)}, u32[]{:S(2)}, u32[]{:S(2)}) %collective-permute-start.1) | collective-permute-done | bytes 294944 | tf_op jit(solution)/shard_map/ppermute | solution.py:597
  24.9 2.1 %collective-permute-start.3 = (bf16[3072,384]{1,0:T(8,128)(2,1)}, bf16[3072,384]{1,0:T(8,128)(2,1)}, u32[]{:S(2)}, u32[]{:S(2)}) collective-permute-start(bf16[3072,384]{1,0:T(8,128)(2,1)} %bitcast.4), channel_id=1, source_target_pairs={{4,8},{12,16},{20,24},{28,32},{36,40},{44,48},{52,56},{60,64},{68,... | collective-permute-start | bytes 7077896 | tf_op jit(solution)/shard_map/ppermute | solution.py:606
  27.1 1.7 %collective-permute-start.9 = (bf16[384,768]{1,0:T(8,128)(2,1)S(1)}, bf16[384,768]{1,0:T(8,128)(2,1)S(1)}, u32[]{:S(2)}, u32[]{:S(2)}) collective-permute-start(bf16[384,768]{1,0:T(8,128)(2,1)S(1)} %constant_dynamic-slice_fusion), channel_id=1, source_target_pairs={{0,1},{1,0},{2,3},{3,2},{4,5},{5,4},{6,7},{7,6},{8,9},{9,8},{10,11... | collective-permute-start | bytes 1769480 | tf_op jit(solution)/shard_map/ppermute | solution.py:618
  28.8 19.2 %shard_map.75 = (bf16[1536,384]{1,0:T(8,128)(2,1)}, f32[1536,384]{1,0:T(8,128)}) custom-call(s32[32,128]{1,0:T(8,128)} %get-tuple-element.36.table, bf16[3072,384]{1,0:T(8,128)(2,1)} %q_ref.7, bf16[3072,384]{1,0:T(8,128)(2,1)} %k_ref.3, bf16[3072,384]{1,0:T(8,128)(2,1)} %v_ref.3, bf16[3072,384]{1,0:T(8,128)(2,1)} %collective-permute-done.4.halo_ref), custom_call_target="tpu_custom_call" | custom-call | flops 15401484288 | bytes 8388608 | tf_op jit(solution)/shard_map/pallas_call | solution.py:217
  48.0 4.0 %shard_map.76 = (bf16[768,384]{1,0:T(8,128)(2,1)}, bf16[768,384]{1,0:T(8,128)(2,1)}, bf16[768,384]{1,0:T(8,128)(2,1)}, bf16[768,384]{1,0:T(8,128)(2,1)}) custom-call(s32[48,128]{1,0:T(8,128)} %get-tuple-element.38.picks, bf16[384,384]{1,0:T(8,128)(2,1)} %get-tuple-element.35.refs_0_, bf16[384,384]{1,0:T(8,128)(2,1)} %copy-done.8, ...), custom_call_target="tpu_custom_call" | custom-call | bytes 4194304 | tf_op jit(solution)/shard_map/pallas_call | solution.py:503
  52.0 3.2 %collective-permute-start.5 = (bf16[768,384]{1,0:T(8,128)(2,1)}, bf16[768,384]{1,0:T(8,128)(2,1)S(1)}, u32[]{:S(2)}, u32[]{:S(2)}) collective-permute-start(bf16[768,384]{1,0:T(8,128)(2,1)} %get-tuple-element.48), channel_id=1, source_target_pairs={{0,32},{4,36},{8,40},{12,44},{16,48},{20,52},{24,56},{28,60},{32,6... | collective-permute-start | bytes 1769480 | tf_op jit(solution)/shard_map/ppermute | solution.py:613
  55.2 3.9 %collective-permute-start.6 = (bf16[768,384]{1,0:T(8,128)(2,1)}, bf16[768,384]{1,0:T(8,128)(2,1)}, u32[]{:S(2)}, u32[]{:S(2)}) collective-permute-start(bf16[768,384]{1,0:T(8,128)(2,1)} %get-tuple-element.49), channel_id=1, source_target_pairs={{0,64},{4,68},{8,72},{12,76},{16,80},{20,84},{24,88},{28,92},{32,9... | collective-permute-start | bytes 1769480 | tf_op jit(solution)/shard_map/ppermute | solution.py:613
  59.8 1.1 pad_maximum_fusion.1
  60.8 2.2 %collective-permute-start.10 = (bf16[768,768]{1,0:T(8,128)(2,1)}, bf16[768,768]{1,0:T(8,128)(2,1)S(1)}, u32[]{:S(2)}, u32[]{:S(2)}) collective-permute-start(bf16[768,768]{1,0:T(8,128)(2,1)} %pad_maximum_fusion.1), channel_id=1, source_target_pairs={{0,3},{1,2},{2,1},{3,0},{4,7},{5,6},{6,5},{7,4},{8,11},{9,10},{10,... | collective-permute-start | bytes 3538952 | tf_op jit(solution)/shard_map/ppermute | solution.py:620
  63.0 19.2 %shard_map.77 = (bf16[1536,384]{1,0:T(8,128)(2,1)}, f32[1536,384]{1,0:T(8,128)}) custom-call(s32[32,128]{1,0:T(8,128)} %get-tuple-element.36.table, bf16[3072,384]{1,0:T(8,128)(2,1)} %q_ref.7, bf16[3072,384]{1,0:T(8,128)(2,1)} %k_ref.3, bf16[3072,384]{1,0:T(8,128)(2,1)} %v_ref.3, bf16[3072,384]{1,0:T(8,128)(2,1)} %collective-permute-done.3.halo_ref, ...), custom_call_target="tpu_custom_call" | custom-call | flops 15401484288 | bytes 8388608 | tf_op jit(solution)/shard_map/pallas_call | solution.py:217
  82.2 4.0 %collective-permute-done.6.c.rest_2_ = bf16[768,384]{1,0:T(8,128)(2,1)} collective-permute-done((bf16[768,384]{1,0:T(8,128)(2,1)}, bf16[768,384]{1,0:T(8,128)(2,1)}, u32[]{:S(2)}, u32[]{:S(2)}) %collective-permute-start.6) | collective-permute-done | bytes 589856 | tf_op jit(solution)/shard_map/ppermute | solution.py:613
  86.3 2.4 %shard_map.78 = bf16[1536,384]{1,0:T(8,128)(2,1)} custom-call(bf16[768,384]{1,0:T(8,128)(2,1)} %get-tuple-element.44.rest_0_.a, bf16[768,384]{1,0:T(8,128)(2,1)} %copy-done.6, bf16[768,384]{1,0:T(8,128)(2,1)} %collective-permute-done.6.c.rest_2_, bf16[768,384]{1,0:T(8,128)(2,1)} %collective-permute-done.7.d.rest_3_, ...), custom_call_target="tpu_custom_call" | custom-call | bytes 2097152 | tf_op jit(solution)/shard_map/pallas_call | solution.py:478
  89.0 1.3 pad_maximum_fusion
  90.6 1.2 collective-permute-done.8.rest_4_
  91.8 1.1 copy-done.7
  92.9 7.5 %shard_map.79 = (bf16[768,384]{1,0:T(8,128)(2,1)}, bf16[768,384]{1,0:T(8,128)(2,1)}) custom-call(s32[32,128]{1,0:T(8,128)} %get-tuple-element.36.table, bf16[3072,384]{1,0:T(8,128)(2,1)} %q_ref.7, bf16[1536,384]{1,0:T(8,128)(2,1)} %get-tuple-element.47.near_ref, f32[1536,384]{1,0:T(8,128)} %get-tuple-element.43.refs_4_.level_ref, ...), custom_call_target="tpu_custom_call" | custom-call | flops 1811939328 | bytes 8388608 | tf_op jit(solution)/shard_map/pallas_call | solution.py:297
  101.1 7.6 %collective-permute-start.16 = (bf16[768,384]{1,0:T(8,128)(2,1)}, bf16[768,384]{1,0:T(8,128)(2,1)S(1)}, u32[]{:S(2)}, u32[]{:S(2)}) collective-permute-start(bf16[768,384]{1,0:T(8,128)(2,1)} %get-tuple-element.60), channel_id=1, source_target_pairs={{0,2},{1,3},{6,4},{7,5},{8,10},{9,11},{14,12},{15,13},{16,18},{17,... | collective-permute-start | bytes 1769480 | tf_op jit(solution)/shard_map/ppermute | solution.py:641
  108.8 1.5 collective-permute-start.17
  110.3 1.2 copy-done
  111.5 7.6 %shard_map.80 = (bf16[768,384]{1,0:T(8,128)(2,1)}, bf16[768,384]{1,0:T(8,128)(2,1)}) custom-call(s32[32,128]{1,0:T(8,128)} %get-tuple-element.36.table, bf16[3072,384]{1,0:T(8,128)(2,1)} %q_ref.7, bf16[1536,384]{1,0:T(8,128)(2,1)} %get-tuple-element.52.near_ref, f32[1536,384]{1,0:T(8,128)} %get-tuple-element.53.after.rest_5_.level_ref, ...), custom_call_target="tpu_custom_call" | custom-call | flops 1811939328 | bytes 8388608 | tf_op jit(solution)/shard_map/pallas_call | solution.py:297
  119.1 2.0 %collective-permute-start.12 = (bf16[768,384]{1,0:T(8,128)(2,1)}, bf16[768,384]{1,0:T(8,128)(2,1)S(1)}, u32[]{:S(2)}, u32[]{:S(2)}) collective-permute-start(bf16[768,384]{1,0:T(8,128)(2,1)} %get-tuple-element.58), channel_id=1, source_target_pairs={{0,1},{1,0},{6,7},{7,6},{8,9},{9,8},{14,15},{15,14},{16,17},{17,16... | collective-permute-start | bytes 1769480 | tf_op jit(solution)/shard_map/ppermute | solution.py:641
  121.1 1.3 collective-permute-start.13
  122.4 1.3 collective-permute-start.14
  123.8 1.5 copy-done.1
  126.1 11.0 %collective-permute-done.12.refs_1_ = bf16[768,384]{1,0:T(8,128)(2,1)S(1)} collective-permute-done((bf16[768,384]{1,0:T(8,128)(2,1)}, bf16[768,384]{1,0:T(8,128)(2,1)S(1)}, u32[]{:S(2)}, u32[]{:S(2)}) %collective-permute-start.12) | collective-permute-done | bytes 589856 | tf_op jit(solution)/shard_map/ppermute | solution.py:641
  137.1 4.9 %collective-permute-done.14.refs_3_ = bf16[768,384]{1,0:T(8,128)(2,1)S(1)} collective-permute-done((bf16[768,384]{1,0:T(8,128)(2,1)}, bf16[768,384]{1,0:T(8,128)(2,1)S(1)}, u32[]{:S(2)}, u32[]{:S(2)}) %collective-permute-start.14) | collective-permute-done | bytes 589856 | tf_op jit(solution)/shard_map/ppermute | solution.py:641
  142.1 5.7 %shard_map.82 = bf16[768,1536]{1,0:T(8,128)(2,1)} custom-call(s32[2]{0:T(128)S(1)} %copy-done.3, bf16[768,384]{1,0:T(8,128)(2,1)S(1)} %copy-done.5, bf16[768,384]{1,0:T(8,128)(2,1)S(1)} %collective-permute-done.12.refs_1_, bf16[768,384]{1,0:T(8,128)(2,1)S(1)} %collective-permute-done.13.refs_2_, ...), custom_call_target="tpu_custom_call", output_to_operand_aliasing={{}: (9, {})} | custom-call | flops 3623878656 | bytes 10485760 | tf_op jit(solution)/shard_map/pallas_call | solution.py:565
  (46 shorter events, 5.1 us)
Async XLA Ops:
  0.7 11.9 %copy-start.11 = (s32[768,16]{0,1:T(8,128)S(1)}, s32[768,16]{0,1:T(8,128)}, u32[]{:S(2)}) copy-start(s32[768,16]{0,1:T(8,128)} %param.12) | copy-start | bytes 147460
  0.7 12.8 %copy-start.12 = (s32[24,16]{0,1:T(8,128)S(1)}, s32[24,16]{0,1:T(8,128)}, u32[]{:S(2)}) copy-start(s32[24,16]{0,1:T(8,128)} %param.11) | copy-start | bytes 4612
  0.7 26.4 %copy-start.2 = (bf16[384,1536]{1,0:T(8,128)(2,1)S(1)}, bf16[384,1536]{1,0:T(8,128)(2,1)}, u32[]{:S(2)}) copy-start(bf16[384,1536]{1,0:T(8,128)(2,1)} %refs_4_.3) | copy-start | bytes 3538948
  6.7 22.1 %collective-permute-start.4 = (bf16[3072,384]{1,0:T(8,128)(2,1)}, bf16[3072,384]{1,0:T(8,128)(2,1)}, u32[]{:S(2)}, u32[]{:S(2)}) collective-permute-start(bf16[3072,384]{1,0:T(8,128)(2,1)} %bitcast.5), channel_id=1, source_target_pairs={{0,4},{4,0},{8,12},{12,8},{16,20},{20,16},{24,28},{28,24},{32,36},... | collective-permute-start | bytes 7077896 | tf_op jit(solution)/shard_map/ppermute | solution.py:603
  6.7 10.8 %collective-permute-start = (bf16[384,384]{1,0:T(8,128)(2,1)}, bf16[384,384]{1,0:T(8,128)(2,1)S(1)}, u32[]{:S(2)}, u32[]{:S(2)}) collective-permute-start(bf16[384,384]{1,0:T(8,128)(2,1)} %get-tuple-element.35.refs_0_), channel_id=1, source_target_pairs={{0,8},{4,12},{8,16},{12,20},{16,24},{20,28},{24,0},{28,4},{32,40},... | collective-permute-start | bytes 884744 | tf_op jit(solution)/shard_map/ppermute | solution.py:597
  8.3 16.6 %collective-permute-start.1 = (bf16[384,384]{1,0:T(8,128)(2,1)}, bf16[384,384]{1,0:T(8,128)(2,1)S(1)}, u32[]{:S(2)}, u32[]{:S(2)}) collective-permute-start(bf16[384,384]{1,0:T(8,128)(2,1)} %get-tuple-element.35.refs_0_), channel_id=1, source_target_pairs={{0,16},{4,20},{8,24},{12,28},{16,0},{20,4},{24,8},{28,12},{32,48},... | collective-permute-start | bytes 884744 | tf_op jit(solution)/shard_map/ppermute | solution.py:597
  11.1 13.9 %collective-permute-start.2 = (bf16[384,384]{1,0:T(8,128)(2,1)}, bf16[384,384]{1,0:T(8,128)(2,1)S(1)}, u32[]{:S(2)}, u32[]{:S(2)}) collective-permute-start(bf16[384,384]{1,0:T(8,128)(2,1)} %get-tuple-element.35.refs_0_), channel_id=1, source_target_pairs={{0,24},{4,28},{8,0},{12,4},{16,8},{20,12},{24,16},{28,20},{32,56},... | collective-permute-start | bytes 884744 | tf_op jit(solution)/shard_map/ppermute | solution.py:597
  17.5 30.5 %copy-start.8 = (bf16[384,384]{1,0:T(8,128)(2,1)}, bf16[384,384]{1,0:T(8,128)(2,1)S(1)}, u32[]{:S(2)}) copy-start(bf16[384,384]{1,0:T(8,128)(2,1)S(1)} %collective-permute-done.refs_1_) | copy-start | bytes 884740
  24.9 23.1 %copy-start.9 = (bf16[384,384]{1,0:T(8,128)(2,1)}, bf16[384,384]{1,0:T(8,128)(2,1)S(1)}, u32[]{:S(2)}) copy-start(bf16[384,384]{1,0:T(8,128)(2,1)S(1)} %collective-permute-done.1.refs_2_) | copy-start | bytes 884740
  24.9 23.1 %copy-start.10 = (bf16[384,384]{1,0:T(8,128)(2,1)}, bf16[384,384]{1,0:T(8,128)(2,1)S(1)}, u32[]{:S(2)}) copy-start(bf16[384,384]{1,0:T(8,128)(2,1)S(1)} %collective-permute-done.2.refs_3_) | copy-start | bytes 884740
  24.9 38.1 %collective-permute-start.3 = (bf16[3072,384]{1,0:T(8,128)(2,1)}, bf16[3072,384]{1,0:T(8,128)(2,1)}, u32[]{:S(2)}, u32[]{:S(2)}) collective-permute-start(bf16[3072,384]{1,0:T(8,128)(2,1)} %bitcast.4), channel_id=1, source_target_pairs={{4,8},{12,16},{20,24},{28,32},{36,40},{44,48},{52,56},{60,64},{68,... | collective-permute-start | bytes 7077896 | tf_op jit(solution)/shard_map/ppermute | solution.py:606
  27.1 32.7 %collective-permute-start.9 = (bf16[384,768]{1,0:T(8,128)(2,1)S(1)}, bf16[384,768]{1,0:T(8,128)(2,1)S(1)}, u32[]{:S(2)}, u32[]{:S(2)}) collective-permute-start(bf16[384,768]{1,0:T(8,128)(2,1)S(1)} %constant_dynamic-slice_fusion), channel_id=1, source_target_pairs={{0,1},{1,0},{2,3},{3,2},{4,5},{5,4},{6,7},{7,6},{8,9},{9,8},{10,11... | collective-permute-start | bytes 1769480 | tf_op jit(solution)/shard_map/ppermute | solution.py:618
  52.0 30.2 %collective-permute-start.5 = (bf16[768,384]{1,0:T(8,128)(2,1)}, bf16[768,384]{1,0:T(8,128)(2,1)S(1)}, u32[]{:S(2)}, u32[]{:S(2)}) collective-permute-start(bf16[768,384]{1,0:T(8,128)(2,1)} %get-tuple-element.48), channel_id=1, source_target_pairs={{0,32},{4,36},{8,40},{12,44},{16,48},{20,52},{24,56},{28,60},{32,6... | collective-permute-start | bytes 1769480 | tf_op jit(solution)/shard_map/ppermute | solution.py:613
  55.2 31.1 %collective-permute-start.6 = (bf16[768,384]{1,0:T(8,128)(2,1)}, bf16[768,384]{1,0:T(8,128)(2,1)}, u32[]{:S(2)}, u32[]{:S(2)}) collective-permute-start(bf16[768,384]{1,0:T(8,128)(2,1)} %get-tuple-element.49), channel_id=1, source_target_pairs={{0,64},{4,68},{8,72},{12,76},{16,80},{20,84},{24,88},{28,92},{32,9... | collective-permute-start | bytes 1769480 | tf_op jit(solution)/shard_map/ppermute | solution.py:613
  59.1 27.2 %collective-permute-start.7 = (bf16[768,384]{1,0:T(8,128)(2,1)}, bf16[768,384]{1,0:T(8,128)(2,1)}, u32[]{:S(2)}, u32[]{:S(2)}) collective-permute-start(bf16[768,384]{1,0:T(8,128)(2,1)} %get-tuple-element.50), channel_id=1, source_target_pairs={{0,96},{4,100},{8,104},{12,108},{16,112},{20,116},{24,120},{28,124... | collective-permute-start | bytes 1769480 | tf_op jit(solution)/shard_map/ppermute | solution.py:613
  60.8 28.2 %collective-permute-start.10 = (bf16[768,768]{1,0:T(8,128)(2,1)}, bf16[768,768]{1,0:T(8,128)(2,1)S(1)}, u32[]{:S(2)}, u32[]{:S(2)}) collective-permute-start(bf16[768,768]{1,0:T(8,128)(2,1)} %pad_maximum_fusion.1), channel_id=1, source_target_pairs={{0,3},{1,2},{2,1},{3,0},{4,7},{5,6},{6,5},{7,4},{8,11},{9,10},{10,... | collective-permute-start | bytes 3538952 | tf_op jit(solution)/shard_map/ppermute | solution.py:620
  82.2 4.0 %copy-start.6 = (bf16[768,384]{1,0:T(8,128)(2,1)}, bf16[768,384]{1,0:T(8,128)(2,1)S(1)}, u32[]{:S(2)}) copy-start(bf16[768,384]{1,0:T(8,128)(2,1)S(1)} %collective-permute-done.5.b.rest_1_) | copy-start | bytes 1769476
  88.7 3.1 %collective-permute-start.8 = (bf16[1536,384]{1,0:T(8,128)(2,1)}, bf16[1536,384]{1,0:T(8,128)(2,1)S(1)}, u32[]{:S(2)}, u32[]{:S(2)}) collective-permute-start(bf16[1536,384]{1,0:T(8,128)(2,1)} %shard_map.78), channel_id=1, source_target_pairs={{0,4},{4,0},{8,12},{12,8},{16,20},{20,16},{24,28},{28,24},{32,36},... | collective-permute-start | bytes 3538952 | tf_op jit(solution)/shard_map/ppermute | solution.py:627
  90.4 19.9 %collective-permute-start.11 = (bf16[1152,768]{1,0:T(8,128)(2,1)}, bf16[1152,768]{1,0:T(8,128)(2,1)S(1)}, u32[]{:S(2)}, u32[]{:S(2)}) collective-permute-start(bf16[1152,768]{1,0:T(8,128)(2,1)} %pad_maximum_fusion), channel_id=1, source_target_pairs={{0,4},{4,0},{8,12},{12,8},{16,20},{20,16},{24,28},{28,24},{32,36},... | collective-permute-start | bytes 5308424 | tf_op jit(solution)/shard_map/ppermute | solution.py:629
  91.8 1.1 copy-start.7
  100.4 22.0 %collective-permute-start.15 = (bf16[768,384]{1,0:T(8,128)(2,1)}, bf16[768,384]{1,0:T(8,128)(2,1)S(1)}, u32[]{:S(2)}, u32[]{:S(2)}) collective-permute-start(bf16[768,384]{1,0:T(8,128)(2,1)} %get-tuple-element.60), channel_id=1, source_target_pairs={{2,3},{3,2},{4,5},{5,4},{10,11},{11,10},{12,13},{13,12},{18,19},{1... | collective-permute-start | bytes 1769480 | tf_op jit(solution)/shard_map/ppermute | solution.py:641
  101.1 22.6 %collective-permute-start.16 = (bf16[768,384]{1,0:T(8,128)(2,1)}, bf16[768,384]{1,0:T(8,128)(2,1)S(1)}, u32[]{:S(2)}, u32[]{:S(2)}) collective-permute-start(bf16[768,384]{1,0:T(8,128)(2,1)} %get-tuple-element.60), channel_id=1, source_target_pairs={{0,2},{1,3},{6,4},{7,5},{8,10},{9,11},{14,12},{15,13},{16,18},{17,... | collective-permute-start | bytes 1769480 | tf_op jit(solution)/shard_map/ppermute | solution.py:641
  108.8 15.0 %copy-start.3 = (s32[2]{0:T(128)S(1)}, s32[2]{0:T(128)}, u32[]{:S(2)}) copy-start(s32[2]{0:T(128)} %pad_add_fusion.scalars) | copy-start | bytes 28
  108.8 15.0 %copy-start.4 = (bf16[768,384]{1,0:T(8,128)(2,1)S(1)}, bf16[768,384]{1,0:T(8,128)(2,1)}, u32[]{:S(2)}) copy-start(bf16[768,384]{1,0:T(8,128)(2,1)} %get-tuple-element.59.refs_0_) | copy-start | bytes 1769476
  108.8 15.0 %collective-permute-start.17 = (bf16[768,384]{1,0:T(8,128)(2,1)}, bf16[768,384]{1,0:T(8,128)(2,1)S(1)}, u32[]{:S(2)}, u32[]{:S(2)}) collective-permute-start(bf16[768,384]{1,0:T(8,128)(2,1)} %get-tuple-element.59.refs_0_), channel_id=1, source_target_pairs={{0,3},{1,2},{6,5},{7,4},{8,11},{9,10},{14,13},{15,12},{16,19},{17,... | collective-permute-start | bytes 1769480 | tf_op jit(solution)/shard_map/ppermute | solution.py:641
  110.3 1.2 copy-start
  119.1 18.0 %collective-permute-start.12 = (bf16[768,384]{1,0:T(8,128)(2,1)}, bf16[768,384]{1,0:T(8,128)(2,1)S(1)}, u32[]{:S(2)}, u32[]{:S(2)}) collective-permute-start(bf16[768,384]{1,0:T(8,128)(2,1)} %get-tuple-element.58), channel_id=1, source_target_pairs={{0,1},{1,0},{6,7},{7,6},{8,9},{9,8},{14,15},{15,14},{16,17},{17,16... | collective-permute-start | bytes 1769480 | tf_op jit(solution)/shard_map/ppermute | solution.py:641
  121.1 16.0 %collective-permute-start.13 = (bf16[768,384]{1,0:T(8,128)(2,1)}, bf16[768,384]{1,0:T(8,128)(2,1)S(1)}, u32[]{:S(2)}, u32[]{:S(2)}) collective-permute-start(bf16[768,384]{1,0:T(8,128)(2,1)} %get-tuple-element.58), channel_id=1, source_target_pairs={{2,0},{3,1},{4,6},{5,7},{10,8},{11,9},{12,14},{13,15},{18,16},{19,... | collective-permute-start | bytes 1769480 | tf_op jit(solution)/shard_map/ppermute | solution.py:641
  122.4 19.6 %collective-permute-start.14 = (bf16[768,384]{1,0:T(8,128)(2,1)}, bf16[768,384]{1,0:T(8,128)(2,1)S(1)}, u32[]{:S(2)}, u32[]{:S(2)}) collective-permute-start(bf16[768,384]{1,0:T(8,128)(2,1)} %get-tuple-element.57.refs_0_), channel_id=1, source_target_pairs={{2,1},{3,0},{4,7},{5,6},{10,9},{11,8},{12,15},{13,14},{18,17},{19,... | collective-permute-start | bytes 1769480 | tf_op jit(solution)/shard_map/ppermute | solution.py:641
  123.8 1.5 %copy-start.1 = (bf16[1152,768]{1,0:T(8,128)(2,1)S(1)}, bf16[1152,768]{1,0:T(8,128)(2,1)}, u32[]{:S(2)}) copy-start(bf16[1152,768]{1,0:T(8,128)(2,1)} %copy-done) | copy-start | bytes 5308420
  125.3 16.8 %copy-start.5 = (bf16[768,384]{1,0:T(8,128)(2,1)S(1)}, bf16[768,384]{1,0:T(8,128)(2,1)}, u32[]{:S(2)}) copy-start(bf16[768,384]{1,0:T(8,128)(2,1)} %get-tuple-element.57.refs_0_) | copy-start | bytes 1769476
